TPU v7x, 32 devices: a whole 2x2x4 slice. The times are simulated.
32 devices in a mesh: leaf: 32 (over z, y, x, core).
Axes of the slice: x: 2, y: 2, z: 4, core: 2. Of those that a mesh axis runs over, the one named last changes fastest.
Arguments:
- rhs: float32 [32768, 128], P('leaf'), may hold values from -6 to 6
- proj_bases: float32 [5, 32768, 256], P(None, 'leaf'), may hold values from -6 to 6
- corr_bases: float32 [5, 32768, 256], P(None, 'leaf'), may hold values from -0.375 to 0.375
- cores: float32 [5, 8192, 512], P(None, 'leaf'), may hold values from -0.25 to 0.25
Outputs:
- solution: float32 [32768, 128], P('leaf')
All inputs are finite; a program needn't handle non-finite values.
Results may differ from a plain program's by a relative error of at most 0.00017.
Values sent between devices are 32-bit elements; how exact they have to be, the bound alone decides.
No kernel may reach another device: no remote copies, remote signals or barrier semaphores. Data moves between devices by JAX's collectives and lax.ppermute only.
A program may use at most 64 MiB of HBM per device.

v0:
```python
import jax
import jax.numpy as jnp
from jax import lax
from jax.experimental import pallas as pl
from jax.experimental.pallas import tpu as pltpu
from jax.sharding import PartitionSpec as P

LEVELS = 5
HIGH = lax.Precision.HIGH
IN_HBM = pl.BlockSpec(memory_space=pltpu.HBM)
IN_VMEM = pl.BlockSpec(memory_space=pltpu.VMEM)


def exchange(value, mask):
    pairs = [(source, source ^ mask) for source in range(lax.axis_size("leaf"))]
    return lax.ppermute(value, "leaf", pairs)


def tie(value, after):
    return lax.optimization_barrier((value, after))[0]


def pair_up(low, mine, other, axis):
    return jnp.where(
        low,
        jnp.concatenate([mine, other], axis),
        jnp.concatenate([other, mine], axis),
    )


def project(basis, state):
    return jnp.einsum("kn,nr->kr", state, basis, precision=HIGH)


def times_transposed(left, right):
    return jnp.einsum("kb,ab->ka", left, right, precision=HIGH)


def parts(value):
    high = value.astype(jnp.bfloat16)
    return high, (value - high.astype(jnp.float32)).astype(jnp.bfloat16)


def three_passes(left, right, dim):
    rows = left.shape[0]
    left_high, left_low = parts(left)
    right_high, right_low = parts(right)

    def one(a, b):
        return lax.dot_general(a, b, (((1,), (dim,)), ((), ())), preferred_element_type=jnp.float32)

    both = one(jnp.concatenate([left_high, left_low], 0), right_high)
    return both[:rows] + (both[rows:] + one(left_high, right_low))


def begin(rhs, proj_bases, corr_bases, cores, first, leaf_core, groups):
    rows, width = rhs.shape
    rank = proj_bases.shape[2]
    shapes = [(width, rank), (width, rows), (rows, rank), (rows, rank)]
    shapes += [(rank, 2 * rank)] if leaf_core else []
    shapes += [(sum(n for _, n in group), 2 * rank) for group in groups]

    def body(x_hbm, p_hbm, w_hbm, c_hbm, *refs):
        outs, (x_ref, p_ref, sems) = list(refs[: len(shapes)]), refs[len(shapes) :]
        q_out, state_out, w_out, p_out = outs[:4]
        rest = outs[4:]
        moves = [(x_hbm, x_ref), (p_hbm.at[first], p_ref)]
        if leaf_core:
            moves.append((c_hbm.at[first], rest.pop(0)))
        moves += [(w_hbm.at[first], w_out), (p_hbm.at[first - 1], p_out)]
        for group, out in zip(groups, rest):
            start = 0
            for level, n in group:
                moves.append((c_hbm.at[level, 0:n], out.at[start : start + n]))
                start += n
        copies = [pltpu.make_async_copy(a, b, sems.at[at]) for at, (a, b) in enumerate(moves)]
        for copy in copies:
            copy.start()
        copies[0].wait()
        state = x_ref[...].T
        state_out[...] = state
        copies[1].wait()
        q_out[...] = three_passes(state, p_ref[...], 0)
        for copy in copies[2:]:
            copy.wait()

    count = 4 + (1 if leaf_core else 0) + sum(len(group) for group in groups)
    return pl.pallas_call(
        body,
        in_specs=[IN_HBM] * 4,
        out_specs=[IN_VMEM] * len(shapes),
        out_shape=[pltpu.VMEM(shape, jnp.float32) for shape in shapes],
        scratch_shapes=[
            pltpu.VMEM((rows, width), jnp.float32),
            pltpu.VMEM((rows, rank), jnp.float32),
            pltpu.SemaphoreType.DMA((count,)),
        ],
        compiler_params=pltpu.CompilerParams(vmem_limit_bytes=52 * 2**20),
        cost_estimate=pl.CostEstimate(
            flops=6 * rows * width * rank, bytes_accessed=2**22, transcendentals=0
        ),
        name="begin",
    )(rhs, proj_bases, corr_bases, cores)


def finish(state, corr, held):
    width, rows = state.shape

    def body(x_ref, w_ref, t_ref, out_ref):
        out_ref[...] = (x_ref[...] - three_passes(t_ref[...], w_ref[...], 1)).T

    return pl.pallas_call(
        body,
        in_specs=[IN_VMEM] * 3,
        out_specs=IN_VMEM,
        out_shape=jax.ShapeDtypeStruct((rows, width), jnp.float32),
        compiler_params=pltpu.CompilerParams(vmem_limit_bytes=24 * 2**20),
        cost_estimate=pl.CostEstimate(
            flops=6 * rows * width * corr.shape[1], bytes_accessed=2**21, transcendentals=0
        ),
        name="finish",
    )(state, corr, held)


def on_device(rhs, proj_bases, corr_bases, cores):
    count = lax.axis_size("leaf")
    me = lax.axis_index("leaf")
    rows_here, width = rhs.shape
    rank = proj_bases.shape[2]
    bits = [(count >> level).bit_length() - 2 for level in range(LEVELS)]
    first = LEVELS - 1
    chain = [level for level in reversed(range(LEVELS)) if bits[level] > 0]

    def low(bit):
        return (me >> bit) & 1 == 0

    parity = me & 1
    for bit in range(1, count.bit_length() - 1):
        parity = parity ^ ((me >> bit) & 1)
    upper = parity == 0

    def across(value, bit):
        return exchange(value, (1 << bit) | (1 if bit > 0 else 0))

    def chip_sum(value):
        half = width // 2
        keep = jnp.where(upper, value[:half], value[half:])
        send = jnp.where(upper, value[half:], value[:half])
        return keep + exchange(send, 1)

    def chip_gather(value):
        return pair_up(upper, value, exchange(value, 1), 0)

    heads = [(level, rank >> bits[level]) for level in chain if bits[level] == 1]
    tails = [(level, rank >> bits[level]) for level in chain if bits[level] > 1]
    groups = [group for group in (heads, tails) if group]
    leaf_core = bits[first] == 0
    value, state, top_corr, next_proj, *fetched = begin(
        rhs, proj_bases, corr_bases, cores, first, leaf_core, groups
    )

    table = {}
    if leaf_core:
        table[first] = fetched.pop(0)

    def finish_table(level, mine):
        part = exchange(mine, 1)
        both = jnp.where(low(0), jnp.stack([mine, part], 1), jnp.stack([part, mine], 1))
        table[level] = both.reshape(rank, 2 * rank)

    block = fetched[-1][None]
    coming = None
    waiting = [level for level, _ in tails]
    gather_bit = 1

    def send(after):
        nonlocal coming
        if waiting and coming is None:
            coming = exchange(tie(block, after), 1 << gather_bit)

    def join(after):
        nonlocal block, coming, waiting, gather_bit
        block = pair_up(low(gather_bit), block, tie(coming, after), 0)
        coming = None
        gather_bit += 1
        done = [level for level in waiting if bits[level] == gather_bit]
        waiting = [level for level in waiting if level not in done]
        start = 0
        for level in done:
            finish_table(level, block[:, start : start + (rank >> gather_bit)])
            start += rank >> gather_bit
        block = block[:, start:]

    def solve(level, value):
        for bit in range(1, bits[level]):
            value = value + across(value, bit)
        while level not in table:
            send(value)
            join(value)
        top = bits[level]
        stacked = pair_up(low(top), value, across(value, top), 1)
        stacked = stacked / jnp.sqrt(jnp.float32(rows_here << top))
        return times_transposed(stacked, table[level])

    def update(corr, state, held):
        return state - jnp.einsum("ka,na->kn", held, corr, precision=HIGH)

    if leaf_core:
        top = pair_up(low(0), value, exchange(value, 1), 1)
        top = top / jnp.sqrt(jnp.float32(rows_here))
        held = times_transposed(top, table[first])
    else:
        held = chip_gather(solve(first, chip_sum(value)))
    state = update(top_corr, state, held)
    value = chip_sum(project(next_proj, state))
    if heads:
        finish_table(heads[0][0], tie(fetched[0], value)[None])
    for level in reversed(range(first)):
        start = value
        held = solve(level, value)
        if level > 0:
            projs, corrs = lax.optimization_barrier((proj_bases, corr_bases, start))[:2]
            ahead = chip_sum(project(projs[level - 1], state))
            own = jnp.einsum("na,nb->ab", projs[level - 1], corrs[level], precision=HIGH)
            if level == first - 1:
                send(own)
            value = ahead - times_transposed(held, own + exchange(own, 1))
            send(value)
            state = update(corrs[level], state, chip_gather(held))
    return finish(state, corr_bases[0], chip_gather(held))


def solution(mesh):
    return jax.shard_map(
        on_device,
        mesh=mesh,
        in_specs=(
            P("leaf", None),
            P(None, "leaf", None),
            P(None, "leaf", None),
            P(None, "leaf", None),
        ),
        out_specs=P("leaf", None),
        check_vma=False,
    )
```

profile of v0, /device:TPU:0, one launch (start us, length us, event | category | flops | bytes accessed | tf_op | source)
XLA Modules:
  0.0 70.4 jit_solution(8281455177479237570)
XLA Ops:
  0.0 2.3 %begin.1 = (f32[128,256]{1,0:T(8,128)S(1)}, f32[128,1024]{1,0:T(8,128)S(1)}, f32[1024,256]{1,0:T(8,128)S(1)}, f32[1024,256]{1,0:T(8,128)S(1)}, f32[256,512]{1,0:...) custom-call(f32[1024,128]{1,0:T(8,128)} %x_hbm.1, f32[5,1024,256]{2,1,0:T(8,128)} %p_hbm.1, ...), custom_call_target="tpu_custom_call" | custom-call | flops 201326592 | bytes 4194304 | tf_op jit(solution)/shard_map/begin/pallas_call | solution.py:88
  2.3 0.7 copy-done
  3.0 0.5 collective-permute-start
  3.5 1.1 %collective-permute-done = f32[128,256]{1,0:T(8,128)} collective-permute-done((f32[128,256]{1,0:T(8,128)S(1)}, f32[128,256]{1,0:T(8,128)}, u32[]{:S(2)}, u32[]{:S(2)}) %collective-permute-start) | collective-permute-done | bytes 131104 | tf_op jit(solution)/shard_map/ppermute | solution.py:16
  4.6 1.4 %fusion.31 = f32[128,256]{1,0:T(8,128)S(1)} fusion(f32[256,512]{1,0:T(8,128)S(1)} %get-tuple-element.27, f32[128,256]{1,0:T(8,128)} %collective-permute-done, f32[128,256]{1,0:T(8,128)S(1)} %get-tuple-element.26, pred[]{:T(512)S(6)} %eq.12), kind=kOutput, calls=%fused_computation.43 | convolution fusion | flops 100925440 | bytes 917505 | tf_op jit(solution)/shard_map/kb,ab->ka/dot_general | solution.py:36
  6.0 0.7 convolution_subtract_fusion.3
  6.7 0.4 fusion.117
  7.1 0.4 copy-done.3
  7.5 0.4 collective-permute-start.1
  7.9 0.9 %collective-permute-done.1 = f32[64,256]{1,0:T(8,128)S(1)} collective-permute-done((f32[64,256]{1,0:T(8,128)S(1)}, f32[64,256]{1,0:T(8,128)S(1)}, u32[]{:S(2)}, u32[]{:S(2)}) %collective-permute-start.1) | collective-permute-done | bytes 65568 | tf_op jit(solution)/shard_map/ppermute | solution.py:16
  8.8 2.7 %collective-permute-start.2 = (f32[64,256]{1,0:T(8,128)S(1)}, f32[64,256]{1,0:T(8,128)S(1)}, u32[]{:S(2)}, u32[]{:S(2)}) collective-permute-start(f32[64,256]{1,0:T(8,128)S(1)} %select_add_fusion), channel_id=1, source_target_pairs={{0,3},{1,2},{2,1},{3,0},{4,7},{5,6},{6,5},{7,4},{8,11},{9,10},{10,... | collective-permute-start | bytes 196616 | tf_op jit(solution)/shard_map/ppermute | solution.py:16
  11.5 1.8 %fusion.14 = f32[128,256]{1,0:T(8,128)S(1)} fusion(f32[128,1024]{1,0:T(8,128)} %copy-done.3, f32[5,1024,256]{2,1,0:T(8,128)} %p_hbm.1), kind=kOutput, calls=%fused_computation.18 | convolution fusion | flops 201326592 | bytes 1703936 | tf_op jit(solution)/shard_map/kn,nr->kr/dot_general | solution.py:32
  13.3 0.4 collective-permute-start.3
  13.7 2.5 %fusion.12 = f32[256,256]{1,0:T(8,128)S(1)} fusion(f32[5,1024,256]{2,1,0:T(8,128)} %p_hbm.1, f32[5,1024,256]{2,1,0:T(8,128)} %w_hbm.1), kind=kOutput, calls=%fused_computation.16 | convolution fusion | flops 402653184 | bytes 2359296 | tf_op jit(solution)/shard_map/na,nb->ab/dot_general | solution.py:224
  16.2 0.2 collective-permute-start.6
  16.5 0.4 collective-permute-start.5
  16.9 0.5 collective-permute-start.9
  17.5 0.4 fusion.45
  17.9 0.1 collective-permute-start.4
  18.0 0.3 add_subtract_fusion.2
  18.3 1.6 %collective-permute-start.7 = (f32[64,256]{1,0:T(8,128)S(1)}, f32[64,256]{1,0:T(8,128)S(1)}, u32[]{:S(2)}, u32[]{:S(2)}) collective-permute-start(f32[64,256]{1,0:T(8,128)S(1)} %add_subtract_fusion.2), channel_id=1, source_target_pairs={{0,3},{1,2},{2,1},{3,0},{4,7},{5,6},{6,5},{7,4},{8,11},{9,10},{10,... | collective-permute-start | bytes 196616 | tf_op jit(solution)/shard_map/ppermute | solution.py:16
  19.9 2.2 %fusion.6 = f32[256,256]{1,0:T(8,128)S(1)} fusion(f32[5,1024,256]{2,1,0:T(8,128)} %p_hbm.1, f32[5,1024,256]{2,1,0:T(8,128)S(1)} %copy-done.2), kind=kOutput, calls=%fused_computation.10 | convolution fusion | flops 402653184 | bytes 2359296 | tf_op jit(solution)/shard_map/na,nb->ab/dot_general | solution.py:224
  22.1 0.1 collective-permute-start.13
  22.2 2.9 %collective-permute-done.7 = f32[64,256]{1,0:T(8,128)S(1)} collective-permute-done((f32[64,256]{1,0:T(8,128)S(1)}, f32[64,256]{1,0:T(8,128)S(1)}, u32[]{:S(2)}, u32[]{:S(2)}) %collective-permute-start.7) | collective-permute-done | bytes 65568 | tf_op jit(solution)/shard_map/ppermute | solution.py:16
  25.2 1.8 %collective-permute-start.8 = (f32[64,256]{1,0:T(8,128)S(1)}, f32[64,256]{1,0:T(8,128)S(1)}, u32[]{:S(2)}, u32[]{:S(2)}) collective-permute-start(f32[64,256]{1,0:T(8,128)S(1)} %add.42), channel_id=1, source_target_pairs={{0,5},{1,4},{2,7},{3,6},{4,1},{5,0},{6,3},{7,2},{8,13},{9,12},{10,... | collective-permute-start | bytes 196616 | tf_op jit(solution)/shard_map/ppermute | solution.py:16
  27.0 0.1 slice_bitcast_fusion.3
  27.1 0.1 collective-permute-start.10
  27.2 0.7 convolution_subtract_fusion.2
  27.9 0.4 fusion.8
  28.3 0.5 collective-permute-start.12
  29.0 0.4 fusion.58
  29.4 0.6 collective-permute-start.11
  30.0 0.3 add_subtract_fusion.1
  30.3 0.8 %collective-permute-start.14 = (f32[64,256]{1,0:T(8,128)S(1)}, f32[64,256]{1,0:T(8,128)S(1)}, u32[]{:S(2)}, u32[]{:S(2)}) collective-permute-start(f32[64,256]{1,0:T(8,128)S(1)} %add_subtract_fusion.1), channel_id=1, source_target_pairs={{0,3},{1,2},{2,1},{3,0},{4,7},{5,6},{6,5},{7,4},{8,11},{9,10},{10,... | collective-permute-start | bytes 196616 | tf_op jit(solution)/shard_map/ppermute | solution.py:16
  31.1 1.0 %fusion = f32[256,256]{1,0:T(8,128)S(1)} fusion(f32[5,1024,256]{2,1,0:T(8,128)S(1)} %bitcast.70, f32[5,1024,256]{2,1,0:T(8,128)S(1)} %copy-done.2), kind=kOutput, calls=%fused_computation.4 | convolution fusion | flops 402653184 | bytes 2359296 | tf_op jit(solution)/shard_map/na,nb->ab/dot_general | solution.py:224
  32.1 0.4 collective-permute-start.21
  32.4 1.4 %collective-permute-start.17 = (f32[2,48,512]{2,1,0:T(8,128)S(1)}, f32[2,48,512]{2,1,0:T(8,128)S(1)}, u32[]{:S(2)}, u32[]{:S(2)}) collective-permute-start(f32[2,48,512]{2,1,0:T(8,128)S(1)} %slice.97), channel_id=1, source_target_pairs={{0,4},{1,5},{2,6},{3,7},{4,0},{5,1},{6,2},{7,3},{8,12},{9,13},{10,... | collective-permute-start | bytes 589832 | tf_op jit(solution)/shard_map/ppermute | solution.py:16
  33.8 0.6 collective-permute-done.14
  34.4 1.4 %collective-permute-start.15 = (f32[64,256]{1,0:T(8,128)S(1)}, f32[64,256]{1,0:T(8,128)S(1)}, u32[]{:S(2)}, u32[]{:S(2)}) collective-permute-start(f32[64,256]{1,0:T(8,128)S(1)} %add.45), channel_id=1, source_target_pairs={{0,5},{1,4},{2,7},{3,6},{4,1},{5,0},{6,3},{7,2},{8,13},{9,12},{10,... | collective-permute-start | bytes 196616 | tf_op jit(solution)/shard_map/ppermute | solution.py:16
  35.9 0.7 convolution_subtract_fusion.1
  36.5 3.6 %collective-permute-done.15 = f32[64,256]{1,0:T(8,128)S(1)} collective-permute-done((f32[64,256]{1,0:T(8,128)S(1)}, f32[64,256]{1,0:T(8,128)S(1)}, u32[]{:S(2)}, u32[]{:S(2)}) %collective-permute-start.15) | collective-permute-done | bytes 65568 | tf_op jit(solution)/shard_map/ppermute | solution.py:16
  40.2 0.6 collective-permute-start.18
  40.9 0.4 fusion.2
  41.3 0.1 collective-permute-start.20
  41.4 1.5 %collective-permute-start.16 = (f32[64,256]{1,0:T(8,128)S(1)}, f32[64,256]{1,0:T(8,128)S(1)}, u32[]{:S(2)}, u32[]{:S(2)}) collective-permute-start(f32[64,256]{1,0:T(8,128)S(1)} %add.46), channel_id=1, source_target_pairs={{0,9},{1,8},{2,11},{3,10},{4,13},{5,12},{6,15},{7,14},{8,1},{9,0},... | collective-permute-start | bytes 196616 | tf_op jit(solution)/shard_map/ppermute | solution.py:16
  42.9 2.3 %collective-permute-done.16 = f32[64,256]{1,0:T(8,128)S(1)} collective-permute-done((f32[64,256]{1,0:T(8,128)S(1)}, f32[64,256]{1,0:T(8,128)S(1)}, u32[]{:S(2)}, u32[]{:S(2)}) %collective-permute-start.16) | collective-permute-done | bytes 65568 | tf_op jit(solution)/shard_map/ppermute | solution.py:16
  45.2 0.4 fusion.71
  45.6 0.3 add_subtract_fusion
  45.9 1.1 %collective-permute-start.22 = (f32[64,256]{1,0:T(8,128)S(1)}, f32[64,256]{1,0:T(8,128)S(1)}, u32[]{:S(2)}, u32[]{:S(2)}) collective-permute-start(f32[64,256]{1,0:T(8,128)S(1)} %add_subtract_fusion), channel_id=1, source_target_pairs={{0,3},{1,2},{2,1},{3,0},{4,7},{5,6},{6,5},{7,4},{8,11},{9,10},{10,... | collective-permute-start | bytes 196616 | tf_op jit(solution)/shard_map/ppermute | solution.py:16
  47.1 2.8 %collective-permute-done.22 = f32[64,256]{1,0:T(8,128)S(1)} collective-permute-done((f32[64,256]{1,0:T(8,128)S(1)}, f32[64,256]{1,0:T(8,128)S(1)}, u32[]{:S(2)}, u32[]{:S(2)}) %collective-permute-start.22) | collective-permute-done | bytes 65568 | tf_op jit(solution)/shard_map/ppermute | solution.py:16
  50.0 1.2 %collective-permute-start.23 = (f32[64,256]{1,0:T(8,128)S(1)}, f32[64,256]{1,0:T(8,128)S(1)}, u32[]{:S(2)}, u32[]{:S(2)}) collective-permute-start(f32[64,256]{1,0:T(8,128)S(1)} %add.49), channel_id=1, source_target_pairs={{0,5},{1,4},{2,7},{3,6},{4,1},{5,0},{6,3},{7,2},{8,13},{9,12},{10,... | collective-permute-start | bytes 196616 | tf_op jit(solution)/shard_map/ppermute | solution.py:16
  51.2 1.6 %collective-permute-start.26 = (f32[4,16,512]{2,1,0:T(8,128)S(1)}, f32[4,16,512]{2,1,0:T(8,128)S(1)}, u32[]{:S(2)}, u32[]{:S(2)}) collective-permute-start(f32[4,16,512]{2,1,0:T(8,128)S(1)} %get-tuple-element.43), channel_id=1, source_target_pairs={{0,8},{1,9},{2,10},{3,11},{4,12},{5,13},{6,14},{7,15},{8,0},{9,1},... | collective-permute-start | bytes 393224 | tf_op jit(solution)/shard_map/ppermute | solution.py:16
  52.7 1.3 %collective-permute-done.23 = f32[64,256]{1,0:T(8,128)S(1)} collective-permute-done((f32[64,256]{1,0:T(8,128)S(1)}, f32[64,256]{1,0:T(8,128)S(1)}, u32[]{:S(2)}, u32[]{:S(2)}) %collective-permute-start.23) | collective-permute-done | bytes 65568 | tf_op jit(solution)/shard_map/ppermute | solution.py:16
  54.0 1.3 %collective-permute-start.24 = (f32[64,256]{1,0:T(8,128)S(1)}, f32[64,256]{1,0:T(8,128)S(1)}, u32[]{:S(2)}, u32[]{:S(2)}) collective-permute-start(f32[64,256]{1,0:T(8,128)S(1)} %add.50), channel_id=1, source_target_pairs={{0,9},{1,8},{2,11},{3,10},{4,13},{5,12},{6,15},{7,14},{8,1},{9,0},... | collective-permute-start | bytes 196616 | tf_op jit(solution)/shard_map/ppermute | solution.py:16
  55.3 2.9 %collective-permute-done.24 = f32[64,256]{1,0:T(8,128)S(1)} collective-permute-done((f32[64,256]{1,0:T(8,128)S(1)}, f32[64,256]{1,0:T(8,128)S(1)}, u32[]{:S(2)}, u32[]{:S(2)}) %collective-permute-start.24) | collective-permute-done | bytes 65568 | tf_op jit(solution)/shard_map/ppermute | solution.py:16
  58.2 0.2 collective-permute-start.27
  58.4 1.3 %slice_bitcast_fusion.w_ref = f32[1024,256]{1,0:T(8,128)S(1)} fusion(f32[5,1024,256]{2,1,0:T(8,128)} %w_hbm.1), kind=kLoop, calls=%fused_computation.22 | loop fusion | bytes 2097152 | tf_op jit(solution)/shard_map/squeeze | solution.py:230
  59.7 0.4 collective-permute-start.19
  60.2 2.1 %collective-permute-start.25 = (f32[64,256]{1,0:T(8,128)S(1)}, f32[64,256]{1,0:T(8,128)S(1)}, u32[]{:S(2)}, u32[]{:S(2)}) collective-permute-start(f32[64,256]{1,0:T(8,128)S(1)} %add.51), channel_id=1, source_target_pairs={{0,17},{1,16},{2,19},{3,18},{4,21},{5,20},{6,23},{7,22},{8,25},{9,... | collective-permute-start | bytes 196616 | tf_op jit(solution)/shard_map/ppermute | solution.py:16
  62.4 4.1 %collective-permute-done.25 = f32[64,256]{1,0:T(8,128)S(1)} collective-permute-done((f32[64,256]{1,0:T(8,128)S(1)}, f32[64,256]{1,0:T(8,128)S(1)}, u32[]{:S(2)}, u32[]{:S(2)}) %collective-permute-start.25) | collective-permute-done | bytes 65568 | tf_op jit(solution)/shard_map/ppermute | solution.py:16
  66.5 0.4 fusion.84
  66.9 0.2 collective-permute-start.28
  67.1 1.9 %convolution_subtract_fusion.x_ref = f32[128,1024]{1,0:T(8,128)S(1)} fusion(f32[128,1024]{1,0:T(8,128)S(1)} %convolution_subtract_fusion.1, f32[5,1024,256]{2,1,0:T(8,128)} %w_hbm.1, f32[64,256]{1,0:T(8,128)S(1)} %collective-permute-done.19, f32[64,256]{1,0:T(8,128)S(1)} %fusion.71, pred[]{:T(512)S(6)} %eq.26), kind=kOutput, calls=%fused_computation | convolution fusion | flops 201555968 | bytes 2228225 | tf_op jit(solution)/shard_map/ka,na->kn/dot_general | solution.py:206
  69.0 1.4 %finish.1 = f32[1024,128]{1,0:T(8,128)} custom-call(f32[128,1024]{1,0:T(8,128)S(1)} %convolution_subtract_fusion.x_ref, f32[1024,256]{1,0:T(8,128)S(1)} %slice_bitcast_fusion.w_ref, f32[128,256]{1,0:T(8,128)S(1)} %maximum_select_fusion.19.t_ref), custom_call_target="tpu_custom_call" | custom-call | flops 201326592 | bytes 2097152 | tf_op jit(solution)/shard_map/finish/pallas_call | solution.py:112
  (58 shorter events, 0.7 us)
Async XLA Ops:
  2.3 0.7 copy-start
  3.0 1.6 %collective-permute-start = (f32[128,256]{1,0:T(8,128)S(1)}, f32[128,256]{1,0:T(8,128)}, u32[]{:S(2)}, u32[]{:S(2)}) collective-permute-start(f32[128,256]{1,0:T(8,128)S(1)} %get-tuple-element.26), channel_id=1, source_target_pairs={{0,1},{1,0},{2,3},{3,2},{4,5},{5,4},{6,7},{7,6},{8,9},{9,8},{10,11... | collective-permute-start | bytes 393224 | tf_op jit(solution)/shard_map/ppermute | solution.py:16
  6.0 10.9 %copy-start.1 = (f32[112,512]{1,0:T(8,128)S(1)}, f32[112,512]{1,0:T(8,128)}, u32[]{:S(2)}) copy-start(f32[112,512]{1,0:T(8,128)} %copy-done) | copy-start | bytes 688132
  6.7 0.8 %copy-start.3 = (f32[128,1024]{1,0:T(8,128)}, f32[128,1024]{1,0:T(8,128)S(1)}, u32[]{:S(2)}) copy-start(f32[128,1024]{1,0:T(8,128)S(1)} %convolution_subtract_fusion.3) | copy-start | bytes 1572868
  6.7 21.2 %slice-start = ((s8[5242880]{0:T(1024)(128)(4,1)}), s8[1048576]{0:T(1024)(128)(4,1)S(1)}, s32[]{:S(2)}) async-start(s8[5242880]{0:T(1024)(128)(4,1)} %bitcast.69), calls=%async_computation | async-start | bytes 2097152
  7.5 1.3 %collective-permute-start.1 = (f32[64,256]{1,0:T(8,128)S(1)}, f32[64,256]{1,0:T(8,128)S(1)}, u32[]{:S(2)}, u32[]{:S(2)}) collective-permute-start(f32[64,256]{1,0:T(8,128)S(1)} %slice_select_fusion.3), channel_id=1, source_target_pairs={{0,1},{1,0},{2,3},{3,2},{4,5},{5,4},{6,7},{7,6},{8,9},{9,8},{10,11... | collective-permute-start | bytes 196616 | tf_op jit(solution)/shard_map/ppermute | solution.py:16
  7.9 12.0 %copy-start.2 = (f32[5,1024,256]{2,1,0:T(8,128)S(1)}, f32[5,1024,256]{2,1,0:T(8,128)}, u32[]{:S(2)}) copy-start(f32[5,1024,256]{2,1,0:T(8,128)} %w_hbm.1) | copy-start | bytes 15728644
  8.8 18.4 %copy-start.4 = (f32[128,1024]{1,0:T(8,128)S(1)}, f32[128,1024]{1,0:T(8,128)}, u32[]{:S(2)}) copy-start(f32[128,1024]{1,0:T(8,128)} %copy-done.3) | copy-start | bytes 1572868
  8.8 8.7 %collective-permute-start.2 = (f32[64,256]{1,0:T(8,128)S(1)}, f32[64,256]{1,0:T(8,128)S(1)}, u32[]{:S(2)}, u32[]{:S(2)}) collective-permute-start(f32[64,256]{1,0:T(8,128)S(1)} %select_add_fusion), channel_id=1, source_target_pairs={{0,3},{1,2},{2,1},{3,0},{4,7},{5,6},{6,5},{7,4},{8,11},{9,10},{10,... | collective-permute-start | bytes 196616 | tf_op jit(solution)/shard_map/ppermute | solution.py:16
  13.3 4.1 %collective-permute-start.3 = (f32[1,128,512]{2,1,0:T(8,128)S(1)}, f32[1,128,512]{2,1,0:T(8,128)S(1)}, u32[]{:S(2)}, u32[]{:S(2)}) collective-permute-start(f32[1,128,512]{2,1,0:T(8,128)S(1)} %bitcast.65), channel_id=1, source_target_pairs={{0,1},{1,0},{2,3},{3,2},{4,5},{5,4},{6,7},{7,6},{8,9},{9,8},{10,11... | collective-permute-start | bytes 786440 | tf_op jit(solution)/shard_map/ppermute | solution.py:16
  16.2 1.8 %collective-permute-start.6 = (f32[256,256]{1,0:T(8,128)S(1)}, f32[256,256]{1,0:T(8,128)S(1)}, u32[]{:S(2)}, u32[]{:S(2)}) collective-permute-start(f32[256,256]{1,0:T(8,128)S(1)} %fusion.12), channel_id=1, source_target_pairs={{0,1},{1,0},{2,3},{3,2},{4,5},{5,4},{6,7},{7,6},{8,9},{9,8},{10,11... | collective-permute-start | bytes 786440 | tf_op jit(solution)/shard_map/ppermute | solution.py:16
  16.5 1.5 %collective-permute-start.5 = (f32[64,256]{1,0:T(8,128)S(1)}, f32[64,256]{1,0:T(8,128)S(1)}, u32[]{:S(2)}, u32[]{:S(2)}) collective-permute-start(f32[64,256]{1,0:T(8,128)S(1)} %slice_select_fusion.2), channel_id=1, source_target_pairs={{0,1},{1,0},{2,3},{3,2},{4,5},{5,4},{6,7},{7,6},{8,9},{9,8},{10,11... | collective-permute-start | bytes 196616 | tf_op jit(solution)/shard_map/ppermute | solution.py:16
  16.9 10.1 %collective-permute-start.9 = (f32[1,112,512]{2,1,0:T(8,128)S(1)}, f32[1,112,512]{2,1,0:T(8,128)S(1)}, u32[]{:S(2)}, u32[]{:S(2)}) collective-permute-start(f32[1,112,512]{2,1,0:T(8,128)S(1)} %bitcast.67), channel_id=1, source_target_pairs={{0,2},{1,3},{2,0},{3,1},{4,6},{5,7},{6,4},{7,5},{8,10},{9,11},{10,... | collective-permute-start | bytes 688136 | tf_op jit(solution)/shard_map/ppermute | solution.py:16
  17.5 10.4 %slice-start.1 = ((s8[5242880]{0:T(1024)(128)(4,1)}), s8[4194304]{0:T(1024)(128)(4,1)S(1)}, s32[]{:S(2)}) async-start(s8[5242880]{0:T(1024)(128)(4,1)} %bitcast.69), calls=%async_computation.1 | async-start | bytes 8388608
  17.9 9.3 %collective-permute-start.4 = (f32[64,256]{1,0:T(8,128)S(1)}, f32[64,256]{1,0:T(8,128)S(1)}, u32[]{:S(2)}, u32[]{:S(2)}) collective-permute-start(f32[64,256]{1,0:T(8,128)S(1)} %fusion.45), channel_id=1, source_target_pairs={{0,1},{1,0},{2,3},{3,2},{4,5},{5,4},{6,7},{7,6},{8,9},{9,8},{10,11... | collective-permute-start | bytes 196616 | tf_op jit(solution)/shard_map/ppermute | solution.py:16
  18.3 6.9 %collective-permute-start.7 = (f32[64,256]{1,0:T(8,128)S(1)}, f32[64,256]{1,0:T(8,128)S(1)}, u32[]{:S(2)}, u32[]{:S(2)}) collective-permute-start(f32[64,256]{1,0:T(8,128)S(1)} %add_subtract_fusion.2), channel_id=1, source_target_pairs={{0,3},{1,2},{2,1},{3,0},{4,7},{5,6},{6,5},{7,4},{8,11},{9,10},{10,... | collective-permute-start | bytes 196616 | tf_op jit(solution)/shard_map/ppermute | solution.py:16
  22.1 7.9 %collective-permute-start.13 = (f32[256,256]{1,0:T(8,128)S(1)}, f32[256,256]{1,0:T(8,128)S(1)}, u32[]{:S(2)}, u32[]{:S(2)}) collective-permute-start(f32[256,256]{1,0:T(8,128)S(1)} %fusion.6), channel_id=1, source_target_pairs={{0,1},{1,0},{2,3},{3,2},{4,5},{5,4},{6,7},{7,6},{8,9},{9,8},{10,11... | collective-permute-start | bytes 786440 | tf_op jit(solution)/shard_map/ppermute | solution.py:16
  25.2 3.8 %collective-permute-start.8 = (f32[64,256]{1,0:T(8,128)S(1)}, f32[64,256]{1,0:T(8,128)S(1)}, u32[]{:S(2)}, u32[]{:S(2)}) collective-permute-start(f32[64,256]{1,0:T(8,128)S(1)} %add.42), channel_id=1, source_target_pairs={{0,5},{1,4},{2,7},{3,6},{4,1},{5,0},{6,3},{7,2},{8,13},{9,12},{10,... | collective-permute-start | bytes 196616 | tf_op jit(solution)/shard_map/ppermute | solution.py:16
  27.1 1.8 %collective-permute-start.10 = (f32[2,64,512]{2,1,0:T(8,128)S(1)}, f32[2,64,512]{2,1,0:T(8,128)S(1)}, u32[]{:S(2)}, u32[]{:S(2)}) collective-permute-start(f32[2,64,512]{2,1,0:T(8,128)S(1)} %get-tuple-element.46), channel_id=1, source_target_pairs={{0,1},{1,0},{2,3},{3,2},{4,5},{5,4},{6,7},{7,6},{8,9},{9,8},{10,11... | collective-permute-start | bytes 786440 | tf_op jit(solution)/shard_map/ppermute | solution.py:16
  28.3 1.7 %collective-permute-start.12 = (f32[64,256]{1,0:T(8,128)S(1)}, f32[64,256]{1,0:T(8,128)S(1)}, u32[]{:S(2)}, u32[]{:S(2)}) collective-permute-start(f32[64,256]{1,0:T(8,128)S(1)} %slice_select_fusion.1), channel_id=1, source_target_pairs={{0,1},{1,0},{2,3},{3,2},{4,5},{5,4},{6,7},{7,6},{8,9},{9,8},{10,11... | collective-permute-start | bytes 196616 | tf_op jit(solution)/shard_map/ppermute | solution.py:16
  29.4 6.5 %collective-permute-start.11 = (f32[64,256]{1,0:T(8,128)S(1)}, f32[64,256]{1,0:T(8,128)S(1)}, u32[]{:S(2)}, u32[]{:S(2)}) collective-permute-start(f32[64,256]{1,0:T(8,128)S(1)} %fusion.58), channel_id=1, source_target_pairs={{0,1},{1,0},{2,3},{3,2},{4,5},{5,4},{6,7},{7,6},{8,9},{9,8},{10,11... | collective-permute-start | bytes 196616 | tf_op jit(solution)/shard_map/ppermute | solution.py:16
  30.3 4.1 %collective-permute-start.14 = (f32[64,256]{1,0:T(8,128)S(1)}, f32[64,256]{1,0:T(8,128)S(1)}, u32[]{:S(2)}, u32[]{:S(2)}) collective-permute-start(f32[64,256]{1,0:T(8,128)S(1)} %add_subtract_fusion.1), channel_id=1, source_target_pairs={{0,3},{1,2},{2,1},{3,0},{4,7},{5,6},{6,5},{7,4},{8,11},{9,10},{10,... | collective-permute-start | bytes 196616 | tf_op jit(solution)/shard_map/ppermute | solution.py:16
  32.1 13.6 %collective-permute-start.21 = (f32[256,256]{1,0:T(8,128)S(1)}, f32[256,256]{1,0:T(8,128)S(1)}, u32[]{:S(2)}, u32[]{:S(2)}) collective-permute-start(f32[256,256]{1,0:T(8,128)S(1)} %fusion), channel_id=1, source_target_pairs={{0,1},{1,0},{2,3},{3,2},{4,5},{5,4},{6,7},{7,6},{8,9},{9,8},{10,11... | collective-permute-start | bytes 786440 | tf_op jit(solution)/shard_map/ppermute | solution.py:16
  32.4 7.7 %collective-permute-start.17 = (f32[2,48,512]{2,1,0:T(8,128)S(1)}, f32[2,48,512]{2,1,0:T(8,128)S(1)}, u32[]{:S(2)}, u32[]{:S(2)}) collective-permute-start(f32[2,48,512]{2,1,0:T(8,128)S(1)} %slice.97), channel_id=1, source_target_pairs={{0,4},{1,5},{2,6},{3,7},{4,0},{5,1},{6,2},{7,3},{8,12},{9,13},{10,... | collective-permute-start | bytes 589832 | tf_op jit(solution)/shard_map/ppermute | solution.py:16
  34.4 5.7 %collective-permute-start.15 = (f32[64,256]{1,0:T(8,128)S(1)}, f32[64,256]{1,0:T(8,128)S(1)}, u32[]{:S(2)}, u32[]{:S(2)}) collective-permute-start(f32[64,256]{1,0:T(8,128)S(1)} %add.45), channel_id=1, source_target_pairs={{0,5},{1,4},{2,7},{3,6},{4,1},{5,0},{6,3},{7,2},{8,13},{9,12},{10,... | collective-permute-start | bytes 196616 | tf_op jit(solution)/shard_map/ppermute | solution.py:16
  40.2 2.6 %collective-permute-start.18 = (f32[4,32,512]{2,1,0:T(8,128)S(1)}, f32[4,32,512]{2,1,0:T(8,128)S(1)}, u32[]{:S(2)}, u32[]{:S(2)}) collective-permute-start(f32[4,32,512]{2,1,0:T(8,128)S(1)} %get-tuple-element.50), channel_id=1, source_target_pairs={{0,1},{1,0},{2,3},{3,2},{4,5},{5,4},{6,7},{7,6},{8,9},{9,8},{10,11... | collective-permute-start | bytes 786440 | tf_op jit(solution)/shard_map/ppermute | solution.py:16
  41.3 4.3 %collective-permute-start.20 = (f32[64,256]{1,0:T(8,128)S(1)}, f32[64,256]{1,0:T(8,128)S(1)}, u32[]{:S(2)}, u32[]{:S(2)}) collective-permute-start(f32[64,256]{1,0:T(8,128)S(1)} %slice_select_fusion), channel_id=1, source_target_pairs={{0,1},{1,0},{2,3},{3,2},{4,5},{5,4},{6,7},{7,6},{8,9},{9,8},{10,11... | collective-permute-start | bytes 196616 | tf_op jit(solution)/shard_map/ppermute | solution.py:16
  41.4 3.9 %collective-permute-start.16 = (f32[64,256]{1,0:T(8,128)S(1)}, f32[64,256]{1,0:T(8,128)S(1)}, u32[]{:S(2)}, u32[]{:S(2)}) collective-permute-start(f32[64,256]{1,0:T(8,128)S(1)} %add.46), channel_id=1, source_target_pairs={{0,9},{1,8},{2,11},{3,10},{4,13},{5,12},{6,15},{7,14},{8,1},{9,0},... | collective-permute-start | bytes 196616 | tf_op jit(solution)/shard_map/ppermute | solution.py:16
  45.9 4.0 %collective-permute-start.22 = (f32[64,256]{1,0:T(8,128)S(1)}, f32[64,256]{1,0:T(8,128)S(1)}, u32[]{:S(2)}, u32[]{:S(2)}) collective-permute-start(f32[64,256]{1,0:T(8,128)S(1)} %add_subtract_fusion), channel_id=1, source_target_pairs={{0,3},{1,2},{2,1},{3,0},{4,7},{5,6},{6,5},{7,4},{8,11},{9,10},{10,... | collective-permute-start | bytes 196616 | tf_op jit(solution)/shard_map/ppermute | solution.py:16
  50.0 4.1 %collective-permute-start.23 = (f32[64,256]{1,0:T(8,128)S(1)}, f32[64,256]{1,0:T(8,128)S(1)}, u32[]{:S(2)}, u32[]{:S(2)}) collective-permute-start(f32[64,256]{1,0:T(8,128)S(1)} %add.49), channel_id=1, source_target_pairs={{0,5},{1,4},{2,7},{3,6},{4,1},{5,0},{6,3},{7,2},{8,13},{9,12},{10,... | collective-permute-start | bytes 196616 | tf_op jit(solution)/shard_map/ppermute | solution.py:16
  51.2 7.0 %collective-permute-start.26 = (f32[4,16,512]{2,1,0:T(8,128)S(1)}, f32[4,16,512]{2,1,0:T(8,128)S(1)}, u32[]{:S(2)}, u32[]{:S(2)}) collective-permute-start(f32[4,16,512]{2,1,0:T(8,128)S(1)} %get-tuple-element.43), channel_id=1, source_target_pairs={{0,8},{1,9},{2,10},{3,11},{4,12},{5,13},{6,14},{7,15},{8,0},{9,1},... | collective-permute-start | bytes 393224 | tf_op jit(solution)/shard_map/ppermute | solution.py:16
  54.0 4.1 %collective-permute-start.24 = (f32[64,256]{1,0:T(8,128)S(1)}, f32[64,256]{1,0:T(8,128)S(1)}, u32[]{:S(2)}, u32[]{:S(2)}) collective-permute-start(f32[64,256]{1,0:T(8,128)S(1)} %add.50), channel_id=1, source_target_pairs={{0,9},{1,8},{2,11},{3,10},{4,13},{5,12},{6,15},{7,14},{8,1},{9,0},... | collective-permute-start | bytes 196616 | tf_op jit(solution)/shard_map/ppermute | solution.py:16
  58.2 4.1 %collective-permute-start.27 = (f32[8,16,512]{2,1,0:T(8,128)S(1)}, f32[8,16,512]{2,1,0:T(8,128)S(1)}, u32[]{:S(2)}, u32[]{:S(2)}) collective-permute-start(f32[8,16,512]{2,1,0:T(8,128)S(1)} %maximum_select_fusion.8), channel_id=1, source_target_pairs={{0,1},{1,0},{2,3},{3,2},{4,5},{5,4},{6,7},{7,6},{8,9},{9,8},{10,11... | collective-permute-start | bytes 786440 | tf_op jit(solution)/shard_map/ppermute | solution.py:16
  59.7 7.4 %collective-permute-start.19 = (f32[64,256]{1,0:T(8,128)S(1)}, f32[64,256]{1,0:T(8,128)S(1)}, u32[]{:S(2)}, u32[]{:S(2)}) collective-permute-start(f32[64,256]{1,0:T(8,128)S(1)} %fusion.71), channel_id=1, source_target_pairs={{0,1},{1,0},{2,3},{3,2},{4,5},{5,4},{6,7},{7,6},{8,9},{9,8},{10,11... | collective-permute-start | bytes 196616 | tf_op jit(solution)/shard_map/ppermute | solution.py:16
  60.2 6.4 %collective-permute-start.25 = (f32[64,256]{1,0:T(8,128)S(1)}, f32[64,256]{1,0:T(8,128)S(1)}, u32[]{:S(2)}, u32[]{:S(2)}) collective-permute-start(f32[64,256]{1,0:T(8,128)S(1)} %add.51), channel_id=1, source_target_pairs={{0,17},{1,16},{2,19},{3,18},{4,21},{5,20},{6,23},{7,22},{8,25},{9,... | collective-permute-start | bytes 196616 | tf_op jit(solution)/shard_map/ppermute | solution.py:16
  66.9 2.1 %collective-permute-start.28 = (f32[64,256]{1,0:T(8,128)S(1)}, f32[64,256]{1,0:T(8,128)S(1)}, u32[]{:S(2)}, u32[]{:S(2)}) collective-permute-start(f32[64,256]{1,0:T(8,128)S(1)} %fusion.84), channel_id=1, source_target_pairs={{0,1},{1,0},{2,3},{3,2},{4,5},{5,4},{6,7},{7,6},{8,9},{9,8},{10,11... | collective-permute-start | bytes 196616 | tf_op jit(solution)/shard_map/ppermute | solution.py:16
where the time goes:
time: 70.7 us; the launch traced here: 70.4 us
  starting transfers between devices  24.3 us (34%)
  waiting for transfers between devices  22.6 us (32%)
  matrix products  16.3 us (23%)
  Pallas kernels  3.68 us (5%)
  local copies, waits for them, and re-layouts  2.62 us (4%)
    ppermute x29, starting transfers between devices, exchange(): return lax.ppermute(value, 'leaf', pairs)  24.3 us
    ppermute x29, waiting for transfers between devices, exchange(): return lax.ppermute(value, 'leaf', pairs)  22.6 us
    dot_general x3, matrix products, on_device(): jnp.einsum('na,nb->ab', projs[level - 1], corrs[level], precision=HIGH)  5.74 us
    dot_general x4, matrix products, update(): return state - jnp.einsum('ka,na->kn', held, corr, precision=HIGH)  3.86 us
    dot_general x8, matrix products, times_transposed(): return jnp.einsum('kb,ab->ka', left, right, precision=HIGH)  3.72 us
    dot_general x4, matrix products, project(): return jnp.einsum('kn,nr->kr', state, basis, precision=HIGH)  3.01 us
    pallas_call x1, Pallas kernels, begin(): pl.pallas_call(body, in_specs=[IN_HBM] * 4, out_specs=[IN_VMEM] * len(sha...  2.33 us
  transfers between devices with their start and end apart: 29, of which 10 were waited for; matrix products, arithmetic and copies ran while one was open for 22% of the time, Pallas kernels for 0%

commit v1 on v0

--- a/solution.py
+++ b/solution.py
@@ -56,14 +56,14 @@
 def begin(rhs, proj_bases, corr_bases, cores, first, leaf_core, groups):
     rows, width = rhs.shape
     rank = proj_bases.shape[2]
-    shapes = [(width, rank), (width, rows), (rows, rank), (rows, rank)]
+    shapes = [(width, rank), (width, rows)] + [(rows, rank)] * 4
     shapes += [(rank, 2 * rank)] if leaf_core else []
     shapes += [(sum(n for _, n in group), 2 * rank) for group in groups]
 
     def body(x_hbm, p_hbm, w_hbm, c_hbm, *refs):
         outs, (x_ref, p_ref, sems) = list(refs[: len(shapes)]), refs[len(shapes) :]
-        q_out, state_out, w_out, p_out = outs[:4]
-        rest = outs[4:]
+        q_out, state_out, w_out, p_out, w_next, p_next = outs[:6]
+        rest = outs[6:]
         moves = [(x_hbm, x_ref), (p_hbm.at[first], p_ref)]
         if leaf_core:
             moves.append((c_hbm.at[first], rest.pop(0)))
@@ -73,6 +73,7 @@
             for level, n in group:
                 moves.append((c_hbm.at[level, 0:n], out.at[start : start + n]))
                 start += n
+        moves += [(w_hbm.at[first - 1], w_next), (p_hbm.at[first - 2], p_next)]
         copies = [pltpu.make_async_copy(a, b, sems.at[at]) for at, (a, b) in enumerate(moves)]
         for copy in copies:
             copy.start()
@@ -84,7 +85,7 @@
         for copy in copies[2:]:
             copy.wait()
 
-    count = 4 + (1 if leaf_core else 0) + sum(len(group) for group in groups)
+    count = 6 + (1 if leaf_core else 0) + sum(len(group) for group in groups)
     return pl.pallas_call(
         body,
         in_specs=[IN_HBM] * 4,
@@ -103,6 +104,31 @@
     )(rhs, proj_bases, corr_bases, cores)
 
 
+def fetch(corr_bases, after):
+    rows, rank = corr_bases.shape[1:]
+
+    def body(w_hbm, _, one, zero, sems):
+        copies = [
+            pltpu.make_async_copy(w_hbm.at[level], out, sems.at[level])
+            for level, out in enumerate((zero, one))
+        ]
+        for copy in copies:
+            copy.start()
+        for copy in copies:
+            copy.wait()
+
+    return pl.pallas_call(
+        body,
+        in_specs=[IN_HBM, pl.BlockSpec(memory_space=pl.ANY)],
+        out_specs=[IN_VMEM] * 2,
+        out_shape=[pltpu.VMEM((rows, rank), jnp.float32)] * 2,
+        scratch_shapes=[pltpu.SemaphoreType.DMA((2,))],
+        compiler_params=pltpu.CompilerParams(vmem_limit_bytes=32 * 2**20),
+        cost_estimate=pl.CostEstimate(flops=0, bytes_accessed=2**22, transcendentals=0),
+        name="fetch",
+    )(corr_bases, after)
+
+
 def finish(state, corr, held):
     width, rows = state.shape
 
@@ -155,7 +181,7 @@
     tails = [(level, rank >> bits[level]) for level in chain if bits[level] > 1]
     groups = [group for group in (heads, tails) if group]
     leaf_core = bits[first] == 0
-    value, state, top_corr, next_proj, *fetched = begin(
+    value, state, top_corr, next_proj, next_corr, after_proj, *fetched = begin(
         rhs, proj_bases, corr_bases, cores, first, leaf_core, groups
     )
 
@@ -168,36 +194,46 @@
         both = jnp.where(low(0), jnp.stack([mine, part], 1), jnp.stack([part, mine], 1))
         table[level] = both.reshape(rank, 2 * rank)
 
-    block = fetched[-1][None]
-    coming = None
-    waiting = [level for level, _ in tails]
-    gather_bit = 1
-
-    def send(after):
-        nonlocal coming
-        if waiting and coming is None:
-            coming = exchange(tie(block, after), 1 << gather_bit)
-
-    def join(after):
-        nonlocal block, coming, waiting, gather_bit
-        block = pair_up(low(gather_bit), block, tie(coming, after), 0)
-        coming = None
-        gather_bit += 1
-        done = [level for level in waiting if bits[level] == gather_bit]
-        waiting = [level for level in waiting if level not in done]
-        start = 0
-        for level in done:
-            finish_table(level, block[:, start : start + (rank >> gather_bit)])
-            start += rank >> gather_bit
-        block = block[:, start:]
-
-    def solve(level, value):
-        for bit in range(1, bits[level]):
+    def gather_steps():
+        block = fetched[-1][None]
+        waiting = [level for level, _ in tails]
+        bit = 1
+        coming = exchange(block, 2)
+        while True:
+            after = yield
+            block = pair_up(low(bit), block, tie(coming, after), 0)
+            bit += 1
+            after = yield
+            rows = rank >> bit
+            for level in [level for level in waiting if bits[level] == bit]:
+                finish_table(level, tie(block[:, :rows], after))
+                block = block[:, rows:]
+            waiting = [level for level in waiting if bits[level] > bit]
+            if waiting:
+                coming = exchange(tie(block, after), 1 << bit)
+            else:
+                return
+
+    steps = gather_steps()
+    next(steps)
+
+    def step(after):
+        try:
+            steps.send(after)
+        except StopIteration:
+            pass
+
+    def solve(level, value, ahead_of):
+        top = bits[level]
+        for bit in range(1, top):
+            value = ahead_of.get(bit, lambda v: v)(value)
             value = value + across(value, bit)
         while level not in table:
-            send(value)
-            join(value)
-        top = bits[level]
+            step(value)
+        if top > 1:
+            step(value)
+            step(value)
+        value = ahead_of.get(top, lambda v: v)(value)
         stacked = pair_up(low(top), value, across(value, top), 1)
         stacked = stacked / jnp.sqrt(jnp.float32(rows_here << top))
         return times_transposed(stacked, table[level])
@@ -210,24 +246,35 @@
         top = top / jnp.sqrt(jnp.float32(rows_here))
         held = times_transposed(top, table[first])
     else:
-        held = chip_gather(solve(first, chip_sum(value)))
+        held = chip_gather(solve(first, chip_sum(value), {}))
     state = update(top_corr, state, held)
     value = chip_sum(project(next_proj, state))
     if heads:
+        step(value)
         finish_table(heads[0][0], tie(fetched[0], value)[None])
-    for level in reversed(range(first)):
+    for level in reversed(range(1, first)):
         start = value
-        held = solve(level, value)
-        if level > 0:
+        held = solve(level, value, {})
+        if level == first - 1:
+            proj, corr = tie(after_proj, start), tie(next_corr, start)
+        else:
             projs, corrs = lax.optimization_barrier((proj_bases, corr_bases, start))[:2]
-            ahead = chip_sum(project(projs[level - 1], state))
-            own = jnp.einsum("na,nb->ab", projs[level - 1], corrs[level], precision=HIGH)
-            if level == first - 1:
-                send(own)
-            value = ahead - times_transposed(held, own + exchange(own, 1))
-            send(value)
-            state = update(corrs[level], state, chip_gather(held))
-    return finish(state, corr_bases[0], chip_gather(held))
+            proj, corr = projs[level - 1], corrs[level]
+        ahead = chip_sum(project(proj, state))
+        own = jnp.einsum("na,nb->ab", proj, corr, precision=HIGH)
+        if heads and level == first - 1:
+            step(own)
+        value = ahead - times_transposed(held, own + exchange(own, 1))
+        if level > 1:
+            state = update(corr, state, chip_gather(held))
+    one_corr, zero_corr = fetch(corr_bases, value)
+    state = update(one_corr, state, chip_gather(held))
+    ahead_of = {
+        bits[0] - 1: lambda v: lax.optimization_barrier((v, one_corr, zero_corr))[0],
+        bits[0]: lambda v: tie(v, state),
+    }
+    held = solve(0, value, ahead_of)
+    return finish(state, zero_corr, chip_gather(held))
 
 
 def solution(mesh):

time: 70.7 us -> 78.5 us (1.11)
  starting transfers between devices: 24.3 us -> 18.6 us
  waiting for transfers between devices: 22.6 us -> 27.6 us
  local copies, waits for them, and re-layouts: 2.62 us -> 7.59 us
  other arithmetic: 0.4 us -> 3.14 us
  Pallas kernels: 3.68 us -> 4.57 us
    unnamed x14 -> x26, local copies, waits for them, and re-layouts: 1.07 us -> 7.41 us
    ppermute x29, starting transfers between devices: 24.3 us -> 18.6 us  [exchange(): return lax.ppermute(value, 'leaf', pairs)]
    ppermute x29, waiting for transfers between devices: 22.6 us -> 27.6 us  [exchange(): return lax.ppermute(value, 'leaf', pairs)]
    dot_general x3, matrix products: 5.74 us -> 4.21 us  [on_device(): own = jnp.einsum('na,nb->ab', proj, corr, precision=HIGH)]
    squeeze x1 -> x0, local copies, waits for them, and re-layouts: 1.29 us -> none  [on_device(): return finish(state, corr_bases[0], chip_gather(held))]
    select_n x5 -> x4, other arithmetic: 0.12 us -> 1.4 us  [pair_up(): jnp.where(low, jnp.concatenate([mine, other], axis), jnp.concatenate([oth...]
    dot_general x4, matrix products: 3.01 us -> 4.04 us  [project(): return jnp.einsum('kn,nr->kr', state, basis, precision=HIGH)]
    add x1, other arithmetic: 0.01 us -> 0.85 us  [chip_sum(): return keep + exchange(send, 1)]
  transfers between devices with their start and end apart: 29 -> 29, of which waited for: 10 -> 11; matrix products, arithmetic and copies ran while one was open for 22% -> 17% of each run, Pallas kernels for 0% -> 0%
where the time goes in v1:
time: 78.5 us; the launch traced here: 78.1 us
  waiting for transfers between devices  27.6 us (35%)
  starting transfers between devices  18.6 us (24%)
  matrix products  16.2 us (21%)
  local copies, waits for them, and re-layouts  7.59 us (10%)
  Pallas kernels  4.57 us (6%)
  other arithmetic  3.14 us (4%)
    ppermute x29, waiting for transfers between devices, exchange(): return lax.ppermute(value, 'leaf', pairs)  27.6 us
    ppermute x29, starting transfers between devices, exchange(): return lax.ppermute(value, 'leaf', pairs)  18.6 us
    unnamed x26, local copies, waits for them, and re-layouts  7.41 us
    dot_general x3, matrix products, on_device(): own = jnp.einsum('na,nb->ab', proj, corr, precision=HIGH)  4.21 us
    dot_general x4, matrix products, project(): return jnp.einsum('kn,nr->kr', state, basis, precision=HIGH)  4.04 us
    dot_general x4, matrix products, update(): return state - jnp.einsum('ka,na->kn', held, corr, precision=HIGH)  4 us
    dot_general x8, matrix products, times_transposed(): return jnp.einsum('kb,ab->ka', left, right, precision=HIGH)  3.99 us
    pallas_call x1, Pallas kernels, begin(): pl.pallas_call(body, in_specs=[IN_HBM] * 4, out_specs=[IN_VMEM] * len(sha...  3.05 us
  transfers between devices with their start and end apart: 29, of which 11 were waited for; matrix products, arithmetic and copies ran while one was open for 17% of the time, Pallas kernels for 0%

profile of v1, /device:TPU:0, one launch (start us, length us, event | category | flops | bytes accessed | tf_op | source)
XLA Modules:
  0.0 78.1 jit_solution(2978819850378581353)
XLA Ops:
  0.0 3.0 %begin.1 = (f32[128,256]{1,0:T(8,128)S(1)}, f32[128,1024]{1,0:T(8,128)S(1)}, f32[1024,256]{1,0:T(8,128)S(1)}, f32[1024,256]{1,0:T(8,128)S(1)}, f32[1024,256]{1,0...) custom-call(f32[1024,128]{1,0:T(8,128)} %x_hbm.1, ...), custom_call_target="tpu_custom_call" | custom-call | flops 201326592 | bytes 4194304 | tf_op jit(solution)/shard_map/begin/pallas_call | solution.py:89
  3.1 1.0 %copy-done.1 = f32[1024,256]{1,0:T(8,128)} copy-done((f32[1024,256]{1,0:T(8,128)}, f32[1024,256]{1,0:T(8,128)S(1)}, u32[]{:S(2)}) %copy-start.1) | copy-done | bytes 1048600
  4.1 1.0 %copy-done.2 = f32[1024,256]{1,0:T(8,128)} copy-done((f32[1024,256]{1,0:T(8,128)}, f32[1024,256]{1,0:T(8,128)S(1)}, u32[]{:S(2)}) %copy-start.2) | copy-done | bytes 1048600
  5.1 0.7 copy-done.5
  5.8 0.8 %copy-done.3 = f32[128,1024]{1,0:T(8,128)} copy-done((f32[128,1024]{1,0:T(8,128)}, f32[128,1024]{1,0:T(8,128)S(1)}, u32[]{:S(2)}) %copy-start.3) | copy-done | bytes 524312
  6.5 0.5 collective-permute-start
  7.0 1.0 %collective-permute-done = f32[128,256]{1,0:T(8,128)S(1)} collective-permute-done((f32[128,256]{1,0:T(8,128)S(1)}, f32[128,256]{1,0:T(8,128)S(1)}, u32[]{:S(2)}, u32[]{:S(2)}) %collective-permute-start) | collective-permute-done | bytes 131104 | tf_op jit(solution)/shard_map/ppermute | solution.py:16
  8.0 0.6 copy-done.8
  8.6 1.7 %fusion.19 = f32[128,256]{1,0:T(8,128)S(1)} fusion(f32[256,512]{1,0:T(8,128)} %copy-done.4, f32[128,256]{1,0:T(8,128)} %copy-done.8, f32[128,256]{1,0:T(8,128)S(1)} %get-tuple-element.34, pred[]{:T(512)S(6)} %eq.12), kind=kOutput, calls=%fused_computation.30 | convolution fusion | flops 100925440 | bytes 917505 | tf_op jit(solution)/shard_map/kb,ab->ka/dot_general | solution.py:36
  10.3 2.0 %convolution_subtract_fusion.3 = f32[128,1024]{1,0:T(8,128)S(1)} fusion(f32[128,1024]{1,0:T(8,128)} %copy-done.3, f32[128,256]{1,0:T(8,128)S(1)} %fusion.19, f32[1024,256]{1,0:T(8,128)} %copy-done.1), kind=kOutput, calls=%fused_computation.3 | convolution fusion | flops 201457664 | bytes 2228224 | tf_op jit(solution)/shard_map/ka,na->kn/dot_general | solution.py:242
  12.3 0.8 %copy-done.6 = f32[128,1024]{1,0:T(8,128)} copy-done((f32[128,1024]{1,0:T(8,128)}, f32[128,1024]{1,0:T(8,128)S(1)}, u32[]{:S(2)}) %copy-start.6) | copy-done | bytes 524312
  13.1 1.6 %fusion.105 = f32[128,256]{1,0:T(8,128)S(1)} fusion(f32[128,1024]{1,0:T(8,128)S(1)} %convolution_subtract_fusion.3, f32[1024,256]{1,0:T(8,128)} %copy-done.2), kind=kOutput, calls=%fused_computation.128 | convolution fusion | flops 201326592 | bytes 1703936 | tf_op jit(solution)/shard_map/kn,nr->kr/dot_general | solution.py:32
  14.7 0.6 slice_select_fusion.3
  15.4 0.4 collective-permute-start.1
  15.7 2.6 %collective-permute-start.9 = (f32[1,112,512]{2,1,0:T(8,128)}, f32[1,112,512]{2,1,0:T(8,128)}, u32[]{:S(2)}, u32[]{:S(2)}) collective-permute-start(f32[1,112,512]{2,1,0:T(8,128)} %bitcast.56), channel_id=1, source_target_pairs={{0,2},{1,3},{2,0},{3,1},{4,6},{5,7},{6,4},{7,5},{8,10},{9,11},{10,... | collective-permute-start | bytes 688136 | tf_op jit(solution)/shard_map/ppermute | solution.py:16
  18.4 0.9 %select_add_fusion = f32[64,256]{1,0:T(8,128)S(1)} fusion(f32[64,256]{1,0:T(8,128)} %collective-permute-done.1, f32[128,256]{1,0:T(8,128)S(1)} %fusion.105, pred[]{:T(512)S(6)} %eq.26), kind=kLoop, calls=%fused_computation.103 | loop fusion | flops 32768 | bytes 262145 | tf_op jit(solution)/shard_map/add | solution.py:175
  19.2 1.3 %collective-permute-start.2 = (f32[64,256]{1,0:T(8,128)S(1)}, f32[64,256]{1,0:T(8,128)S(1)}, u32[]{:S(2)}, u32[]{:S(2)}) collective-permute-start(f32[64,256]{1,0:T(8,128)S(1)} %select_add_fusion), channel_id=1, source_target_pairs={{0,3},{1,2},{2,1},{3,0},{4,7},{5,6},{6,5},{7,4},{8,11},{9,10},{10,... | collective-permute-start | bytes 196616 | tf_op jit(solution)/shard_map/ppermute | solution.py:16
  20.5 1.6 %fusion.106 = f32[128,256]{1,0:T(8,128)S(1)} fusion(f32[128,1024]{1,0:T(8,128)} %copy-done.6, f32[1024,256]{1,0:T(8,128)S(1)} %get-tuple-element.43), kind=kOutput, calls=%fused_computation.129 | convolution fusion | flops 201326592 | bytes 1703936 | tf_op jit(solution)/shard_map/kn,nr->kr/dot_general | solution.py:32
  22.1 1.0 %fusion.107 = f32[256,256]{1,0:T(8,128)S(1)} fusion(f32[1024,256]{1,0:T(8,128)S(1)} %get-tuple-element.43, f32[1024,256]{1,0:T(8,128)S(1)} %get-tuple-element.41), kind=kOutput, calls=%fused_computation.130 | convolution fusion | flops 402653184 | bytes 2359296 | tf_op jit(solution)/shard_map/na,nb->ab/dot_general | solution.py:264
  23.1 0.4 collective-permute-start.6
  23.7 0.4 collective-permute-start.5
  24.1 1.0 %collective-permute-done.9 = f32[1,112,512]{2,1,0:T(8,128)} collective-permute-done((f32[1,112,512]{2,1,0:T(8,128)}, f32[1,112,512]{2,1,0:T(8,128)}, u32[]{:S(2)}, u32[]{:S(2)}) %collective-permute-start.9) | collective-permute-done | bytes 229408 | tf_op jit(solution)/shard_map/ppermute | solution.py:16
  25.1 1.3 %maximum_select_fusion.4 = f32[2,112,512]{2,1,0:T(8,128)S(1)} fusion(f32[1,112,512]{2,1,0:T(8,128)} %collective-permute-done.9, f32[1,112,512]{2,1,0:T(8,128)} %bitcast.57, pred[]{:T(512)S(6)} %eq.27), kind=kLoop, calls=%fused_computation.26 | loop fusion | flops 344064 | bytes 917505 | tf_op jit(solution)/shard_map/jit(_where)/select_n | solution.py:24
  26.6 2.1 %collective-permute-start.17 = (f32[2,48,512]{2,1,0:T(8,128)S(1)}, f32[2,48,512]{2,1,0:T(8,128)S(1)}, u32[]{:S(2)}, u32[]{:S(2)}) collective-permute-start(f32[2,48,512]{2,1,0:T(8,128)S(1)} %slice.79), channel_id=1, source_target_pairs={{0,4},{1,5},{2,6},{3,7},{4,0},{5,1},{6,2},{7,3},{8,12},{9,13},{10,... | collective-permute-start | bytes 589832 | tf_op jit(solution)/shard_map/ppermute | solution.py:16
  28.8 0.4 fusion.33
  29.4 0.3 add_subtract_fusion.2
  29.7 1.5 %collective-permute-start.7 = (f32[64,256]{1,0:T(8,128)S(1)}, f32[64,256]{1,0:T(8,128)S(1)}, u32[]{:S(2)}, u32[]{:S(2)}) collective-permute-start(f32[64,256]{1,0:T(8,128)S(1)} %add_subtract_fusion.2), channel_id=1, source_target_pairs={{0,3},{1,2},{2,1},{3,0},{4,7},{5,6},{6,5},{7,4},{8,11},{9,10},{10,... | collective-permute-start | bytes 196616 | tf_op jit(solution)/shard_map/ppermute | solution.py:16
  31.2 2.2 %fusion.5 = f32[256,256]{1,0:T(8,128)S(1)} fusion(f32[5,1024,256]{2,1,0:T(8,128)} %p_hbm.1, f32[5,1024,256]{2,1,0:T(8,128)S(1)} %bitcast.53), kind=kOutput, calls=%fused_computation.9 | convolution fusion | flops 402653184 | bytes 2359296 | tf_op jit(solution)/shard_map/na,nb->ab/dot_general | solution.py:264
  33.4 0.2 collective-permute-start.13
  33.7 0.7 convolution_subtract_fusion.2
  34.4 0.4 fusion.7
  34.9 0.5 collective-permute-start.8
  35.4 3.4 %collective-permute-done.8 = f32[64,256]{1,0:T(8,128)S(1)} collective-permute-done((f32[64,256]{1,0:T(8,128)S(1)}, f32[64,256]{1,0:T(8,128)S(1)}, u32[]{:S(2)}, u32[]{:S(2)}) %collective-permute-start.8) | collective-permute-done | bytes 65568 | tf_op jit(solution)/shard_map/ppermute | solution.py:16
  38.9 0.4 fusion.46
  39.2 0.3 collective-permute-start.11
  39.7 0.3 collective-permute-start.12
  40.0 0.3 collective-permute-start.18
  40.2 1.6 %collective-permute-start.26 = (f32[4,16,512]{2,1,0:T(8,128)S(1)}, f32[4,16,512]{2,1,0:T(8,128)S(1)}, u32[]{:S(2)}, u32[]{:S(2)}) collective-permute-start(f32[4,16,512]{2,1,0:T(8,128)S(1)} %slice.83), channel_id=1, source_target_pairs={{0,8},{1,9},{2,10},{3,11},{4,12},{5,13},{6,14},{7,15},{8,0},{9,1},... | collective-permute-start | bytes 393224 | tf_op jit(solution)/shard_map/ppermute | solution.py:16
  41.8 0.7 convolution_subtract_fusion.1
  42.5 0.3 add_subtract_fusion.1
  43.0 1.0 %fusion = f32[256,256]{1,0:T(8,128)S(1)} fusion(f32[5,1024,256]{2,1,0:T(8,128)S(1)} %bitcast.53, f32[5,1024,256]{2,1,0:T(8,128)S(1)} %bitcast.59), kind=kOutput, calls=%fused_computation.4 | convolution fusion | flops 402653184 | bytes 2359296 | tf_op jit(solution)/shard_map/na,nb->ab/dot_general | solution.py:264
  44.0 0.6 collective-permute-start.21
  44.6 0.4 fusion.3
  45.0 2.1 %collective-permute-done.14 = f32[64,256]{1,0:T(8,128)S(1)} collective-permute-done((f32[64,256]{1,0:T(8,128)S(1)}, f32[64,256]{1,0:T(8,128)S(1)}, u32[]{:S(2)}, u32[]{:S(2)}) %collective-permute-start.14) | collective-permute-done | bytes 65568 | tf_op jit(solution)/shard_map/ppermute | solution.py:16
  47.2 0.3 collective-permute-start.15
  47.5 0.5 collective-permute-start.20
  47.9 3.4 %collective-permute-done.15 = f32[64,256]{1,0:T(8,128)S(1)} collective-permute-done((f32[64,256]{1,0:T(8,128)S(1)}, f32[64,256]{1,0:T(8,128)S(1)}, u32[]{:S(2)}, u32[]{:S(2)}) %collective-permute-start.15) | collective-permute-done | bytes 65568 | tf_op jit(solution)/shard_map/ppermute | solution.py:16
  51.5 4.0 %collective-permute-done.16 = f32[64,256]{1,0:T(8,128)S(1)} collective-permute-done((f32[64,256]{1,0:T(8,128)S(1)}, f32[64,256]{1,0:T(8,128)S(1)}, u32[]{:S(2)}, u32[]{:S(2)}) %collective-permute-start.16) | collective-permute-done | bytes 65568 | tf_op jit(solution)/shard_map/ppermute | solution.py:16
  55.5 0.4 fusion.59
  55.9 0.3 add_subtract_fusion._
  56.2 0.3 collective-permute-start.22
  56.5 0.4 collective-permute-start.19
  56.9 3.4 %collective-permute-done.22 = f32[64,256]{1,0:T(8,128)S(1)} collective-permute-done((f32[64,256]{1,0:T(8,128)S(1)}, f32[64,256]{1,0:T(8,128)S(1)}, u32[]{:S(2)}, u32[]{:S(2)}) %collective-permute-start.22) | collective-permute-done | bytes 65568 | tf_op jit(solution)/shard_map/ppermute | solution.py:16
  60.3 0.3 collective-permute-start.23
  60.7 0.4 collective-permute-start.27
  61.1 2.5 %copy-done = f32[5,1024,256]{2,1,0:T(8,128)S(1)} copy-done((f32[5,1024,256]{2,1,0:T(8,128)S(1)}, f32[5,1024,256]{2,1,0:T(8,128)}, u32[]{:S(2)}) %copy-start) | copy-done | bytes 5242904
  63.8 0.7 collective-permute-done.23
  64.6 0.7 convolution_subtract_fusion.x_ref
  65.3 3.4 %collective-permute-done.24 = f32[64,256]{1,0:T(8,128)S(1)} collective-permute-done((f32[64,256]{1,0:T(8,128)S(1)}, f32[64,256]{1,0:T(8,128)S(1)}, u32[]{:S(2)}, u32[]{:S(2)}) %collective-permute-start.24) | collective-permute-done | bytes 65568 | tf_op jit(solution)/shard_map/ppermute | solution.py:16
  68.7 2.4 %collective-permute-start.25 = (f32[64,256]{1,0:T(8,128)S(1)}, f32[64,256]{1,0:T(8,128)S(1)}, u32[]{:S(2)}, u32[]{:S(2)}) collective-permute-start(f32[64,256]{1,0:T(8,128)S(1)} %add.51), channel_id=1, source_target_pairs={{0,17},{1,16},{2,19},{3,18},{4,21},{5,20},{6,23},{7,22},{8,25},{9,... | collective-permute-start | bytes 196616 | tf_op jit(solution)/shard_map/ppermute | solution.py:16
  71.2 3.9 %collective-permute-done.25 = f32[64,256]{1,0:T(8,128)S(1)} collective-permute-done((f32[64,256]{1,0:T(8,128)S(1)}, f32[64,256]{1,0:T(8,128)S(1)}, u32[]{:S(2)}, u32[]{:S(2)}) %collective-permute-start.25) | collective-permute-done | bytes 65568 | tf_op jit(solution)/shard_map/ppermute | solution.py:16
  75.1 0.4 fusion.72
  75.6 1.1 %collective-permute-done.28 = f32[64,256]{1,0:T(8,128)S(1)} collective-permute-done((f32[64,256]{1,0:T(8,128)S(1)}, f32[64,256]{1,0:T(8,128)S(1)}, u32[]{:S(2)}, u32[]{:S(2)}) %collective-permute-start.28) | collective-permute-done | bytes 65568 | tf_op jit(solution)/shard_map/ppermute | solution.py:16
  76.8 1.4 %finish.1 = f32[1024,128]{1,0:T(8,128)} custom-call(f32[128,1024]{1,0:T(8,128)S(1)} %convolution_subtract_fusion.x_ref, f32[1024,256]{1,0:T(8,128)S(1)} %get-tuple-element.55.w_ref, f32[128,256]{1,0:T(8,128)S(1)} %maximum_select_fusion.18.t_ref), custom_call_target="tpu_custom_call" | custom-call | flops 201326592 | bytes 2097152 | tf_op jit(solution)/shard_map/finish/pallas_call | solution.py:138
  (70 shorter events, 1.7 us)
Async XLA Ops:
  3.1 1.0 %copy-start.1 = (f32[1024,256]{1,0:T(8,128)}, f32[1024,256]{1,0:T(8,128)S(1)}, u32[]{:S(2)}) copy-start(f32[1024,256]{1,0:T(8,128)S(1)} %get-tuple-element.36) | copy-start | bytes 3145732
  4.1 1.0 %copy-start.2 = (f32[1024,256]{1,0:T(8,128)}, f32[1024,256]{1,0:T(8,128)S(1)}, u32[]{:S(2)}) copy-start(f32[1024,256]{1,0:T(8,128)S(1)} %get-tuple-element.37) | copy-start | bytes 3145732
  5.1 0.7 copy-start.5
  5.7 0.8 %copy-start.3 = (f32[128,1024]{1,0:T(8,128)}, f32[128,1024]{1,0:T(8,128)S(1)}, u32[]{:S(2)}) copy-start(f32[128,1024]{1,0:T(8,128)S(1)} %get-tuple-element.33) | copy-start | bytes 1572868
  5.7 1.2 %copy-start.4 = (f32[256,512]{1,0:T(8,128)}, f32[256,512]{1,0:T(8,128)S(1)}, u32[]{:S(2)}) copy-start(f32[256,512]{1,0:T(8,128)S(1)} %get-tuple-element.35) | copy-start | bytes 1572868
  6.5 1.4 %collective-permute-start = (f32[128,256]{1,0:T(8,128)S(1)}, f32[128,256]{1,0:T(8,128)S(1)}, u32[]{:S(2)}, u32[]{:S(2)}) collective-permute-start(f32[128,256]{1,0:T(8,128)S(1)} %get-tuple-element.34), channel_id=1, source_target_pairs={{0,1},{1,0},{2,3},{3,2},{4,5},{5,4},{6,7},{7,6},{8,9},{9,8},{10,11... | collective-permute-start | bytes 393224 | tf_op jit(solution)/shard_map/ppermute | solution.py:16
  8.0 0.6 copy-start.8
  8.6 22.5 %slice-start = ((s8[5242880]{0:T(1024)(128)(4,1)}), s8[1048576]{0:T(1024)(128)(4,1)S(1)}, s32[]{:S(2)}) async-start(s8[5242880]{0:T(1024)(128)(4,1)} %bitcast.52), calls=%async_computation | async-start | bytes 2097152
  12.3 0.8 %copy-start.6 = (f32[128,1024]{1,0:T(8,128)}, f32[128,1024]{1,0:T(8,128)S(1)}, u32[]{:S(2)}) copy-start(f32[128,1024]{1,0:T(8,128)S(1)} %convolution_subtract_fusion.3) | copy-start | bytes 1572868
  15.4 3.0 %collective-permute-start.1 = (f32[64,256]{1,0:T(8,128)}, f32[64,256]{1,0:T(8,128)}, u32[]{:S(2)}, u32[]{:S(2)}) collective-permute-start(f32[64,256]{1,0:T(8,128)} %slice_select_fusion.3), channel_id=1, source_target_pairs={{0,1},{1,0},{2,3},{3,2},{4,5},{5,4},{6,7},{7,6},{8,9},{9,8},{10,11... | collective-permute-start | bytes 196616 | tf_op jit(solution)/shard_map/ppermute | solution.py:16
  15.7 9.4 %collective-permute-start.9 = (f32[1,112,512]{2,1,0:T(8,128)}, f32[1,112,512]{2,1,0:T(8,128)}, u32[]{:S(2)}, u32[]{:S(2)}) collective-permute-start(f32[1,112,512]{2,1,0:T(8,128)} %bitcast.56), channel_id=1, source_target_pairs={{0,2},{1,3},{2,0},{3,1},{4,6},{5,7},{6,4},{7,5},{8,10},{9,11},{10,... | collective-permute-start | bytes 688136 | tf_op jit(solution)/shard_map/ppermute | solution.py:16
  19.2 9.5 %collective-permute-start.2 = (f32[64,256]{1,0:T(8,128)S(1)}, f32[64,256]{1,0:T(8,128)S(1)}, u32[]{:S(2)}, u32[]{:S(2)}) collective-permute-start(f32[64,256]{1,0:T(8,128)S(1)} %select_add_fusion), channel_id=1, source_target_pairs={{0,3},{1,2},{2,1},{3,0},{4,7},{5,6},{6,5},{7,4},{8,11},{9,10},{10,... | collective-permute-start | bytes 196616 | tf_op jit(solution)/shard_map/ppermute | solution.py:16
  20.5 10.7 %slice-start.1 = ((s8[5242880]{0:T(1024)(128)(4,1)}), s8[4194304]{0:T(1024)(128)(4,1)S(1)}, s32[]{:S(2)}) async-start(s8[5242880]{0:T(1024)(128)(4,1)} %bitcast.52), calls=%async_computation.1 | async-start | bytes 8388608
  20.5 13.9 %slice-start.2 = ((s8[5242880]{0:T(1024)(128)(4,1)}), s8[4194304]{0:T(1024)(128)(4,1)S(1)}, s32[]{:S(2)}) async-start(s8[5242880]{0:T(1024)(128)(4,1)} %bitcast.58), calls=%async_computation.2 | async-start | bytes 8388608
  22.1 11.6 %copy-start.7 = (f32[128,1024]{1,0:T(8,128)S(1)}, f32[128,1024]{1,0:T(8,128)}, u32[]{:S(2)}) copy-start(f32[128,1024]{1,0:T(8,128)} %copy-done.6) | copy-start | bytes 1572868
  23.1 6.2 %collective-permute-start.6 = (f32[256,256]{1,0:T(8,128)S(1)}, f32[256,256]{1,0:T(8,128)S(1)}, u32[]{:S(2)}, u32[]{:S(2)}) collective-permute-start(f32[256,256]{1,0:T(8,128)S(1)} %fusion.107), channel_id=1, source_target_pairs={{0,1},{1,0},{2,3},{3,2},{4,5},{5,4},{6,7},{7,6},{8,9},{9,8},{10,11... | collective-permute-start | bytes 786440 | tf_op jit(solution)/shard_map/ppermute | solution.py:16
  23.5 3.1 %collective-permute-start.3 = (f32[1,128,512]{2,1,0:T(8,128)S(1)}, f32[1,128,512]{2,1,0:T(8,128)S(1)}, u32[]{:S(2)}, u32[]{:S(2)}) collective-permute-start(f32[1,128,512]{2,1,0:T(8,128)S(1)} %bitcast.54), channel_id=1, source_target_pairs={{0,1},{1,0},{2,3},{3,2},{4,5},{5,4},{6,7},{7,6},{8,9},{9,8},{10,11... | collective-permute-start | bytes 786440 | tf_op jit(solution)/shard_map/ppermute | solution.py:16
  23.7 5.7 %collective-permute-start.5 = (f32[64,256]{1,0:T(8,128)S(1)}, f32[64,256]{1,0:T(8,128)S(1)}, u32[]{:S(2)}, u32[]{:S(2)}) collective-permute-start(f32[64,256]{1,0:T(8,128)S(1)} %slice_select_fusion.2), channel_id=1, source_target_pairs={{0,1},{1,0},{2,3},{3,2},{4,5},{5,4},{6,7},{7,6},{8,9},{9,8},{10,11... | collective-permute-start | bytes 196616 | tf_op jit(solution)/shard_map/ppermute | solution.py:16
  26.5 7.1 %collective-permute-start.10 = (f32[2,64,512]{2,1,0:T(8,128)S(1)}, f32[2,64,512]{2,1,0:T(8,128)S(1)}, u32[]{:S(2)}, u32[]{:S(2)}) collective-permute-start(f32[2,64,512]{2,1,0:T(8,128)S(1)} %slice.76), channel_id=1, source_target_pairs={{0,1},{1,0},{2,3},{3,2},{4,5},{5,4},{6,7},{7,6},{8,9},{9,8},{10,11... | collective-permute-start | bytes 786440 | tf_op jit(solution)/shard_map/ppermute | solution.py:16
  26.6 8.8 %collective-permute-start.17 = (f32[2,48,512]{2,1,0:T(8,128)S(1)}, f32[2,48,512]{2,1,0:T(8,128)S(1)}, u32[]{:S(2)}, u32[]{:S(2)}) collective-permute-start(f32[2,48,512]{2,1,0:T(8,128)S(1)} %slice.79), channel_id=1, source_target_pairs={{0,4},{1,5},{2,6},{3,7},{4,0},{5,1},{6,2},{7,3},{8,12},{9,13},{10,... | collective-permute-start | bytes 589832 | tf_op jit(solution)/shard_map/ppermute | solution.py:16
  28.7 5.7 %slice-start.3 = ((s8[5242880]{0:T(1024)(128)(4,1)}), s8[1048576]{0:T(1024)(128)(4,1)S(1)}, s32[]{:S(2)}) async-start(s8[5242880]{0:T(1024)(128)(4,1)} %bitcast.58), calls=%async_computation.3 | async-start | bytes 2097152
  29.1 4.6 %collective-permute-start.4 = (f32[64,256]{1,0:T(8,128)S(1)}, f32[64,256]{1,0:T(8,128)S(1)}, u32[]{:S(2)}, u32[]{:S(2)}) collective-permute-start(f32[64,256]{1,0:T(8,128)S(1)} %fusion.33), channel_id=1, source_target_pairs={{0,1},{1,0},{2,3},{3,2},{4,5},{5,4},{6,7},{7,6},{8,9},{9,8},{10,11... | collective-permute-start | bytes 196616 | tf_op jit(solution)/shard_map/ppermute | solution.py:16
  29.7 5.2 %collective-permute-start.7 = (f32[64,256]{1,0:T(8,128)S(1)}, f32[64,256]{1,0:T(8,128)S(1)}, u32[]{:S(2)}, u32[]{:S(2)}) collective-permute-start(f32[64,256]{1,0:T(8,128)S(1)} %add_subtract_fusion.2), channel_id=1, source_target_pairs={{0,3},{1,2},{2,1},{3,0},{4,7},{5,6},{6,5},{7,4},{8,11},{9,10},{10,... | collective-permute-start | bytes 196616 | tf_op jit(solution)/shard_map/ppermute | solution.py:16
  33.4 9.1 %collective-permute-start.13 = (f32[256,256]{1,0:T(8,128)S(1)}, f32[256,256]{1,0:T(8,128)S(1)}, u32[]{:S(2)}, u32[]{:S(2)}) collective-permute-start(f32[256,256]{1,0:T(8,128)S(1)} %fusion.5), channel_id=1, source_target_pairs={{0,1},{1,0},{2,3},{3,2},{4,5},{5,4},{6,7},{7,6},{8,9},{9,8},{10,11... | collective-permute-start | bytes 786440 | tf_op jit(solution)/shard_map/ppermute | solution.py:16
  34.9 4.0 %collective-permute-start.8 = (f32[64,256]{1,0:T(8,128)S(1)}, f32[64,256]{1,0:T(8,128)S(1)}, u32[]{:S(2)}, u32[]{:S(2)}) collective-permute-start(f32[64,256]{1,0:T(8,128)S(1)} %add.42), channel_id=1, source_target_pairs={{0,5},{1,4},{2,7},{3,6},{4,1},{5,0},{6,3},{7,2},{8,13},{9,12},{10,... | collective-permute-start | bytes 196616 | tf_op jit(solution)/shard_map/ppermute | solution.py:16
  39.2 2.6 %collective-permute-start.11 = (f32[64,256]{1,0:T(8,128)S(1)}, f32[64,256]{1,0:T(8,128)S(1)}, u32[]{:S(2)}, u32[]{:S(2)}) collective-permute-start(f32[64,256]{1,0:T(8,128)S(1)} %fusion.46), channel_id=1, source_target_pairs={{0,1},{1,0},{2,3},{3,2},{4,5},{5,4},{6,7},{7,6},{8,9},{9,8},{10,11... | collective-permute-start | bytes 196616 | tf_op jit(solution)/shard_map/ppermute | solution.py:16
  39.7 2.8 %collective-permute-start.12 = (f32[64,256]{1,0:T(8,128)S(1)}, f32[64,256]{1,0:T(8,128)S(1)}, u32[]{:S(2)}, u32[]{:S(2)}) collective-permute-start(f32[64,256]{1,0:T(8,128)S(1)} %slice_select_fusion.1), channel_id=1, source_target_pairs={{0,1},{1,0},{2,3},{3,2},{4,5},{5,4},{6,7},{7,6},{8,9},{9,8},{10,11... | collective-permute-start | bytes 196616 | tf_op jit(solution)/shard_map/ppermute | solution.py:16
  40.0 11.4 %collective-permute-start.18 = (f32[4,32,512]{2,1,0:T(8,128)S(1)}, f32[4,32,512]{2,1,0:T(8,128)S(1)}, u32[]{:S(2)}, u32[]{:S(2)}) collective-permute-start(f32[4,32,512]{2,1,0:T(8,128)S(1)} %slice.80), channel_id=1, source_target_pairs={{0,1},{1,0},{2,3},{3,2},{4,5},{5,4},{6,7},{7,6},{8,9},{9,8},{10,11... | collective-permute-start | bytes 786440 | tf_op jit(solution)/shard_map/ppermute | solution.py:16
  40.2 16.3 %collective-permute-start.26 = (f32[4,16,512]{2,1,0:T(8,128)S(1)}, f32[4,16,512]{2,1,0:T(8,128)S(1)}, u32[]{:S(2)}, u32[]{:S(2)}) collective-permute-start(f32[4,16,512]{2,1,0:T(8,128)S(1)} %slice.83), channel_id=1, source_target_pairs={{0,8},{1,9},{2,10},{3,11},{4,12},{5,13},{6,14},{7,15},{8,0},{9,1},... | collective-permute-start | bytes 393224 | tf_op jit(solution)/shard_map/ppermute | solution.py:16
  42.8 4.3 %collective-permute-start.14 = (f32[64,256]{1,0:T(8,128)S(1)}, f32[64,256]{1,0:T(8,128)S(1)}, u32[]{:S(2)}, u32[]{:S(2)}) collective-permute-start(f32[64,256]{1,0:T(8,128)S(1)} %add_subtract_fusion.1), channel_id=1, source_target_pairs={{0,3},{1,2},{2,1},{3,0},{4,7},{5,6},{6,5},{7,4},{8,11},{9,10},{10,... | collective-permute-start | bytes 196616 | tf_op jit(solution)/shard_map/ppermute | solution.py:16
  44.0 11.9 %collective-permute-start.21 = (f32[256,256]{1,0:T(8,128)S(1)}, f32[256,256]{1,0:T(8,128)S(1)}, u32[]{:S(2)}, u32[]{:S(2)}) collective-permute-start(f32[256,256]{1,0:T(8,128)S(1)} %fusion), channel_id=1, source_target_pairs={{0,1},{1,0},{2,3},{3,2},{4,5},{5,4},{6,7},{7,6},{8,9},{9,8},{10,11... | collective-permute-start | bytes 786440 | tf_op jit(solution)/shard_map/ppermute | solution.py:16
  47.2 4.2 %collective-permute-start.15 = (f32[64,256]{1,0:T(8,128)S(1)}, f32[64,256]{1,0:T(8,128)S(1)}, u32[]{:S(2)}, u32[]{:S(2)}) collective-permute-start(f32[64,256]{1,0:T(8,128)S(1)} %add.45), channel_id=1, source_target_pairs={{0,5},{1,4},{2,7},{3,6},{4,1},{5,0},{6,3},{7,2},{8,13},{9,12},{10,... | collective-permute-start | bytes 196616 | tf_op jit(solution)/shard_map/ppermute | solution.py:16
  47.5 8.4 %collective-permute-start.20 = (f32[64,256]{1,0:T(8,128)S(1)}, f32[64,256]{1,0:T(8,128)S(1)}, u32[]{:S(2)}, u32[]{:S(2)}) collective-permute-start(f32[64,256]{1,0:T(8,128)S(1)} %slice_select_fusion), channel_id=1, source_target_pairs={{0,1},{1,0},{2,3},{3,2},{4,5},{5,4},{6,7},{7,6},{8,9},{9,8},{10,11... | collective-permute-start | bytes 196616 | tf_op jit(solution)/shard_map/ppermute | solution.py:16
  51.3 4.2 %collective-permute-start.16 = (f32[64,256]{1,0:T(8,128)S(1)}, f32[64,256]{1,0:T(8,128)S(1)}, u32[]{:S(2)}, u32[]{:S(2)}) collective-permute-start(f32[64,256]{1,0:T(8,128)S(1)} %add.46), channel_id=1, source_target_pairs={{0,9},{1,8},{2,11},{3,10},{4,13},{5,12},{6,15},{7,14},{8,1},{9,0},... | collective-permute-start | bytes 196616 | tf_op jit(solution)/shard_map/ppermute | solution.py:16
  56.2 4.2 %collective-permute-start.22 = (f32[64,256]{1,0:T(8,128)S(1)}, f32[64,256]{1,0:T(8,128)S(1)}, u32[]{:S(2)}, u32[]{:S(2)}) collective-permute-start(f32[64,256]{1,0:T(8,128)S(1)} %add_subtract_fusion._), channel_id=1, source_target_pairs={{0,3},{1,2},{2,1},{3,0},{4,7},{5,6},{6,5},{7,4},{8,11},{9,10},{10,... | collective-permute-start | bytes 196616 | tf_op jit(solution)/shard_map/ppermute | solution.py:16
  56.5 8.1 %collective-permute-start.19 = (f32[64,256]{1,0:T(8,128)S(1)}, f32[64,256]{1,0:T(8,128)S(1)}, u32[]{:S(2)}, u32[]{:S(2)}) collective-permute-start(f32[64,256]{1,0:T(8,128)S(1)} %fusion.59), channel_id=1, source_target_pairs={{0,1},{1,0},{2,3},{3,2},{4,5},{5,4},{6,7},{7,6},{8,9},{9,8},{10,11... | collective-permute-start | bytes 196616 | tf_op jit(solution)/shard_map/ppermute | solution.py:16
  60.3 4.1 %collective-permute-start.23 = (f32[64,256]{1,0:T(8,128)S(1)}, f32[64,256]{1,0:T(8,128)S(1)}, u32[]{:S(2)}, u32[]{:S(2)}) collective-permute-start(f32[64,256]{1,0:T(8,128)S(1)} %add.49), channel_id=1, source_target_pairs={{0,5},{1,4},{2,7},{3,6},{4,1},{5,0},{6,3},{7,2},{8,13},{9,12},{10,... | collective-permute-start | bytes 196616 | tf_op jit(solution)/shard_map/ppermute | solution.py:16
  60.7 10.4 %collective-permute-start.27 = (f32[8,16,512]{2,1,0:T(8,128)S(1)}, f32[8,16,512]{2,1,0:T(8,128)S(1)}, u32[]{:S(2)}, u32[]{:S(2)}) collective-permute-start(f32[8,16,512]{2,1,0:T(8,128)S(1)} %maximum_select_fusion.7), channel_id=1, source_target_pairs={{0,1},{1,0},{2,3},{3,2},{4,5},{5,4},{6,7},{7,6},{8,9},{9,8},{10,11... | collective-permute-start | bytes 786440 | tf_op jit(solution)/shard_map/ppermute | solution.py:16
  61.1 2.5 %copy-start = (f32[5,1024,256]{2,1,0:T(8,128)S(1)}, f32[5,1024,256]{2,1,0:T(8,128)}, u32[]{:S(2)}) copy-start(f32[5,1024,256]{2,1,0:T(8,128)} %w_hbm.3) | copy-start | bytes 15728644
  64.5 4.1 %collective-permute-start.24 = (f32[64,256]{1,0:T(8,128)S(1)}, f32[64,256]{1,0:T(8,128)S(1)}, u32[]{:S(2)}, u32[]{:S(2)}) collective-permute-start(f32[64,256]{1,0:T(8,128)S(1)} %add.50), channel_id=1, source_target_pairs={{0,9},{1,8},{2,11},{3,10},{4,13},{5,12},{6,15},{7,14},{8,1},{9,0},... | collective-permute-start | bytes 196616 | tf_op jit(solution)/shard_map/ppermute | solution.py:16
  68.7 6.4 %collective-permute-start.25 = (f32[64,256]{1,0:T(8,128)S(1)}, f32[64,256]{1,0:T(8,128)S(1)}, u32[]{:S(2)}, u32[]{:S(2)}) collective-permute-start(f32[64,256]{1,0:T(8,128)S(1)} %add.51), channel_id=1, source_target_pairs={{0,17},{1,16},{2,19},{3,18},{4,21},{5,20},{6,23},{7,22},{8,25},{9,... | collective-permute-start | bytes 196616 | tf_op jit(solution)/shard_map/ppermute | solution.py:16
  75.4 1.3 %collective-permute-start.28 = (f32[64,256]{1,0:T(8,128)S(1)}, f32[64,256]{1,0:T(8,128)S(1)}, u32[]{:S(2)}, u32[]{:S(2)}) collective-permute-start(f32[64,256]{1,0:T(8,128)S(1)} %fusion.72), channel_id=1, source_target_pairs={{0,1},{1,0},{2,3},{3,2},{4,5},{5,4},{6,7},{7,6},{8,9},{9,8},{10,11... | collective-permute-start | bytes 196616 | tf_op jit(solution)/shard_map/ppermute | solution.py:16

commit v2 on v1

--- a/solution.py
+++ b/solution.py
@@ -56,14 +56,14 @@
 def begin(rhs, proj_bases, corr_bases, cores, first, leaf_core, groups):
     rows, width = rhs.shape
     rank = proj_bases.shape[2]
-    shapes = [(width, rank), (width, rows)] + [(rows, rank)] * 4
+    shapes = [(width, rank), (width, rows)] + [(rows, rank)] * 2
     shapes += [(rank, 2 * rank)] if leaf_core else []
     shapes += [(sum(n for _, n in group), 2 * rank) for group in groups]
 
     def body(x_hbm, p_hbm, w_hbm, c_hbm, *refs):
         outs, (x_ref, p_ref, sems) = list(refs[: len(shapes)]), refs[len(shapes) :]
-        q_out, state_out, w_out, p_out, w_next, p_next = outs[:6]
-        rest = outs[6:]
+        q_out, state_out, w_out, p_out = outs[:4]
+        rest = outs[4:]
         moves = [(x_hbm, x_ref), (p_hbm.at[first], p_ref)]
         if leaf_core:
             moves.append((c_hbm.at[first], rest.pop(0)))
@@ -73,7 +73,6 @@
             for level, n in group:
                 moves.append((c_hbm.at[level, 0:n], out.at[start : start + n]))
                 start += n
-        moves += [(w_hbm.at[first - 1], w_next), (p_hbm.at[first - 2], p_next)]
         copies = [pltpu.make_async_copy(a, b, sems.at[at]) for at, (a, b) in enumerate(moves)]
         for copy in copies:
             copy.start()
@@ -85,7 +84,7 @@
         for copy in copies[2:]:
             copy.wait()
 
-    count = 6 + (1 if leaf_core else 0) + sum(len(group) for group in groups)
+    count = 4 + (1 if leaf_core else 0) + sum(len(group) for group in groups)
     return pl.pallas_call(
         body,
         in_specs=[IN_HBM] * 4,
@@ -104,31 +103,6 @@
     )(rhs, proj_bases, corr_bases, cores)
 
 
-def fetch(corr_bases, after):
-    rows, rank = corr_bases.shape[1:]
-
-    def body(w_hbm, _, one, zero, sems):
-        copies = [
-            pltpu.make_async_copy(w_hbm.at[level], out, sems.at[level])
-            for level, out in enumerate((zero, one))
-        ]
-        for copy in copies:
-            copy.start()
-        for copy in copies:
-            copy.wait()
-
-    return pl.pallas_call(
-        body,
-        in_specs=[IN_HBM, pl.BlockSpec(memory_space=pl.ANY)],
-        out_specs=[IN_VMEM] * 2,
-        out_shape=[pltpu.VMEM((rows, rank), jnp.float32)] * 2,
-        scratch_shapes=[pltpu.SemaphoreType.DMA((2,))],
-        compiler_params=pltpu.CompilerParams(vmem_limit_bytes=32 * 2**20),
-        cost_estimate=pl.CostEstimate(flops=0, bytes_accessed=2**22, transcendentals=0),
-        name="fetch",
-    )(corr_bases, after)
-
-
 def finish(state, corr, held):
     width, rows = state.shape
 
@@ -140,7 +114,7 @@
         in_specs=[IN_VMEM] * 3,
         out_specs=IN_VMEM,
         out_shape=jax.ShapeDtypeStruct((rows, width), jnp.float32),
-        compiler_params=pltpu.CompilerParams(vmem_limit_bytes=24 * 2**20),
+        compiler_params=pltpu.CompilerParams(vmem_limit_bytes=16 * 2**20),
         cost_estimate=pl.CostEstimate(
             flops=6 * rows * width * corr.shape[1], bytes_accessed=2**21, transcendentals=0
         ),
@@ -181,7 +155,7 @@
     tails = [(level, rank >> bits[level]) for level in chain if bits[level] > 1]
     groups = [group for group in (heads, tails) if group]
     leaf_core = bits[first] == 0
-    value, state, top_corr, next_proj, next_corr, after_proj, *fetched = begin(
+    value, state, top_corr, next_proj, *fetched = begin(
         rhs, proj_bases, corr_bases, cores, first, leaf_core, groups
     )
 
@@ -255,11 +229,8 @@
     for level in reversed(range(1, first)):
         start = value
         held = solve(level, value, {})
-        if level == first - 1:
-            proj, corr = tie(after_proj, start), tie(next_corr, start)
-        else:
-            projs, corrs = lax.optimization_barrier((proj_bases, corr_bases, start))[:2]
-            proj, corr = projs[level - 1], corrs[level]
+        projs, corrs = lax.optimization_barrier((proj_bases, corr_bases, start))[:2]
+        proj, corr = projs[level - 1], corrs[level]
         ahead = chip_sum(project(proj, state))
         own = jnp.einsum("na,nb->ab", proj, corr, precision=HIGH)
         if heads and level == first - 1:
@@ -267,10 +238,11 @@
         value = ahead - times_transposed(held, own + exchange(own, 1))
         if level > 1:
             state = update(corr, state, chip_gather(held))
-    one_corr, zero_corr = fetch(corr_bases, value)
+    last_corrs = tie(corr_bases, value)
+    one_corr, zero_corr = last_corrs[1], last_corrs[0]
     state = update(one_corr, state, chip_gather(held))
     ahead_of = {
-        bits[0] - 1: lambda v: lax.optimization_barrier((v, one_corr, zero_corr))[0],
+        bits[0] - 1: lambda v: tie(v, zero_corr),
         bits[0]: lambda v: tie(v, state),
     }
     held = solve(0, value, ahead_of)

time: 78.5 us -> 72.6 us (0.925)
  local copies, waits for them, and re-layouts: 7.59 us -> 1.31 us
  matrix products: 16.2 us -> 20.5 us
  other arithmetic: 3.14 us -> 0.38 us
  Pallas kernels: 4.57 us -> 3.68 us
    unnamed x26 -> x12, local copies, waits for them, and re-layouts: 7.41 us -> 1.07 us
    dot_general x3, matrix products: 4.21 us -> 7.34 us  [on_device(): own = jnp.einsum('na,nb->ab', proj, corr, precision=HIGH)]
    dot_general x4, matrix products: 4.04 us -> 5.46 us  [project(): return jnp.einsum('kn,nr->kr', state, basis, precision=HIGH)]
    select_n x4, other arithmetic: 1.4 us -> 0.09 us  [pair_up(): jnp.where(low, jnp.concatenate([mine, other], axis), jnp.concatenate([oth...]
    add x1, other arithmetic: 0.85 us -> 0.01 us  [chip_sum(): return keep + exchange(send, 1)]
  transfers between devices with their start and end apart: 29 -> 29, of which waited for: 11 -> 11; matrix products, arithmetic and copies ran while one was open for 17% -> 25% of each run, Pallas kernels for 0% -> 0%
where the time goes in v2:
time: 72.6 us; the launch traced here: 72.2 us
  waiting for transfers between devices  27.4 us (38%)
  matrix products  20.5 us (28%)
  starting transfers between devices  18.5 us (25%)
  Pallas kernels  3.68 us (5%)
  local copies, waits for them, and re-layouts  1.31 us (2%)
    ppermute x29, waiting for transfers between devices, exchange(): return lax.ppermute(value, 'leaf', pairs)  27.4 us
    ppermute x29, starting transfers between devices, exchange(): return lax.ppermute(value, 'leaf', pairs)  18.5 us
    dot_general x3, matrix products, on_device(): own = jnp.einsum('na,nb->ab', proj, corr, precision=HIGH)  7.34 us
    dot_general x4, matrix products, project(): return jnp.einsum('kn,nr->kr', state, basis, precision=HIGH)  5.46 us
    dot_general x4, matrix products, update(): return state - jnp.einsum('ka,na->kn', held, corr, precision=HIGH)  3.93 us
    dot_general x8, matrix products, times_transposed(): return jnp.einsum('kb,ab->ka', left, right, precision=HIGH)  3.72 us
    pallas_call x1, Pallas kernels, begin(): pl.pallas_call(body, in_specs=[IN_HBM] * 4, out_specs=[IN_VMEM] * len(sha...  2.33 us
  transfers between devices with their start and end apart: 29, of which 11 were waited for; matrix products, arithmetic and copies ran while one was open for 25% of the time, Pallas kernels for 0%

profile of v2, /device:TPU:0, one launch (start us, length us, event | category | flops | bytes accessed | tf_op | source)
XLA Modules:
  0.0 72.2 jit_solution(44176564899487027)
XLA Ops:
  0.0 2.3 %begin.1 = (f32[128,256]{1,0:T(8,128)S(1)}, f32[128,1024]{1,0:T(8,128)S(1)}, f32[1024,256]{1,0:T(8,128)S(1)}, f32[1024,256]{1,0:T(8,128)S(1)}, f32[256,512]{1,0:...) custom-call(f32[1024,128]{1,0:T(8,128)} %x_hbm.1, f32[5,1024,256]{2,1,0:T(8,128)} %p_hbm.1, ...), custom_call_target="tpu_custom_call" | custom-call | flops 201326592 | bytes 4194304 | tf_op jit(solution)/shard_map/begin/pallas_call | solution.py:88
  2.3 0.7 copy-done
  3.0 0.5 collective-permute-start
  3.5 1.1 %collective-permute-done = f32[128,256]{1,0:T(8,128)} collective-permute-done((f32[128,256]{1,0:T(8,128)S(1)}, f32[128,256]{1,0:T(8,128)}, u32[]{:S(2)}, u32[]{:S(2)}) %collective-permute-start) | collective-permute-done | bytes 131104 | tf_op jit(solution)/shard_map/ppermute | solution.py:16
  4.6 1.4 %fusion.31 = f32[128,256]{1,0:T(8,128)S(1)} fusion(f32[256,512]{1,0:T(8,128)S(1)} %get-tuple-element.32, f32[128,256]{1,0:T(8,128)} %collective-permute-done, f32[128,256]{1,0:T(8,128)S(1)} %get-tuple-element.31, pred[]{:T(512)S(6)} %eq.12), kind=kOutput, calls=%fused_computation.43 | convolution fusion | flops 100925440 | bytes 917505 | tf_op jit(solution)/shard_map/kb,ab->ka/dot_general | solution.py:36
  6.0 0.7 convolution_subtract_fusion.3
  6.7 0.4 fusion.117
  7.1 0.4 copy-done.2
  7.5 0.4 collective-permute-start.1
  7.9 2.6 %collective-permute-start.9 = (f32[1,112,512]{2,1,0:T(8,128)}, f32[1,112,512]{2,1,0:T(8,128)S(1)}, u32[]{:S(2)}, u32[]{:S(2)}) collective-permute-start(f32[1,112,512]{2,1,0:T(8,128)} %bitcast.64), channel_id=1, source_target_pairs={{0,2},{1,3},{2,0},{3,1},{4,6},{5,7},{6,4},{7,5},{8,10},{9,11},{10,... | collective-permute-start | bytes 688136 | tf_op jit(solution)/shard_map/ppermute | solution.py:16
  10.5 0.9 %collective-permute-start.2 = (f32[64,256]{1,0:T(8,128)S(1)}, f32[64,256]{1,0:T(8,128)S(1)}, u32[]{:S(2)}, u32[]{:S(2)}) collective-permute-start(f32[64,256]{1,0:T(8,128)S(1)} %select_add_fusion), channel_id=1, source_target_pairs={{0,3},{1,2},{2,1},{3,0},{4,7},{5,6},{6,5},{7,4},{8,11},{9,10},{10,... | collective-permute-start | bytes 196616 | tf_op jit(solution)/shard_map/ppermute | solution.py:16
  11.5 1.8 %fusion.14 = f32[128,256]{1,0:T(8,128)S(1)} fusion(f32[128,1024]{1,0:T(8,128)} %copy-done.2, f32[5,1024,256]{2,1,0:T(8,128)} %p_hbm.1), kind=kOutput, calls=%fused_computation.18 | convolution fusion | flops 201326592 | bytes 1703936 | tf_op jit(solution)/shard_map/kn,nr->kr/dot_general | solution.py:32
  13.3 2.6 %fusion.12 = f32[256,256]{1,0:T(8,128)S(1)} fusion(f32[5,1024,256]{2,1,0:T(8,128)} %p_hbm.1, f32[5,1024,256]{2,1,0:T(8,128)} %w_hbm.1), kind=kOutput, calls=%fused_computation.16 | convolution fusion | flops 402653184 | bytes 2359296 | tf_op jit(solution)/shard_map/na,nb->ab/dot_general | solution.py:235
  15.9 0.4 collective-permute-start.6
  16.3 0.2 collective-permute-start.3
  16.5 0.4 collective-permute-start.5
  16.9 0.3 collective-permute-done.9
  17.3 0.1 collective-permute-start.10
  17.3 0.5 collective-permute-done.3
  17.9 1.6 %collective-permute-start.17 = (f32[2,48,512]{2,1,0:T(8,128)S(1)}, f32[2,48,512]{2,1,0:T(8,128)S(1)}, u32[]{:S(2)}, u32[]{:S(2)}) collective-permute-start(f32[2,48,512]{2,1,0:T(8,128)S(1)} %slice.95), channel_id=1, source_target_pairs={{0,4},{1,5},{2,6},{3,7},{4,0},{5,1},{6,2},{7,3},{8,12},{9,13},{10,... | collective-permute-start | bytes 589832 | tf_op jit(solution)/shard_map/ppermute | solution.py:16
  19.5 0.4 fusion.45
  19.9 0.2 collective-permute-start.4
  20.1 0.3 add_subtract_fusion.2
  20.4 1.5 %collective-permute-start.7 = (f32[64,256]{1,0:T(8,128)S(1)}, f32[64,256]{1,0:T(8,128)S(1)}, u32[]{:S(2)}, u32[]{:S(2)}) collective-permute-start(f32[64,256]{1,0:T(8,128)S(1)} %add_subtract_fusion.2), channel_id=1, source_target_pairs={{0,3},{1,2},{2,1},{3,0},{4,7},{5,6},{6,5},{7,4},{8,11},{9,10},{10,... | collective-permute-start | bytes 196616 | tf_op jit(solution)/shard_map/ppermute | solution.py:16
  21.9 2.5 %fusion.6 = f32[256,256]{1,0:T(8,128)S(1)} fusion(f32[5,1024,256]{2,1,0:T(8,128)} %p_hbm.1, f32[5,1024,256]{2,1,0:T(8,128)} %w_hbm.1), kind=kOutput, calls=%fused_computation.10 | convolution fusion | flops 402653184 | bytes 2359296 | tf_op jit(solution)/shard_map/na,nb->ab/dot_general | solution.py:235
  24.4 0.2 collective-permute-start.13
  24.8 2.0 %convolution_subtract_fusion.2 = f32[128,1024]{1,0:T(8,128)S(1)} fusion(f32[128,1024]{1,0:T(8,128)S(1)} %copy-done.3, f32[5,1024,256]{2,1,0:T(8,128)} %w_hbm.1, f32[64,256]{1,0:T(8,128)S(1)} %collective-permute-done.4, f32[64,256]{1,0:T(8,128)S(1)} %fusion.45, pred[]{:T(512)S(6)} %eq.26), kind=kOutput, calls=%fused_computation.2 | convolution fusion | flops 201555968 | bytes 2228225 | tf_op jit(solution)/shard_map/ka,na->kn/dot_general | solution.py:216
  26.8 1.6 %fusion.8 = f32[128,256]{1,0:T(8,128)S(1)} fusion(f32[128,1024]{1,0:T(8,128)S(1)} %convolution_subtract_fusion.2, f32[5,1024,256]{2,1,0:T(8,128)} %p_hbm.1), kind=kOutput, calls=%fused_computation.12 | convolution fusion | flops 201326592 | bytes 1703936 | tf_op jit(solution)/shard_map/kn,nr->kr/dot_general | solution.py:32
  28.4 0.5 collective-permute-start.8
  29.0 3.4 %collective-permute-done.8 = f32[64,256]{1,0:T(8,128)S(1)} collective-permute-done((f32[64,256]{1,0:T(8,128)S(1)}, f32[64,256]{1,0:T(8,128)S(1)}, u32[]{:S(2)}, u32[]{:S(2)}) %collective-permute-start.8) | collective-permute-done | bytes 65568 | tf_op jit(solution)/shard_map/ppermute | solution.py:16
  32.4 0.4 fusion.58
  32.8 0.4 collective-permute-start.11
  33.2 0.3 collective-permute-start.12
  33.5 0.3 collective-permute-start.18
  33.8 1.6 %collective-permute-start.26 = (f32[4,16,512]{2,1,0:T(8,128)S(1)}, f32[4,16,512]{2,1,0:T(8,128)S(1)}, u32[]{:S(2)}, u32[]{:S(2)}) collective-permute-start(f32[4,16,512]{2,1,0:T(8,128)S(1)} %slice.99), channel_id=1, source_target_pairs={{0,8},{1,9},{2,10},{3,11},{4,12},{5,13},{6,14},{7,15},{8,0},{9,1},... | collective-permute-start | bytes 393224 | tf_op jit(solution)/shard_map/ppermute | solution.py:16
  35.4 0.7 convolution_subtract_fusion.1
  36.1 0.3 add_subtract_fusion.1
  36.4 0.1 collective-permute-start.14
  36.5 2.2 %fusion.1 = f32[256,256]{1,0:T(8,128)S(1)} fusion(f32[5,1024,256]{2,1,0:T(8,128)S(1)} %bitcast.67, f32[5,1024,256]{2,1,0:T(8,128)} %p_hbm.1), kind=kOutput, calls=%fused_computation.5 | convolution fusion | flops 402653184 | bytes 2359296 | tf_op jit(solution)/shard_map/na,nb->ab/dot_general | solution.py:235
  38.8 0.6 collective-permute-start.21
  39.4 1.6 %fusion.4 = f32[128,256]{1,0:T(8,128)S(1)} fusion(f32[128,1024]{1,0:T(8,128)S(1)} %convolution_subtract_fusion.1, f32[5,1024,256]{2,1,0:T(8,128)} %p_hbm.1), kind=kOutput, calls=%fused_computation.8 | convolution fusion | flops 201326592 | bytes 1703936 | tf_op jit(solution)/shard_map/kn,nr->kr/dot_general | solution.py:32
  41.1 0.2 collective-permute-start.15
  41.3 0.6 collective-permute-start.20
  41.8 3.5 %collective-permute-done.15 = f32[64,256]{1,0:T(8,128)S(1)} collective-permute-done((f32[64,256]{1,0:T(8,128)S(1)}, f32[64,256]{1,0:T(8,128)S(1)}, u32[]{:S(2)}, u32[]{:S(2)}) %collective-permute-start.15) | collective-permute-done | bytes 65568 | tf_op jit(solution)/shard_map/ppermute | solution.py:16
  45.3 0.1 collective-permute-start.16
  45.6 3.9 %collective-permute-done.16 = f32[64,256]{1,0:T(8,128)S(1)} collective-permute-done((f32[64,256]{1,0:T(8,128)S(1)}, f32[64,256]{1,0:T(8,128)S(1)}, u32[]{:S(2)}, u32[]{:S(2)}) %collective-permute-start.16) | collective-permute-done | bytes 65568 | tf_op jit(solution)/shard_map/ppermute | solution.py:16
  49.5 0.4 fusion.71
  49.9 0.3 add_subtract_fusion
  50.2 1.3 %collective-permute-start.22 = (f32[64,256]{1,0:T(8,128)S(1)}, f32[64,256]{1,0:T(8,128)S(1)}, u32[]{:S(2)}, u32[]{:S(2)}) collective-permute-start(f32[64,256]{1,0:T(8,128)S(1)} %add_subtract_fusion), channel_id=1, source_target_pairs={{0,3},{1,2},{2,1},{3,0},{4,7},{5,6},{6,5},{7,4},{8,11},{9,10},{10,... | collective-permute-start | bytes 196616 | tf_op jit(solution)/shard_map/ppermute | solution.py:16
  51.5 0.5 collective-permute-start.27
  51.9 0.1 collective-permute-start.19
  52.1 2.3 %collective-permute-done.22 = f32[64,256]{1,0:T(8,128)S(1)} collective-permute-done((f32[64,256]{1,0:T(8,128)S(1)}, f32[64,256]{1,0:T(8,128)S(1)}, u32[]{:S(2)}, u32[]{:S(2)}) %collective-permute-start.22) | collective-permute-done | bytes 65568 | tf_op jit(solution)/shard_map/ppermute | solution.py:16
  54.4 0.3 collective-permute-start.23
  54.7 0.1 slice_bitcast_fusion.w_ref
  54.7 3.8 %collective-permute-done.23 = f32[64,256]{1,0:T(8,128)S(1)} collective-permute-done((f32[64,256]{1,0:T(8,128)S(1)}, f32[64,256]{1,0:T(8,128)S(1)}, u32[]{:S(2)}, u32[]{:S(2)}) %collective-permute-start.23) | collective-permute-done | bytes 65568 | tf_op jit(solution)/shard_map/ppermute | solution.py:16
  58.5 0.1 collective-permute-start.24
  58.6 0.7 convolution_subtract_fusion.x_ref
  59.3 3.4 %collective-permute-done.24 = f32[64,256]{1,0:T(8,128)S(1)} collective-permute-done((f32[64,256]{1,0:T(8,128)S(1)}, f32[64,256]{1,0:T(8,128)S(1)}, u32[]{:S(2)}, u32[]{:S(2)}) %collective-permute-start.24) | collective-permute-done | bytes 65568 | tf_op jit(solution)/shard_map/ppermute | solution.py:16
  62.7 2.4 %collective-permute-start.25 = (f32[64,256]{1,0:T(8,128)S(1)}, f32[64,256]{1,0:T(8,128)S(1)}, u32[]{:S(2)}, u32[]{:S(2)}) collective-permute-start(f32[64,256]{1,0:T(8,128)S(1)} %add.51), channel_id=1, source_target_pairs={{0,17},{1,16},{2,19},{3,18},{4,21},{5,20},{6,23},{7,22},{8,25},{9,... | collective-permute-start | bytes 196616 | tf_op jit(solution)/shard_map/ppermute | solution.py:16
  65.2 4.0 %collective-permute-done.25 = f32[64,256]{1,0:T(8,128)S(1)} collective-permute-done((f32[64,256]{1,0:T(8,128)S(1)}, f32[64,256]{1,0:T(8,128)S(1)}, u32[]{:S(2)}, u32[]{:S(2)}) %collective-permute-start.25) | collective-permute-done | bytes 65568 | tf_op jit(solution)/shard_map/ppermute | solution.py:16
  69.2 0.4 fusion.84
  69.5 0.2 collective-permute-start.28
  69.7 1.1 %collective-permute-done.28 = f32[64,256]{1,0:T(8,128)S(1)} collective-permute-done((f32[64,256]{1,0:T(8,128)S(1)}, f32[64,256]{1,0:T(8,128)S(1)}, u32[]{:S(2)}, u32[]{:S(2)}) %collective-permute-start.28) | collective-permute-done | bytes 65568 | tf_op jit(solution)/shard_map/ppermute | solution.py:16
  70.9 1.4 %finish.1 = f32[1024,128]{1,0:T(8,128)} custom-call(f32[128,1024]{1,0:T(8,128)S(1)} %convolution_subtract_fusion.x_ref, f32[1024,256]{1,0:T(8,128)S(1)} %slice_bitcast_fusion.w_ref, f32[128,256]{1,0:T(8,128)S(1)} %maximum_select_fusion.18.t_ref), custom_call_target="tpu_custom_call" | custom-call | flops 201326592 | bytes 2097152 | tf_op jit(solution)/shard_map/finish/pallas_call | solution.py:112
  (55 shorter events, 0.6 us)
Async XLA Ops:
  2.3 0.7 copy-start
  3.0 1.6 %collective-permute-start = (f32[128,256]{1,0:T(8,128)S(1)}, f32[128,256]{1,0:T(8,128)}, u32[]{:S(2)}, u32[]{:S(2)}) collective-permute-start(f32[128,256]{1,0:T(8,128)S(1)} %get-tuple-element.31), channel_id=1, source_target_pairs={{0,1},{1,0},{2,3},{3,2},{4,5},{5,4},{6,7},{7,6},{8,9},{9,8},{10,11... | collective-permute-start | bytes 393224 | tf_op jit(solution)/shard_map/ppermute | solution.py:16
  6.0 11.2 %copy-start.1 = (f32[112,512]{1,0:T(8,128)S(1)}, f32[112,512]{1,0:T(8,128)}, u32[]{:S(2)}) copy-start(f32[112,512]{1,0:T(8,128)} %copy-done) | copy-start | bytes 688132
  6.6 0.8 %copy-start.2 = (f32[128,1024]{1,0:T(8,128)}, f32[128,1024]{1,0:T(8,128)S(1)}, u32[]{:S(2)}) copy-start(f32[128,1024]{1,0:T(8,128)S(1)} %convolution_subtract_fusion.3) | copy-start | bytes 1572868
  7.5 3.1 %collective-permute-start.1 = (f32[64,256]{1,0:T(8,128)S(1)}, f32[64,256]{1,0:T(8,128)S(1)}, u32[]{:S(2)}, u32[]{:S(2)}) collective-permute-start(f32[64,256]{1,0:T(8,128)S(1)} %slice_select_fusion.3), channel_id=1, source_target_pairs={{0,1},{1,0},{2,3},{3,2},{4,5},{5,4},{6,7},{7,6},{8,9},{9,8},{10,11... | collective-permute-start | bytes 196616 | tf_op jit(solution)/shard_map/ppermute | solution.py:16
  7.9 9.3 %collective-permute-start.9 = (f32[1,112,512]{2,1,0:T(8,128)}, f32[1,112,512]{2,1,0:T(8,128)S(1)}, u32[]{:S(2)}, u32[]{:S(2)}) collective-permute-start(f32[1,112,512]{2,1,0:T(8,128)} %bitcast.64), channel_id=1, source_target_pairs={{0,2},{1,3},{2,0},{3,1},{4,6},{5,7},{6,4},{7,5},{8,10},{9,11},{10,... | collective-permute-start | bytes 688136 | tf_op jit(solution)/shard_map/ppermute | solution.py:16
  10.5 8.9 %collective-permute-start.2 = (f32[64,256]{1,0:T(8,128)S(1)}, f32[64,256]{1,0:T(8,128)S(1)}, u32[]{:S(2)}, u32[]{:S(2)}) collective-permute-start(f32[64,256]{1,0:T(8,128)S(1)} %select_add_fusion), channel_id=1, source_target_pairs={{0,3},{1,2},{2,1},{3,0},{4,7},{5,6},{6,5},{7,4},{8,11},{9,10},{10,... | collective-permute-start | bytes 196616 | tf_op jit(solution)/shard_map/ppermute | solution.py:16
  13.3 11.5 %copy-start.3 = (f32[128,1024]{1,0:T(8,128)S(1)}, f32[128,1024]{1,0:T(8,128)}, u32[]{:S(2)}) copy-start(f32[128,1024]{1,0:T(8,128)} %copy-done.2) | copy-start | bytes 1572868
  15.9 4.2 %collective-permute-start.6 = (f32[256,256]{1,0:T(8,128)S(1)}, f32[256,256]{1,0:T(8,128)S(1)}, u32[]{:S(2)}, u32[]{:S(2)}) collective-permute-start(f32[256,256]{1,0:T(8,128)S(1)} %fusion.12), channel_id=1, source_target_pairs={{0,1},{1,0},{2,3},{3,2},{4,5},{5,4},{6,7},{7,6},{8,9},{9,8},{10,11... | collective-permute-start | bytes 786440 | tf_op jit(solution)/shard_map/ppermute | solution.py:16
  16.3 1.6 %collective-permute-start.3 = (f32[1,128,512]{2,1,0:T(8,128)S(1)}, f32[1,128,512]{2,1,0:T(8,128)S(1)}, u32[]{:S(2)}, u32[]{:S(2)}) collective-permute-start(f32[1,128,512]{2,1,0:T(8,128)S(1)} %bitcast.62), channel_id=1, source_target_pairs={{0,1},{1,0},{2,3},{3,2},{4,5},{5,4},{6,7},{7,6},{8,9},{9,8},{10,11... | collective-permute-start | bytes 786440 | tf_op jit(solution)/shard_map/ppermute | solution.py:16
  16.5 3.6 %collective-permute-start.5 = (f32[64,256]{1,0:T(8,128)S(1)}, f32[64,256]{1,0:T(8,128)S(1)}, u32[]{:S(2)}, u32[]{:S(2)}) collective-permute-start(f32[64,256]{1,0:T(8,128)S(1)} %slice_select_fusion.2), channel_id=1, source_target_pairs={{0,1},{1,0},{2,3},{3,2},{4,5},{5,4},{6,7},{7,6},{8,9},{9,8},{10,11... | collective-permute-start | bytes 196616 | tf_op jit(solution)/shard_map/ppermute | solution.py:16
  17.3 7.4 %collective-permute-start.10 = (f32[2,64,512]{2,1,0:T(8,128)S(1)}, f32[2,64,512]{2,1,0:T(8,128)S(1)}, u32[]{:S(2)}, u32[]{:S(2)}) collective-permute-start(f32[2,64,512]{2,1,0:T(8,128)S(1)} %slice.92), channel_id=1, source_target_pairs={{0,1},{1,0},{2,3},{3,2},{4,5},{5,4},{6,7},{7,6},{8,9},{9,8},{10,11... | collective-permute-start | bytes 786440 | tf_op jit(solution)/shard_map/ppermute | solution.py:16
  17.9 11.1 %collective-permute-start.17 = (f32[2,48,512]{2,1,0:T(8,128)S(1)}, f32[2,48,512]{2,1,0:T(8,128)S(1)}, u32[]{:S(2)}, u32[]{:S(2)}) collective-permute-start(f32[2,48,512]{2,1,0:T(8,128)S(1)} %slice.95), channel_id=1, source_target_pairs={{0,4},{1,5},{2,6},{3,7},{4,0},{5,1},{6,2},{7,3},{8,12},{9,13},{10,... | collective-permute-start | bytes 589832 | tf_op jit(solution)/shard_map/ppermute | solution.py:16
  19.4 16.0 %slice-start = ((s8[5242880]{0:T(1024)(128)(4,1)}), s8[4194304]{0:T(1024)(128)(4,1)S(1)}, s32[]{:S(2)}) async-start(s8[5242880]{0:T(1024)(128)(4,1)} %bitcast.66), calls=%async_computation | async-start | bytes 8388608
  19.9 4.9 %collective-permute-start.4 = (f32[64,256]{1,0:T(8,128)S(1)}, f32[64,256]{1,0:T(8,128)S(1)}, u32[]{:S(2)}, u32[]{:S(2)}) collective-permute-start(f32[64,256]{1,0:T(8,128)S(1)} %fusion.45), channel_id=1, source_target_pairs={{0,1},{1,0},{2,3},{3,2},{4,5},{5,4},{6,7},{7,6},{8,9},{9,8},{10,11... | collective-permute-start | bytes 196616 | tf_op jit(solution)/shard_map/ppermute | solution.py:16
  20.4 8.0 %collective-permute-start.7 = (f32[64,256]{1,0:T(8,128)S(1)}, f32[64,256]{1,0:T(8,128)S(1)}, u32[]{:S(2)}, u32[]{:S(2)}) collective-permute-start(f32[64,256]{1,0:T(8,128)S(1)} %add_subtract_fusion.2), channel_id=1, source_target_pairs={{0,3},{1,2},{2,1},{3,0},{4,7},{5,6},{6,5},{7,4},{8,11},{9,10},{10,... | collective-permute-start | bytes 196616 | tf_op jit(solution)/shard_map/ppermute | solution.py:16
  24.4 11.6 %collective-permute-start.13 = (f32[256,256]{1,0:T(8,128)S(1)}, f32[256,256]{1,0:T(8,128)S(1)}, u32[]{:S(2)}, u32[]{:S(2)}) collective-permute-start(f32[256,256]{1,0:T(8,128)S(1)} %fusion.6), channel_id=1, source_target_pairs={{0,1},{1,0},{2,3},{3,2},{4,5},{5,4},{6,7},{7,6},{8,9},{9,8},{10,11... | collective-permute-start | bytes 786440 | tf_op jit(solution)/shard_map/ppermute | solution.py:16
  24.7 10.7 %slice-start.1 = ((s8[5242880]{0:T(1024)(128)(4,1)}), s8[1048576]{0:T(1024)(128)(4,1)S(1)}, s32[]{:S(2)}) async-start(s8[5242880]{0:T(1024)(128)(4,1)} %bitcast.66), calls=%async_computation.1 | async-start | bytes 2097152
  28.4 4.0 %collective-permute-start.8 = (f32[64,256]{1,0:T(8,128)S(1)}, f32[64,256]{1,0:T(8,128)S(1)}, u32[]{:S(2)}, u32[]{:S(2)}) collective-permute-start(f32[64,256]{1,0:T(8,128)S(1)} %add.42), channel_id=1, source_target_pairs={{0,5},{1,4},{2,7},{3,6},{4,1},{5,0},{6,3},{7,2},{8,13},{9,12},{10,... | collective-permute-start | bytes 196616 | tf_op jit(solution)/shard_map/ppermute | solution.py:16
  32.8 2.6 %collective-permute-start.11 = (f32[64,256]{1,0:T(8,128)S(1)}, f32[64,256]{1,0:T(8,128)S(1)}, u32[]{:S(2)}, u32[]{:S(2)}) collective-permute-start(f32[64,256]{1,0:T(8,128)S(1)} %fusion.58), channel_id=1, source_target_pairs={{0,1},{1,0},{2,3},{3,2},{4,5},{5,4},{6,7},{7,6},{8,9},{9,8},{10,11... | collective-permute-start | bytes 196616 | tf_op jit(solution)/shard_map/ppermute | solution.py:16
  33.2 2.8 %collective-permute-start.12 = (f32[64,256]{1,0:T(8,128)S(1)}, f32[64,256]{1,0:T(8,128)S(1)}, u32[]{:S(2)}, u32[]{:S(2)}) collective-permute-start(f32[64,256]{1,0:T(8,128)S(1)} %slice_select_fusion.1), channel_id=1, source_target_pairs={{0,1},{1,0},{2,3},{3,2},{4,5},{5,4},{6,7},{7,6},{8,9},{9,8},{10,11... | collective-permute-start | bytes 196616 | tf_op jit(solution)/shard_map/ppermute | solution.py:16
  33.5 12.0 %collective-permute-start.18 = (f32[4,32,512]{2,1,0:T(8,128)S(1)}, f32[4,32,512]{2,1,0:T(8,128)S(1)}, u32[]{:S(2)}, u32[]{:S(2)}) collective-permute-start(f32[4,32,512]{2,1,0:T(8,128)S(1)} %slice.96), channel_id=1, source_target_pairs={{0,1},{1,0},{2,3},{3,2},{4,5},{5,4},{6,7},{7,6},{8,9},{9,8},{10,11... | collective-permute-start | bytes 786440 | tf_op jit(solution)/shard_map/ppermute | solution.py:16
  33.8 11.8 %collective-permute-start.26 = (f32[4,16,512]{2,1,0:T(8,128)S(1)}, f32[4,16,512]{2,1,0:T(8,128)S(1)}, u32[]{:S(2)}, u32[]{:S(2)}) collective-permute-start(f32[4,16,512]{2,1,0:T(8,128)S(1)} %slice.99), channel_id=1, source_target_pairs={{0,8},{1,9},{2,10},{3,11},{4,12},{5,13},{6,14},{7,15},{8,0},{9,1},... | collective-permute-start | bytes 393224 | tf_op jit(solution)/shard_map/ppermute | solution.py:16
  36.4 4.6 %collective-permute-start.14 = (f32[64,256]{1,0:T(8,128)S(1)}, f32[64,256]{1,0:T(8,128)S(1)}, u32[]{:S(2)}, u32[]{:S(2)}) collective-permute-start(f32[64,256]{1,0:T(8,128)S(1)} %add_subtract_fusion.1), channel_id=1, source_target_pairs={{0,3},{1,2},{2,1},{3,0},{4,7},{5,6},{6,5},{7,4},{8,11},{9,10},{10,... | collective-permute-start | bytes 196616 | tf_op jit(solution)/shard_map/ppermute | solution.py:16
  38.8 11.1 %collective-permute-start.21 = (f32[256,256]{1,0:T(8,128)S(1)}, f32[256,256]{1,0:T(8,128)S(1)}, u32[]{:S(2)}, u32[]{:S(2)}) collective-permute-start(f32[256,256]{1,0:T(8,128)S(1)} %fusion.1), channel_id=1, source_target_pairs={{0,1},{1,0},{2,3},{3,2},{4,5},{5,4},{6,7},{7,6},{8,9},{9,8},{10,11... | collective-permute-start | bytes 786440 | tf_op jit(solution)/shard_map/ppermute | solution.py:16
  41.1 4.3 %collective-permute-start.15 = (f32[64,256]{1,0:T(8,128)S(1)}, f32[64,256]{1,0:T(8,128)S(1)}, u32[]{:S(2)}, u32[]{:S(2)}) collective-permute-start(f32[64,256]{1,0:T(8,128)S(1)} %add.45), channel_id=1, source_target_pairs={{0,5},{1,4},{2,7},{3,6},{4,1},{5,0},{6,3},{7,2},{8,13},{9,12},{10,... | collective-permute-start | bytes 196616 | tf_op jit(solution)/shard_map/ppermute | solution.py:16
  41.3 8.6 %collective-permute-start.20 = (f32[64,256]{1,0:T(8,128)S(1)}, f32[64,256]{1,0:T(8,128)S(1)}, u32[]{:S(2)}, u32[]{:S(2)}) collective-permute-start(f32[64,256]{1,0:T(8,128)S(1)} %slice_select_fusion), channel_id=1, source_target_pairs={{0,1},{1,0},{2,3},{3,2},{4,5},{5,4},{6,7},{7,6},{8,9},{9,8},{10,11... | collective-permute-start | bytes 196616 | tf_op jit(solution)/shard_map/ppermute | solution.py:16
  45.3 4.2 %collective-permute-start.16 = (f32[64,256]{1,0:T(8,128)S(1)}, f32[64,256]{1,0:T(8,128)S(1)}, u32[]{:S(2)}, u32[]{:S(2)}) collective-permute-start(f32[64,256]{1,0:T(8,128)S(1)} %add.46), channel_id=1, source_target_pairs={{0,9},{1,8},{2,11},{3,10},{4,13},{5,12},{6,15},{7,14},{8,1},{9,0},... | collective-permute-start | bytes 196616 | tf_op jit(solution)/shard_map/ppermute | solution.py:16
  50.2 4.2 %collective-permute-start.22 = (f32[64,256]{1,0:T(8,128)S(1)}, f32[64,256]{1,0:T(8,128)S(1)}, u32[]{:S(2)}, u32[]{:S(2)}) collective-permute-start(f32[64,256]{1,0:T(8,128)S(1)} %add_subtract_fusion), channel_id=1, source_target_pairs={{0,3},{1,2},{2,1},{3,0},{4,7},{5,6},{6,5},{7,4},{8,11},{9,10},{10,... | collective-permute-start | bytes 196616 | tf_op jit(solution)/shard_map/ppermute | solution.py:16
  51.5 13.6 %collective-permute-start.27 = (f32[8,16,512]{2,1,0:T(8,128)S(1)}, f32[8,16,512]{2,1,0:T(8,128)S(1)}, u32[]{:S(2)}, u32[]{:S(2)}) collective-permute-start(f32[8,16,512]{2,1,0:T(8,128)S(1)} %maximum_select_fusion.7), channel_id=1, source_target_pairs={{0,1},{1,0},{2,3},{3,2},{4,5},{5,4},{6,7},{7,6},{8,9},{9,8},{10,11... | collective-permute-start | bytes 786440 | tf_op jit(solution)/shard_map/ppermute | solution.py:16
  51.9 6.7 %collective-permute-start.19 = (f32[64,256]{1,0:T(8,128)S(1)}, f32[64,256]{1,0:T(8,128)S(1)}, u32[]{:S(2)}, u32[]{:S(2)}) collective-permute-start(f32[64,256]{1,0:T(8,128)S(1)} %fusion.71), channel_id=1, source_target_pairs={{0,1},{1,0},{2,3},{3,2},{4,5},{5,4},{6,7},{7,6},{8,9},{9,8},{10,11... | collective-permute-start | bytes 196616 | tf_op jit(solution)/shard_map/ppermute | solution.py:16
  54.4 4.2 %collective-permute-start.23 = (f32[64,256]{1,0:T(8,128)S(1)}, f32[64,256]{1,0:T(8,128)S(1)}, u32[]{:S(2)}, u32[]{:S(2)}) collective-permute-start(f32[64,256]{1,0:T(8,128)S(1)} %add.49), channel_id=1, source_target_pairs={{0,5},{1,4},{2,7},{3,6},{4,1},{5,0},{6,3},{7,2},{8,13},{9,12},{10,... | collective-permute-start | bytes 196616 | tf_op jit(solution)/shard_map/ppermute | solution.py:16
  58.5 4.2 %collective-permute-start.24 = (f32[64,256]{1,0:T(8,128)S(1)}, f32[64,256]{1,0:T(8,128)S(1)}, u32[]{:S(2)}, u32[]{:S(2)}) collective-permute-start(f32[64,256]{1,0:T(8,128)S(1)} %add.50), channel_id=1, source_target_pairs={{0,9},{1,8},{2,11},{3,10},{4,13},{5,12},{6,15},{7,14},{8,1},{9,0},... | collective-permute-start | bytes 196616 | tf_op jit(solution)/shard_map/ppermute | solution.py:16
  62.7 6.4 %collective-permute-start.25 = (f32[64,256]{1,0:T(8,128)S(1)}, f32[64,256]{1,0:T(8,128)S(1)}, u32[]{:S(2)}, u32[]{:S(2)}) collective-permute-start(f32[64,256]{1,0:T(8,128)S(1)} %add.51), channel_id=1, source_target_pairs={{0,17},{1,16},{2,19},{3,18},{4,21},{5,20},{6,23},{7,22},{8,25},{9,... | collective-permute-start | bytes 196616 | tf_op jit(solution)/shard_map/ppermute | solution.py:16
  69.5 1.3 %collective-permute-start.28 = (f32[64,256]{1,0:T(8,128)S(1)}, f32[64,256]{1,0:T(8,128)S(1)}, u32[]{:S(2)}, u32[]{:S(2)}) collective-permute-start(f32[64,256]{1,0:T(8,128)S(1)} %fusion.84), channel_id=1, source_target_pairs={{0,1},{1,0},{2,3},{3,2},{4,5},{5,4},{6,7},{7,6},{8,9},{9,8},{10,11... | collective-permute-start | bytes 196616 | tf_op jit(solution)/shard_map/ppermute | solution.py:16

commit v3 on v2

--- a/solution.py
+++ b/solution.py
@@ -7,7 +7,6 @@
 
 LEVELS = 5
 HIGH = lax.Precision.HIGH
-IN_HBM = pl.BlockSpec(memory_space=pltpu.HBM)
 IN_VMEM = pl.BlockSpec(memory_space=pltpu.VMEM)
 
 
@@ -53,54 +52,27 @@
     return both[:rows] + (both[rows:] + one(left_high, right_low))
 
 
-def begin(rhs, proj_bases, corr_bases, cores, first, leaf_core, groups):
-    rows, width = rhs.shape
-    rank = proj_bases.shape[2]
-    shapes = [(width, rank), (width, rows)] + [(rows, rank)] * 2
-    shapes += [(rank, 2 * rank)] if leaf_core else []
-    shapes += [(sum(n for _, n in group), 2 * rank) for group in groups]
-
-    def body(x_hbm, p_hbm, w_hbm, c_hbm, *refs):
-        outs, (x_ref, p_ref, sems) = list(refs[: len(shapes)]), refs[len(shapes) :]
-        q_out, state_out, w_out, p_out = outs[:4]
-        rest = outs[4:]
-        moves = [(x_hbm, x_ref), (p_hbm.at[first], p_ref)]
-        if leaf_core:
-            moves.append((c_hbm.at[first], rest.pop(0)))
-        moves += [(w_hbm.at[first], w_out), (p_hbm.at[first - 1], p_out)]
-        for group, out in zip(groups, rest):
+def pack(cores, groups, after):
+    width = cores.shape[2]
+
+    def body(core_ref, _, *outs):
+        for group, out in zip(groups, outs):
             start = 0
             for level, n in group:
-                moves.append((c_hbm.at[level, 0:n], out.at[start : start + n]))
+                out[start : start + n, :] = core_ref[level, 0:n, :]
                 start += n
-        copies = [pltpu.make_async_copy(a, b, sems.at[at]) for at, (a, b) in enumerate(moves)]
-        for copy in copies:
-            copy.start()
-        copies[0].wait()
-        state = x_ref[...].T
-        state_out[...] = state
-        copies[1].wait()
-        q_out[...] = three_passes(state, p_ref[...], 0)
-        for copy in copies[2:]:
-            copy.wait()
-
-    count = 4 + (1 if leaf_core else 0) + sum(len(group) for group in groups)
+
     return pl.pallas_call(
         body,
-        in_specs=[IN_HBM] * 4,
-        out_specs=[IN_VMEM] * len(shapes),
-        out_shape=[pltpu.VMEM(shape, jnp.float32) for shape in shapes],
-        scratch_shapes=[
-            pltpu.VMEM((rows, width), jnp.float32),
-            pltpu.VMEM((rows, rank), jnp.float32),
-            pltpu.SemaphoreType.DMA((count,)),
+        in_specs=[IN_VMEM, pl.BlockSpec(memory_space=pl.ANY)],
+        out_specs=[IN_VMEM] * len(groups),
+        out_shape=[
+            jax.ShapeDtypeStruct((sum(n for _, n in group), width), jnp.float32) for group in groups
         ],
-        compiler_params=pltpu.CompilerParams(vmem_limit_bytes=52 * 2**20),
-        cost_estimate=pl.CostEstimate(
-            flops=6 * rows * width * rank, bytes_accessed=2**22, transcendentals=0
-        ),
-        name="begin",
-    )(rhs, proj_bases, corr_bases, cores)
+        compiler_params=pltpu.CompilerParams(vmem_limit_bytes=16 * 2**20),
+        cost_estimate=pl.CostEstimate(flops=0, bytes_accessed=2**20, transcendentals=0),
+        name="pack",
+    )(cores, after)
 
 
 def finish(state, corr, held):
@@ -155,13 +127,13 @@
     tails = [(level, rank >> bits[level]) for level in chain if bits[level] > 1]
     groups = [group for group in (heads, tails) if group]
     leaf_core = bits[first] == 0
-    value, state, top_corr, next_proj, *fetched = begin(
-        rhs, proj_bases, corr_bases, cores, first, leaf_core, groups
-    )
+    value = jnp.einsum("nk,nr->kr", rhs, proj_bases[first], precision=HIGH)
+    state = rhs.T
+    fetched = pack(cores, groups, value)
 
     table = {}
     if leaf_core:
-        table[first] = fetched.pop(0)
+        table[first] = cores[first]
 
     def finish_table(level, mine):
         part = exchange(mine, 1)
@@ -221,8 +193,8 @@
         held = times_transposed(top, table[first])
     else:
         held = chip_gather(solve(first, chip_sum(value), {}))
-    state = update(top_corr, state, held)
-    value = chip_sum(project(next_proj, state))
+    state = update(corr_bases[first], state, held)
+    value = chip_sum(project(proj_bases[first - 1], state))
     if heads:
         step(value)
         finish_table(heads[0][0], tie(fetched[0], value)[None])

time: 72.6 us -> 70 us (0.964)
  waiting for transfers between devices: 27.4 us -> 19.6 us
  matrix products: 20.5 us -> 25.1 us
  starting transfers between devices: 18.5 us -> 21 us
  Pallas kernels: 3.68 us -> 1.39 us
    ppermute x29, waiting for transfers between devices: 27.4 us -> 19.6 us  [exchange(): return lax.ppermute(value, 'leaf', pairs)]
    ppermute x29, starting transfers between devices: 18.5 us -> 21 us  [exchange(): return lax.ppermute(value, 'leaf', pairs)]
    pallas_call x1, Pallas kernels: 2.33 us -> 0.03 us  [pack(): pl.pallas_call(body, in_specs=[IN_VMEM, pl.BlockSpec(memory_space=pl.ANY)...]
    dot_general x0 -> x1, matrix products: none -> 2.12 us  [on_device(): value = jnp.einsum('nk,nr->kr', rhs, proj_bases[first], precision=HIGH)]
    dot_general x4, matrix products: 5.46 us -> 6.88 us  [project(): return jnp.einsum('kn,nr->kr', state, basis, precision=HIGH)]
    dot_general x4, matrix products: 3.93 us -> 5.07 us  [update(): return state - jnp.einsum('ka,na->kn', held, corr, precision=HIGH)]
  transfers between devices with their start and end apart: 29 -> 29, of which waited for: 11 -> 9; matrix products, arithmetic and copies ran while one was open for 25% -> 27% of each run, Pallas kernels for 0% -> 0%
where the time goes in v3:
time: 70 us; the launch traced here: 69.5 us
  matrix products  25.1 us (36%)
  starting transfers between devices  21 us (30%)
  waiting for transfers between devices  19.6 us (28%)
  local copies, waits for them, and re-layouts  1.51 us (2%)
  Pallas kernels  1.39 us (2%)
    ppermute x29, starting transfers between devices, exchange(): return lax.ppermute(value, 'leaf', pairs)  21 us
    ppermute x29, waiting for transfers between devices, exchange(): return lax.ppermute(value, 'leaf', pairs)  19.6 us
    dot_general x3, matrix products, on_device(): own = jnp.einsum('na,nb->ab', proj, corr, precision=HIGH)  7.28 us
    dot_general x4, matrix products, project(): return jnp.einsum('kn,nr->kr', state, basis, precision=HIGH)  6.88 us
    dot_general x4, matrix products, update(): return state - jnp.einsum('ka,na->kn', held, corr, precision=HIGH)  5.07 us
    dot_general x8, matrix products, times_transposed(): return jnp.einsum('kb,ab->ka', left, right, precision=HIGH)  3.79 us
    dot_general x1, matrix products, on_device(): value = jnp.einsum('nk,nr->kr', rhs, proj_bases[first], precision=HIGH)  2.12 us
  transfers between devices with their start and end apart: 29, of which 9 were waited for; matrix products, arithmetic and copies ran while one was open for 27% of the time, Pallas kernels for 0%

profile of v3, /device:TPU:0, one launch (start us, length us, event | category | flops | bytes accessed | tf_op | source)
XLA Modules:
  0.0 69.5 jit_solution(17430353636180074465)
XLA Ops:
  0.0 2.1 %fusion.21._ = f32[128,256]{1,0:T(8,128)S(1)} fusion(f32[1024,128]{1,0:T(8,128)} %param.4, f32[5,1024,256]{2,1,0:T(8,128)} %param.5), kind=kOutput, calls=%fused_computation.25 | convolution fusion | flops 201326592 | bytes 1703936 | tf_op jit(solution)/shard_map/nk,nr->kr/dot_general | solution.py:130
  2.1 0.5 collective-permute-start
  2.6 1.2 %copy.6 = f32[1024,128]{0,1:T(8,128)S(1)} copy(f32[1024,128]{1,0:T(8,128)} %param.4) | data formatting | bytes 1048576 | tf_op args[0]
  3.9 1.4 %fusion.38 = f32[128,256]{1,0:T(8,128)S(1)} fusion(f32[5,256,512]{2,1,0:T(8,128)} %core_ref.1, f32[128,256]{1,0:T(8,128)S(1)} %collective-permute-done, f32[128,256]{1,0:T(8,128)S(1)} %fusion.21._, pred[]{:T(512)S(6)} %eq.12), kind=kOutput, calls=%fused_computation.47 | convolution fusion | flops 100925440 | bytes 917505 | tf_op jit(solution)/shard_map/kb,ab->ka/dot_general | solution.py:35
  5.4 1.9 %convolution_subtract_fusion.3 = f32[128,1024]{1,0:T(8,128)S(1)} fusion(f32[128,256]{1,0:T(8,128)S(1)} %fusion.38, f32[5,1024,256]{2,1,0:T(8,128)} %param.6, f32[1024,128]{0,1:T(8,128)S(1)} %copy.6), kind=kOutput, calls=%fused_computation.3 | convolution fusion | flops 201457664 | bytes 2228224 | tf_op jit(solution)/shard_map/ka,na->kn/dot_general | solution.py:188
  7.3 0.0 copy-start.1
  7.3 1.8 %fusion.18 = f32[128,256]{1,0:T(8,128)S(1)} fusion(f32[128,1024]{1,0:T(8,128)S(1)} %convolution_subtract_fusion.3, f32[5,1024,256]{2,1,0:T(8,128)} %param.5), kind=kOutput, calls=%fused_computation.22 | convolution fusion | flops 201326592 | bytes 1703936 | tf_op jit(solution)/shard_map/kn,nr->kr/dot_general | solution.py:31
  9.1 0.1 collective-permute-start.1
  9.3 3.0 %collective-permute-start.9 = (f32[1,112,512]{2,1,0:T(8,128)S(1)}, f32[1,112,512]{2,1,0:T(8,128)S(1)}, u32[]{:S(2)}, u32[]{:S(2)}) collective-permute-start(f32[1,112,512]{2,1,0:T(8,128)S(1)} %bitcast.76), channel_id=1, source_target_pairs={{0,2},{1,3},{2,0},{3,1},{4,6},{5,7},{6,4},{7,5},{8,10},{9,11},{10,... | collective-permute-start | bytes 688136 | tf_op jit(solution)/shard_map/ppermute | solution.py:15
  12.3 0.8 %collective-permute-start.2 = (f32[64,256]{1,0:T(8,128)S(1)}, f32[64,256]{1,0:T(8,128)S(1)}, u32[]{:S(2)}, u32[]{:S(2)}) collective-permute-start(f32[64,256]{1,0:T(8,128)S(1)} %select_add_fusion), channel_id=1, source_target_pairs={{0,3},{1,2},{2,1},{3,0},{4,7},{5,6},{6,5},{7,4},{8,11},{9,10},{10,... | collective-permute-start | bytes 196616 | tf_op jit(solution)/shard_map/ppermute | solution.py:15
  13.1 0.2 collective-permute-start.3
  13.3 1.8 %fusion.14 = f32[128,256]{1,0:T(8,128)S(1)} fusion(f32[128,1024]{1,0:T(8,128)} %copy-done.1, f32[5,1024,256]{2,1,0:T(8,128)} %param.5), kind=kOutput, calls=%fused_computation.18 | convolution fusion | flops 201326592 | bytes 1703936 | tf_op jit(solution)/shard_map/kn,nr->kr/dot_general | solution.py:31
  15.1 0.0 copy-start.2
  15.1 0.4 collective-permute-start.5
  15.5 2.5 %fusion.12 = f32[256,256]{1,0:T(8,128)S(1)} fusion(f32[5,1024,256]{2,1,0:T(8,128)} %param.5, f32[5,1024,256]{2,1,0:T(8,128)} %param.6), kind=kOutput, calls=%fused_computation.16 | convolution fusion | flops 402653184 | bytes 2359296 | tf_op jit(solution)/shard_map/na,nb->ab/dot_general | solution.py:207
  18.1 0.2 collective-permute-start.6
  18.3 0.4 collective-permute-done.9
  18.8 0.1 collective-permute-start.10
  18.9 2.0 %collective-permute-start.17 = (f32[2,48,512]{2,1,0:T(8,128)S(1)}, f32[2,48,512]{2,1,0:T(8,128)S(1)}, u32[]{:S(2)}, u32[]{:S(2)}) collective-permute-start(f32[2,48,512]{2,1,0:T(8,128)S(1)} %slice.111), channel_id=1, source_target_pairs={{0,4},{1,5},{2,6},{3,7},{4,0},{5,1},{6,2},{7,3},{8,12},{9,13},{10,... | collective-permute-start | bytes 589832 | tf_op jit(solution)/shard_map/ppermute | solution.py:15
  20.9 0.4 fusion.55
  21.3 0.2 collective-permute-start.4
  21.5 0.3 add_subtract_fusion.2
  21.8 1.5 %collective-permute-start.7 = (f32[64,256]{1,0:T(8,128)S(1)}, f32[64,256]{1,0:T(8,128)S(1)}, u32[]{:S(2)}, u32[]{:S(2)}) collective-permute-start(f32[64,256]{1,0:T(8,128)S(1)} %add_subtract_fusion.2), channel_id=1, source_target_pairs={{0,3},{1,2},{2,1},{3,0},{4,7},{5,6},{6,5},{7,4},{8,11},{9,10},{10,... | collective-permute-start | bytes 196616 | tf_op jit(solution)/shard_map/ppermute | solution.py:15
  23.3 2.5 %fusion.6 = f32[256,256]{1,0:T(8,128)S(1)} fusion(f32[5,1024,256]{2,1,0:T(8,128)} %param.5, f32[5,1024,256]{2,1,0:T(8,128)} %param.6), kind=kOutput, calls=%fused_computation.10 | convolution fusion | flops 402653184 | bytes 2359296 | tf_op jit(solution)/shard_map/na,nb->ab/dot_general | solution.py:207
  25.9 0.2 collective-permute-start.13
  26.1 0.0 slice-start.1
  26.2 0.5 collective-permute-start.8
  26.8 1.9 %convolution_subtract_fusion.2 = f32[128,1024]{1,0:T(8,128)S(1)} fusion(f32[128,1024]{1,0:T(8,128)S(1)} %copy-done.2, f32[5,1024,256]{2,1,0:T(8,128)} %param.6, f32[64,256]{1,0:T(8,128)S(1)} %collective-permute-done.4, f32[64,256]{1,0:T(8,128)S(1)} %fusion.55, pred[]{:T(512)S(6)} %eq.26), kind=kOutput, calls=%fused_computation.2 | convolution fusion | flops 201555968 | bytes 2228225 | tf_op jit(solution)/shard_map/ka,na->kn/dot_general | solution.py:188
  28.6 1.6 %fusion.8 = f32[128,256]{1,0:T(8,128)S(1)} fusion(f32[128,1024]{1,0:T(8,128)S(1)} %convolution_subtract_fusion.2, f32[5,1024,256]{2,1,0:T(8,128)} %param.5), kind=kOutput, calls=%fused_computation.12 | convolution fusion | flops 201326592 | bytes 1703936 | tf_op jit(solution)/shard_map/kn,nr->kr/dot_general | solution.py:31
  30.3 0.4 fusion.68
  30.7 0.2 collective-permute-start.11
  31.0 0.4 collective-permute-start.12
  31.4 0.2 collective-permute-start.18
  31.6 1.6 %collective-permute-start.26 = (f32[4,16,512]{2,1,0:T(8,128)S(1)}, f32[4,16,512]{2,1,0:T(8,128)S(1)}, u32[]{:S(2)}, u32[]{:S(2)}) collective-permute-start(f32[4,16,512]{2,1,0:T(8,128)S(1)} %slice.115), channel_id=1, source_target_pairs={{0,8},{1,9},{2,10},{3,11},{4,12},{5,13},{6,14},{7,15},{8,0},{9,1},... | collective-permute-start | bytes 393224 | tf_op jit(solution)/shard_map/ppermute | solution.py:15
  33.2 0.7 convolution_subtract_fusion.1
  33.9 0.3 add_subtract_fusion.1
  34.2 1.0 %collective-permute-start.14 = (f32[64,256]{1,0:T(8,128)S(1)}, f32[64,256]{1,0:T(8,128)S(1)}, u32[]{:S(2)}, u32[]{:S(2)}) collective-permute-start(f32[64,256]{1,0:T(8,128)S(1)} %add_subtract_fusion.1), channel_id=1, source_target_pairs={{0,3},{1,2},{2,1},{3,0},{4,7},{5,6},{6,5},{7,4},{8,11},{9,10},{10,... | collective-permute-start | bytes 196616 | tf_op jit(solution)/shard_map/ppermute | solution.py:15
  35.2 1.6 %fusion.4 = f32[128,256]{1,0:T(8,128)S(1)} fusion(f32[128,1024]{1,0:T(8,128)S(1)} %convolution_subtract_fusion.1, f32[5,1024,256]{2,1,0:T(8,128)} %param.5), kind=kOutput, calls=%fused_computation.8 | convolution fusion | flops 201326592 | bytes 1703936 | tf_op jit(solution)/shard_map/kn,nr->kr/dot_general | solution.py:31
  36.9 0.4 collective-permute-start.20
  37.3 1.1 %collective-permute-done.14 = f32[64,256]{1,0:T(8,128)S(1)} collective-permute-done((f32[64,256]{1,0:T(8,128)S(1)}, f32[64,256]{1,0:T(8,128)S(1)}, u32[]{:S(2)}, u32[]{:S(2)}) %collective-permute-start.14) | collective-permute-done | bytes 65568 | tf_op jit(solution)/shard_map/ppermute | solution.py:15
  38.4 1.3 %collective-permute-start.15 = (f32[64,256]{1,0:T(8,128)S(1)}, f32[64,256]{1,0:T(8,128)S(1)}, u32[]{:S(2)}, u32[]{:S(2)}) collective-permute-start(f32[64,256]{1,0:T(8,128)S(1)} %add.45), channel_id=1, source_target_pairs={{0,5},{1,4},{2,7},{3,6},{4,1},{5,0},{6,3},{7,2},{8,13},{9,12},{10,... | collective-permute-start | bytes 196616 | tf_op jit(solution)/shard_map/ppermute | solution.py:15
  39.7 2.2 %fusion.1 = f32[256,256]{1,0:T(8,128)S(1)} fusion(f32[5,1024,256]{2,1,0:T(8,128)S(1)} %bitcast.79, f32[5,1024,256]{2,1,0:T(8,128)} %param.5), kind=kOutput, calls=%fused_computation.5 | convolution fusion | flops 402653184 | bytes 2359296 | tf_op jit(solution)/shard_map/na,nb->ab/dot_general | solution.py:207
  41.9 0.5 collective-permute-start.21
  42.4 0.2 collective-permute-done.15
  42.6 0.2 collective-permute-start.16
  42.9 3.9 %collective-permute-done.16 = f32[64,256]{1,0:T(8,128)S(1)} collective-permute-done((f32[64,256]{1,0:T(8,128)S(1)}, f32[64,256]{1,0:T(8,128)S(1)}, u32[]{:S(2)}, u32[]{:S(2)}) %collective-permute-start.16) | collective-permute-done | bytes 65568 | tf_op jit(solution)/shard_map/ppermute | solution.py:15
  46.7 0.4 fusion.81
  47.1 0.3 add_subtract_fusion
  47.4 0.9 %collective-permute-start.22 = (f32[64,256]{1,0:T(8,128)S(1)}, f32[64,256]{1,0:T(8,128)S(1)}, u32[]{:S(2)}, u32[]{:S(2)}) collective-permute-start(f32[64,256]{1,0:T(8,128)S(1)} %add_subtract_fusion), channel_id=1, source_target_pairs={{0,3},{1,2},{2,1},{3,0},{4,7},{5,6},{6,5},{7,4},{8,11},{9,10},{10,... | collective-permute-start | bytes 196616 | tf_op jit(solution)/shard_map/ppermute | solution.py:15
  48.4 0.5 collective-permute-start.27
  48.8 0.1 collective-permute-start.19
  49.0 2.6 %collective-permute-done.22 = f32[64,256]{1,0:T(8,128)S(1)} collective-permute-done((f32[64,256]{1,0:T(8,128)S(1)}, f32[64,256]{1,0:T(8,128)S(1)}, u32[]{:S(2)}, u32[]{:S(2)}) %collective-permute-start.22) | collective-permute-done | bytes 65568 | tf_op jit(solution)/shard_map/ppermute | solution.py:15
  51.6 1.3 %collective-permute-start.23 = (f32[64,256]{1,0:T(8,128)S(1)}, f32[64,256]{1,0:T(8,128)S(1)}, u32[]{:S(2)}, u32[]{:S(2)}) collective-permute-start(f32[64,256]{1,0:T(8,128)S(1)} %add.49), channel_id=1, source_target_pairs={{0,5},{1,4},{2,7},{3,6},{4,1},{5,0},{6,3},{7,2},{8,13},{9,12},{10,... | collective-permute-start | bytes 196616 | tf_op jit(solution)/shard_map/ppermute | solution.py:15
  52.9 0.1 slice_bitcast_fusion.w_ref
  52.9 2.8 %collective-permute-done.23 = f32[64,256]{1,0:T(8,128)S(1)} collective-permute-done((f32[64,256]{1,0:T(8,128)S(1)}, f32[64,256]{1,0:T(8,128)S(1)}, u32[]{:S(2)}, u32[]{:S(2)}) %collective-permute-start.23) | collective-permute-done | bytes 65568 | tf_op jit(solution)/shard_map/ppermute | solution.py:15
  55.8 0.1 collective-permute-start.24
  55.9 0.7 convolution_subtract_fusion.x_ref
  56.6 3.4 %collective-permute-done.24 = f32[64,256]{1,0:T(8,128)S(1)} collective-permute-done((f32[64,256]{1,0:T(8,128)S(1)}, f32[64,256]{1,0:T(8,128)S(1)}, u32[]{:S(2)}, u32[]{:S(2)}) %collective-permute-start.24) | collective-permute-done | bytes 65568 | tf_op jit(solution)/shard_map/ppermute | solution.py:15
  59.9 2.4 %collective-permute-start.25 = (f32[64,256]{1,0:T(8,128)S(1)}, f32[64,256]{1,0:T(8,128)S(1)}, u32[]{:S(2)}, u32[]{:S(2)}) collective-permute-start(f32[64,256]{1,0:T(8,128)S(1)} %add.51), channel_id=1, source_target_pairs={{0,17},{1,16},{2,19},{3,18},{4,21},{5,20},{6,23},{7,22},{8,25},{9,... | collective-permute-start | bytes 196616 | tf_op jit(solution)/shard_map/ppermute | solution.py:15
  62.4 4.0 %collective-permute-done.25 = f32[64,256]{1,0:T(8,128)S(1)} collective-permute-done((f32[64,256]{1,0:T(8,128)S(1)}, f32[64,256]{1,0:T(8,128)S(1)}, u32[]{:S(2)}, u32[]{:S(2)}) %collective-permute-start.25) | collective-permute-done | bytes 65568 | tf_op jit(solution)/shard_map/ppermute | solution.py:15
  66.5 0.4 fusion.94
  66.8 0.2 collective-permute-start.28
  67.0 1.1 %collective-permute-done.28 = f32[64,256]{1,0:T(8,128)S(1)} collective-permute-done((f32[64,256]{1,0:T(8,128)S(1)}, f32[64,256]{1,0:T(8,128)S(1)}, u32[]{:S(2)}, u32[]{:S(2)}) %collective-permute-start.28) | collective-permute-done | bytes 65568 | tf_op jit(solution)/shard_map/ppermute | solution.py:15
  68.2 1.4 %finish.1 = f32[1024,128]{1,0:T(8,128)} custom-call(f32[128,1024]{1,0:T(8,128)S(1)} %convolution_subtract_fusion.x_ref, f32[1024,256]{1,0:T(8,128)S(1)} %slice_bitcast_fusion.w_ref, f32[128,256]{1,0:T(8,128)S(1)} %maximum_select_fusion.18.t_ref), custom_call_target="tpu_custom_call" | custom-call | flops 201326592 | bytes 2097152 | tf_op jit(solution)/shard_map/finish/pallas_call | solution.py:84
  (55 shorter events, 0.7 us)
Async XLA Ops:
  0.0 9.3 %copy-start = (f32[5,256,512]{2,1,0:T(8,128)S(1)}, f32[5,256,512]{2,1,0:T(8,128)}, u32[]{:S(2)}) copy-start(f32[5,256,512]{2,1,0:T(8,128)} %core_ref.1) | copy-start | bytes 7864324
  2.1 1.8 %collective-permute-start = (f32[128,256]{1,0:T(8,128)S(1)}, f32[128,256]{1,0:T(8,128)S(1)}, u32[]{:S(2)}, u32[]{:S(2)}) collective-permute-start(f32[128,256]{1,0:T(8,128)S(1)} %fusion.21._), channel_id=1, source_target_pairs={{0,1},{1,0},{2,3},{3,2},{4,5},{5,4},{6,7},{7,6},{8,9},{9,8},{10,11... | collective-permute-start | bytes 393224 | tf_op jit(solution)/shard_map/ppermute | solution.py:15
  7.3 1.9 %copy-start.1 = (f32[128,1024]{1,0:T(8,128)}, f32[128,1024]{1,0:T(8,128)S(1)}, u32[]{:S(2)}) copy-start(f32[128,1024]{1,0:T(8,128)S(1)} %convolution_subtract_fusion.3) | copy-start | bytes 1572868
  9.1 3.2 %collective-permute-start.1 = (f32[64,256]{1,0:T(8,128)S(1)}, f32[64,256]{1,0:T(8,128)S(1)}, u32[]{:S(2)}, u32[]{:S(2)}) collective-permute-start(f32[64,256]{1,0:T(8,128)S(1)} %slice_select_fusion.3), channel_id=1, source_target_pairs={{0,1},{1,0},{2,3},{3,2},{4,5},{5,4},{6,7},{7,6},{8,9},{9,8},{10,11... | collective-permute-start | bytes 196616 | tf_op jit(solution)/shard_map/ppermute | solution.py:15
  9.3 9.4 %collective-permute-start.9 = (f32[1,112,512]{2,1,0:T(8,128)S(1)}, f32[1,112,512]{2,1,0:T(8,128)S(1)}, u32[]{:S(2)}, u32[]{:S(2)}) collective-permute-start(f32[1,112,512]{2,1,0:T(8,128)S(1)} %bitcast.76), channel_id=1, source_target_pairs={{0,2},{1,3},{2,0},{3,1},{4,6},{5,7},{6,4},{7,5},{8,10},{9,11},{10,... | collective-permute-start | bytes 688136 | tf_op jit(solution)/shard_map/ppermute | solution.py:15
  12.3 8.6 %collective-permute-start.2 = (f32[64,256]{1,0:T(8,128)S(1)}, f32[64,256]{1,0:T(8,128)S(1)}, u32[]{:S(2)}, u32[]{:S(2)}) collective-permute-start(f32[64,256]{1,0:T(8,128)S(1)} %select_add_fusion), channel_id=1, source_target_pairs={{0,3},{1,2},{2,1},{3,0},{4,7},{5,6},{6,5},{7,4},{8,11},{9,10},{10,... | collective-permute-start | bytes 196616 | tf_op jit(solution)/shard_map/ppermute | solution.py:15
  13.1 5.7 %collective-permute-start.3 = (f32[1,128,512]{2,1,0:T(8,128)S(1)}, f32[1,128,512]{2,1,0:T(8,128)S(1)}, u32[]{:S(2)}, u32[]{:S(2)}) collective-permute-start(f32[1,128,512]{2,1,0:T(8,128)S(1)} %bitcast.74), channel_id=1, source_target_pairs={{0,1},{1,0},{2,3},{3,2},{4,5},{5,4},{6,7},{7,6},{8,9},{9,8},{10,11... | collective-permute-start | bytes 786440 | tf_op jit(solution)/shard_map/ppermute | solution.py:15
  15.1 11.6 %copy-start.2 = (f32[128,1024]{1,0:T(8,128)S(1)}, f32[128,1024]{1,0:T(8,128)}, u32[]{:S(2)}) copy-start(f32[128,1024]{1,0:T(8,128)} %copy-done.1) | copy-start | bytes 1572868
  15.1 6.4 %collective-permute-start.5 = (f32[64,256]{1,0:T(8,128)S(1)}, f32[64,256]{1,0:T(8,128)S(1)}, u32[]{:S(2)}, u32[]{:S(2)}) collective-permute-start(f32[64,256]{1,0:T(8,128)S(1)} %slice_select_fusion.2), channel_id=1, source_target_pairs={{0,1},{1,0},{2,3},{3,2},{4,5},{5,4},{6,7},{7,6},{8,9},{9,8},{10,11... | collective-permute-start | bytes 196616 | tf_op jit(solution)/shard_map/ppermute | solution.py:15
  18.1 3.4 %collective-permute-start.6 = (f32[256,256]{1,0:T(8,128)S(1)}, f32[256,256]{1,0:T(8,128)S(1)}, u32[]{:S(2)}, u32[]{:S(2)}) collective-permute-start(f32[256,256]{1,0:T(8,128)S(1)} %fusion.12), channel_id=1, source_target_pairs={{0,1},{1,0},{2,3},{3,2},{4,5},{5,4},{6,7},{7,6},{8,9},{9,8},{10,11... | collective-permute-start | bytes 786440 | tf_op jit(solution)/shard_map/ppermute | solution.py:15
  18.8 7.3 %collective-permute-start.10 = (f32[2,64,512]{2,1,0:T(8,128)S(1)}, f32[2,64,512]{2,1,0:T(8,128)S(1)}, u32[]{:S(2)}, u32[]{:S(2)}) collective-permute-start(f32[2,64,512]{2,1,0:T(8,128)S(1)} %slice.108), channel_id=1, source_target_pairs={{0,1},{1,0},{2,3},{3,2},{4,5},{5,4},{6,7},{7,6},{8,9},{9,8},{10,11... | collective-permute-start | bytes 786440 | tf_op jit(solution)/shard_map/ppermute | solution.py:15
  18.9 11.4 %collective-permute-start.17 = (f32[2,48,512]{2,1,0:T(8,128)S(1)}, f32[2,48,512]{2,1,0:T(8,128)S(1)}, u32[]{:S(2)}, u32[]{:S(2)}) collective-permute-start(f32[2,48,512]{2,1,0:T(8,128)S(1)} %slice.111), channel_id=1, source_target_pairs={{0,4},{1,5},{2,6},{3,7},{4,0},{5,1},{6,2},{7,3},{8,12},{9,13},{10,... | collective-permute-start | bytes 589832 | tf_op jit(solution)/shard_map/ppermute | solution.py:15
  20.9 12.3 %slice-start = ((s8[5242880]{0:T(1024)(128)(4,1)}), s8[4194304]{0:T(1024)(128)(4,1)S(1)}, s32[]{:S(2)}) async-start(s8[5242880]{0:T(1024)(128)(4,1)} %bitcast.78), calls=%async_computation | async-start | bytes 8388608
  21.3 5.5 %collective-permute-start.4 = (f32[64,256]{1,0:T(8,128)S(1)}, f32[64,256]{1,0:T(8,128)S(1)}, u32[]{:S(2)}, u32[]{:S(2)}) collective-permute-start(f32[64,256]{1,0:T(8,128)S(1)} %fusion.55), channel_id=1, source_target_pairs={{0,1},{1,0},{2,3},{3,2},{4,5},{5,4},{6,7},{7,6},{8,9},{9,8},{10,11... | collective-permute-start | bytes 196616 | tf_op jit(solution)/shard_map/ppermute | solution.py:15
  21.8 4.4 %collective-permute-start.7 = (f32[64,256]{1,0:T(8,128)S(1)}, f32[64,256]{1,0:T(8,128)S(1)}, u32[]{:S(2)}, u32[]{:S(2)}) collective-permute-start(f32[64,256]{1,0:T(8,128)S(1)} %add_subtract_fusion.2), channel_id=1, source_target_pairs={{0,3},{1,2},{2,1},{3,0},{4,7},{5,6},{6,5},{7,4},{8,11},{9,10},{10,... | collective-permute-start | bytes 196616 | tf_op jit(solution)/shard_map/ppermute | solution.py:15
  25.9 8.0 %collective-permute-start.13 = (f32[256,256]{1,0:T(8,128)S(1)}, f32[256,256]{1,0:T(8,128)S(1)}, u32[]{:S(2)}, u32[]{:S(2)}) collective-permute-start(f32[256,256]{1,0:T(8,128)S(1)} %fusion.6), channel_id=1, source_target_pairs={{0,1},{1,0},{2,3},{3,2},{4,5},{5,4},{6,7},{7,6},{8,9},{9,8},{10,11... | collective-permute-start | bytes 786440 | tf_op jit(solution)/shard_map/ppermute | solution.py:15
  26.1 7.0 %slice-start.1 = ((s8[5242880]{0:T(1024)(128)(4,1)}), s8[1048576]{0:T(1024)(128)(4,1)S(1)}, s32[]{:S(2)}) async-start(s8[5242880]{0:T(1024)(128)(4,1)} %bitcast.78), calls=%async_computation.1 | async-start | bytes 2097152
  26.2 4.1 %collective-permute-start.8 = (f32[64,256]{1,0:T(8,128)S(1)}, f32[64,256]{1,0:T(8,128)S(1)}, u32[]{:S(2)}, u32[]{:S(2)}) collective-permute-start(f32[64,256]{1,0:T(8,128)S(1)} %add.42), channel_id=1, source_target_pairs={{0,5},{1,4},{2,7},{3,6},{4,1},{5,0},{6,3},{7,2},{8,13},{9,12},{10,... | collective-permute-start | bytes 196616 | tf_op jit(solution)/shard_map/ppermute | solution.py:15
  30.7 2.5 %collective-permute-start.11 = (f32[64,256]{1,0:T(8,128)S(1)}, f32[64,256]{1,0:T(8,128)S(1)}, u32[]{:S(2)}, u32[]{:S(2)}) collective-permute-start(f32[64,256]{1,0:T(8,128)S(1)} %fusion.68), channel_id=1, source_target_pairs={{0,1},{1,0},{2,3},{3,2},{4,5},{5,4},{6,7},{7,6},{8,9},{9,8},{10,11... | collective-permute-start | bytes 196616 | tf_op jit(solution)/shard_map/ppermute | solution.py:15
  31.0 2.8 %collective-permute-start.12 = (f32[64,256]{1,0:T(8,128)S(1)}, f32[64,256]{1,0:T(8,128)S(1)}, u32[]{:S(2)}, u32[]{:S(2)}) collective-permute-start(f32[64,256]{1,0:T(8,128)S(1)} %slice_select_fusion.1), channel_id=1, source_target_pairs={{0,1},{1,0},{2,3},{3,2},{4,5},{5,4},{6,7},{7,6},{8,9},{9,8},{10,11... | collective-permute-start | bytes 196616 | tf_op jit(solution)/shard_map/ppermute | solution.py:15
  31.4 11.3 %collective-permute-start.18 = (f32[4,32,512]{2,1,0:T(8,128)S(1)}, f32[4,32,512]{2,1,0:T(8,128)S(1)}, u32[]{:S(2)}, u32[]{:S(2)}) collective-permute-start(f32[4,32,512]{2,1,0:T(8,128)S(1)} %slice.112), channel_id=1, source_target_pairs={{0,1},{1,0},{2,3},{3,2},{4,5},{5,4},{6,7},{7,6},{8,9},{9,8},{10,11... | collective-permute-start | bytes 786440 | tf_op jit(solution)/shard_map/ppermute | solution.py:15
  31.6 11.3 %collective-permute-start.26 = (f32[4,16,512]{2,1,0:T(8,128)S(1)}, f32[4,16,512]{2,1,0:T(8,128)S(1)}, u32[]{:S(2)}, u32[]{:S(2)}) collective-permute-start(f32[4,16,512]{2,1,0:T(8,128)S(1)} %slice.115), channel_id=1, source_target_pairs={{0,8},{1,9},{2,10},{3,11},{4,12},{5,13},{6,14},{7,15},{8,0},{9,1},... | collective-permute-start | bytes 393224 | tf_op jit(solution)/shard_map/ppermute | solution.py:15
  34.2 4.2 %collective-permute-start.14 = (f32[64,256]{1,0:T(8,128)S(1)}, f32[64,256]{1,0:T(8,128)S(1)}, u32[]{:S(2)}, u32[]{:S(2)}) collective-permute-start(f32[64,256]{1,0:T(8,128)S(1)} %add_subtract_fusion.1), channel_id=1, source_target_pairs={{0,3},{1,2},{2,1},{3,0},{4,7},{5,6},{6,5},{7,4},{8,11},{9,10},{10,... | collective-permute-start | bytes 196616 | tf_op jit(solution)/shard_map/ppermute | solution.py:15
  36.9 10.2 %collective-permute-start.20 = (f32[64,256]{1,0:T(8,128)S(1)}, f32[64,256]{1,0:T(8,128)S(1)}, u32[]{:S(2)}, u32[]{:S(2)}) collective-permute-start(f32[64,256]{1,0:T(8,128)S(1)} %slice_select_fusion), channel_id=1, source_target_pairs={{0,1},{1,0},{2,3},{3,2},{4,5},{5,4},{6,7},{7,6},{8,9},{9,8},{10,11... | collective-permute-start | bytes 196616 | tf_op jit(solution)/shard_map/ppermute | solution.py:15
  38.4 4.2 %collective-permute-start.15 = (f32[64,256]{1,0:T(8,128)S(1)}, f32[64,256]{1,0:T(8,128)S(1)}, u32[]{:S(2)}, u32[]{:S(2)}) collective-permute-start(f32[64,256]{1,0:T(8,128)S(1)} %add.45), channel_id=1, source_target_pairs={{0,5},{1,4},{2,7},{3,6},{4,1},{5,0},{6,3},{7,2},{8,13},{9,12},{10,... | collective-permute-start | bytes 196616 | tf_op jit(solution)/shard_map/ppermute | solution.py:15
  41.9 5.2 %collective-permute-start.21 = (f32[256,256]{1,0:T(8,128)S(1)}, f32[256,256]{1,0:T(8,128)S(1)}, u32[]{:S(2)}, u32[]{:S(2)}) collective-permute-start(f32[256,256]{1,0:T(8,128)S(1)} %fusion.1), channel_id=1, source_target_pairs={{0,1},{1,0},{2,3},{3,2},{4,5},{5,4},{6,7},{7,6},{8,9},{9,8},{10,11... | collective-permute-start | bytes 786440 | tf_op jit(solution)/shard_map/ppermute | solution.py:15
  42.6 4.2 %collective-permute-start.16 = (f32[64,256]{1,0:T(8,128)S(1)}, f32[64,256]{1,0:T(8,128)S(1)}, u32[]{:S(2)}, u32[]{:S(2)}) collective-permute-start(f32[64,256]{1,0:T(8,128)S(1)} %add.46), channel_id=1, source_target_pairs={{0,9},{1,8},{2,11},{3,10},{4,13},{5,12},{6,15},{7,14},{8,1},{9,0},... | collective-permute-start | bytes 196616 | tf_op jit(solution)/shard_map/ppermute | solution.py:15
  47.4 4.2 %collective-permute-start.22 = (f32[64,256]{1,0:T(8,128)S(1)}, f32[64,256]{1,0:T(8,128)S(1)}, u32[]{:S(2)}, u32[]{:S(2)}) collective-permute-start(f32[64,256]{1,0:T(8,128)S(1)} %add_subtract_fusion), channel_id=1, source_target_pairs={{0,3},{1,2},{2,1},{3,0},{4,7},{5,6},{6,5},{7,4},{8,11},{9,10},{10,... | collective-permute-start | bytes 196616 | tf_op jit(solution)/shard_map/ppermute | solution.py:15
  48.4 13.9 %collective-permute-start.27 = (f32[8,16,512]{2,1,0:T(8,128)S(1)}, f32[8,16,512]{2,1,0:T(8,128)S(1)}, u32[]{:S(2)}, u32[]{:S(2)}) collective-permute-start(f32[8,16,512]{2,1,0:T(8,128)S(1)} %maximum_select_fusion.7), channel_id=1, source_target_pairs={{0,1},{1,0},{2,3},{3,2},{4,5},{5,4},{6,7},{7,6},{8,9},{9,8},{10,11... | collective-permute-start | bytes 786440 | tf_op jit(solution)/shard_map/ppermute | solution.py:15
  48.8 7.1 %collective-permute-start.19 = (f32[64,256]{1,0:T(8,128)S(1)}, f32[64,256]{1,0:T(8,128)S(1)}, u32[]{:S(2)}, u32[]{:S(2)}) collective-permute-start(f32[64,256]{1,0:T(8,128)S(1)} %fusion.81), channel_id=1, source_target_pairs={{0,1},{1,0},{2,3},{3,2},{4,5},{5,4},{6,7},{7,6},{8,9},{9,8},{10,11... | collective-permute-start | bytes 196616 | tf_op jit(solution)/shard_map/ppermute | solution.py:15
  51.6 4.2 %collective-permute-start.23 = (f32[64,256]{1,0:T(8,128)S(1)}, f32[64,256]{1,0:T(8,128)S(1)}, u32[]{:S(2)}, u32[]{:S(2)}) collective-permute-start(f32[64,256]{1,0:T(8,128)S(1)} %add.49), channel_id=1, source_target_pairs={{0,5},{1,4},{2,7},{3,6},{4,1},{5,0},{6,3},{7,2},{8,13},{9,12},{10,... | collective-permute-start | bytes 196616 | tf_op jit(solution)/shard_map/ppermute | solution.py:15
  55.8 4.2 %collective-permute-start.24 = (f32[64,256]{1,0:T(8,128)S(1)}, f32[64,256]{1,0:T(8,128)S(1)}, u32[]{:S(2)}, u32[]{:S(2)}) collective-permute-start(f32[64,256]{1,0:T(8,128)S(1)} %add.50), channel_id=1, source_target_pairs={{0,9},{1,8},{2,11},{3,10},{4,13},{5,12},{6,15},{7,14},{8,1},{9,0},... | collective-permute-start | bytes 196616 | tf_op jit(solution)/shard_map/ppermute | solution.py:15
  59.9 6.5 %collective-permute-start.25 = (f32[64,256]{1,0:T(8,128)S(1)}, f32[64,256]{1,0:T(8,128)S(1)}, u32[]{:S(2)}, u32[]{:S(2)}) collective-permute-start(f32[64,256]{1,0:T(8,128)S(1)} %add.51), channel_id=1, source_target_pairs={{0,17},{1,16},{2,19},{3,18},{4,21},{5,20},{6,23},{7,22},{8,25},{9,... | collective-permute-start | bytes 196616 | tf_op jit(solution)/shard_map/ppermute | solution.py:15
  66.8 1.3 %collective-permute-start.28 = (f32[64,256]{1,0:T(8,128)S(1)}, f32[64,256]{1,0:T(8,128)S(1)}, u32[]{:S(2)}, u32[]{:S(2)}) collective-permute-start(f32[64,256]{1,0:T(8,128)S(1)} %fusion.94), channel_id=1, source_target_pairs={{0,1},{1,0},{2,3},{3,2},{4,5},{5,4},{6,7},{7,6},{8,9},{9,8},{10,11... | collective-permute-start | bytes 196616 | tf_op jit(solution)/shard_map/ppermute | solution.py:15

commit v4 on v2

--- a/solution.py
+++ b/solution.py
@@ -56,14 +56,14 @@
 def begin(rhs, proj_bases, corr_bases, cores, first, leaf_core, groups):
     rows, width = rhs.shape
     rank = proj_bases.shape[2]
-    shapes = [(width, rank), (width, rows)] + [(rows, rank)] * 2
+    shapes = [(width, rank), (width, rows)] + [(rows, rank)] * 4
     shapes += [(rank, 2 * rank)] if leaf_core else []
     shapes += [(sum(n for _, n in group), 2 * rank) for group in groups]
 
     def body(x_hbm, p_hbm, w_hbm, c_hbm, *refs):
         outs, (x_ref, p_ref, sems) = list(refs[: len(shapes)]), refs[len(shapes) :]
-        q_out, state_out, w_out, p_out = outs[:4]
-        rest = outs[4:]
+        q_out, state_out, w_out, p_out, w_next, p_next = outs[:6]
+        rest = outs[6:]
         moves = [(x_hbm, x_ref), (p_hbm.at[first], p_ref)]
         if leaf_core:
             moves.append((c_hbm.at[first], rest.pop(0)))
@@ -73,6 +73,7 @@
             for level, n in group:
                 moves.append((c_hbm.at[level, 0:n], out.at[start : start + n]))
                 start += n
+        moves += [(w_hbm.at[first - 1], w_next), (p_hbm.at[first - 2], p_next)]
         copies = [pltpu.make_async_copy(a, b, sems.at[at]) for at, (a, b) in enumerate(moves)]
         for copy in copies:
             copy.start()
@@ -84,7 +85,7 @@
         for copy in copies[2:]:
             copy.wait()
 
-    count = 4 + (1 if leaf_core else 0) + sum(len(group) for group in groups)
+    count = 6 + (1 if leaf_core else 0) + sum(len(group) for group in groups)
     return pl.pallas_call(
         body,
         in_specs=[IN_HBM] * 4,
@@ -95,7 +96,7 @@
             pltpu.VMEM((rows, rank), jnp.float32),
             pltpu.SemaphoreType.DMA((count,)),
         ],
-        compiler_params=pltpu.CompilerParams(vmem_limit_bytes=52 * 2**20),
+        compiler_params=pltpu.CompilerParams(vmem_limit_bytes=48 * 2**20),
         cost_estimate=pl.CostEstimate(
             flops=6 * rows * width * rank, bytes_accessed=2**22, transcendentals=0
         ),
@@ -155,7 +156,7 @@
     tails = [(level, rank >> bits[level]) for level in chain if bits[level] > 1]
     groups = [group for group in (heads, tails) if group]
     leaf_core = bits[first] == 0
-    value, state, top_corr, next_proj, *fetched = begin(
+    value, state, top_corr, next_proj, next_corr, after_proj, *fetched = begin(
         rhs, proj_bases, corr_bases, cores, first, leaf_core, groups
     )
 
@@ -229,8 +230,11 @@
     for level in reversed(range(1, first)):
         start = value
         held = solve(level, value, {})
-        projs, corrs = lax.optimization_barrier((proj_bases, corr_bases, start))[:2]
-        proj, corr = projs[level - 1], corrs[level]
+        if level == first - 1:
+            proj, corr = tie(after_proj, start), tie(next_corr, start)
+        else:
+            projs, corrs = lax.optimization_barrier((proj_bases, corr_bases, start))[:2]
+            proj, corr = projs[level - 1], corrs[level]
         ahead = chip_sum(project(proj, state))
         own = jnp.einsum("na,nb->ab", proj, corr, precision=HIGH)
         if heads and level == first - 1:

time: 72.6 us -> 77.5 us (1.067)
  local copies, waits for them, and re-layouts: 1.31 us -> 4.29 us
  waiting for transfers between devices: 27.4 us -> 28.8 us
  matrix products: 20.5 us -> 19.7 us
    unnamed x12 -> x18, local copies, waits for them, and re-layouts: 1.07 us -> 4.04 us
    dot_general x3, matrix products: 7.34 us -> 5.74 us  [on_device(): own = jnp.einsum('na,nb->ab', proj, corr, precision=HIGH)]
    ppermute x29, waiting for transfers between devices: 27.4 us -> 28.8 us  [exchange(): return lax.ppermute(value, 'leaf', pairs)]
    dot_general x4, matrix products: 5.46 us -> 6.34 us  [project(): return jnp.einsum('kn,nr->kr', state, basis, precision=HIGH)]
  transfers between devices with their start and end apart: 29 -> 29, of which waited for: 11 -> 10; matrix products, arithmetic and copies ran while one was open for 25% -> 19% of each run, Pallas kernels for 0% -> 0%
where the time goes in v4:
time: 77.5 us; the launch traced here: 77.1 us
  waiting for transfers between devices  28.8 us (37%)
  matrix products  19.7 us (25%)
  starting transfers between devices  19 us (25%)
  Pallas kernels  4.4 us (6%)
  local copies, waits for them, and re-layouts  4.29 us (6%)
    ppermute x29, waiting for transfers between devices, exchange(): return lax.ppermute(value, 'leaf', pairs)  28.8 us
    ppermute x29, starting transfers between devices, exchange(): return lax.ppermute(value, 'leaf', pairs)  19 us
    dot_general x4, matrix products, project(): return jnp.einsum('kn,nr->kr', state, basis, precision=HIGH)  6.34 us
    dot_general x3, matrix products, on_device(): own = jnp.einsum('na,nb->ab', proj, corr, precision=HIGH)  5.74 us
    unnamed x18, local copies, waits for them, and re-layouts  4.04 us
    dot_general x8, matrix products, times_transposed(): return jnp.einsum('kb,ab->ka', left, right, precision=HIGH)  3.93 us
    dot_general x4, matrix products, update(): return state - jnp.einsum('ka,na->kn', held, corr, precision=HIGH)  3.68 us
    pallas_call x1, Pallas kernels, begin(): pl.pallas_call(body, in_specs=[IN_HBM] * 4, out_specs=[IN_VMEM] * len(sha...  3.05 us
  transfers between devices with their start and end apart: 29, of which 10 were waited for; matrix products, arithmetic and copies ran while one was open for 19% of the time, Pallas kernels for 0%

profile of v4, /device:TPU:0, one launch (start us, length us, event | category | flops | bytes accessed | tf_op | source)
XLA Modules:
  0.0 77.1 jit_solution(10564154309361698160)
XLA Ops:
  0.0 3.0 %begin.1 = (f32[128,256]{1,0:T(8,128)S(1)}, f32[128,1024]{1,0:T(8,128)S(1)}, f32[1024,256]{1,0:T(8,128)S(1)}, f32[1024,256]{1,0:T(8,128)S(1)}, f32[1024,256]{1,0...) custom-call(f32[1024,128]{1,0:T(8,128)} %x_hbm.1, ...), custom_call_target="tpu_custom_call" | custom-call | flops 201326592 | bytes 4194304 | tf_op jit(solution)/shard_map/begin/pallas_call | solution.py:89
  3.1 1.0 %copy-done = f32[1024,256]{1,0:T(8,128)} copy-done((f32[1024,256]{1,0:T(8,128)}, f32[1024,256]{1,0:T(8,128)S(1)}, u32[]{:S(2)}) %copy-start) | copy-done | bytes 1048600
  4.0 0.8 %copy-done.1 = f32[128,1024]{1,0:T(8,128)} copy-done((f32[128,1024]{1,0:T(8,128)}, f32[128,1024]{1,0:T(8,128)S(1)}, u32[]{:S(2)}) %copy-start.1) | copy-done | bytes 524312
  4.8 0.8 %copy-done.2 = f32[256,512]{1,0:T(8,128)} copy-done((f32[256,512]{1,0:T(8,128)}, f32[256,512]{1,0:T(8,128)S(1)}, u32[]{:S(2)}) %copy-start.2) | copy-done | bytes 524312
  5.6 0.7 copy-done.3
  6.3 0.5 collective-permute-start
  6.8 1.1 %collective-permute-done = f32[128,256]{1,0:T(8,128)} collective-permute-done((f32[128,256]{1,0:T(8,128)S(1)}, f32[128,256]{1,0:T(8,128)}, u32[]{:S(2)}, u32[]{:S(2)}) %collective-permute-start) | collective-permute-done | bytes 131104 | tf_op jit(solution)/shard_map/ppermute | solution.py:16
  7.9 1.6 %fusion.21 = f32[128,256]{1,0:T(8,128)S(1)} fusion(f32[256,512]{1,0:T(8,128)} %copy-done.2, f32[128,256]{1,0:T(8,128)} %collective-permute-done, f32[128,256]{1,0:T(8,128)S(1)} %get-tuple-element.33, pred[]{:T(512)S(6)} %eq.12), kind=kOutput, calls=%fused_computation.33 | convolution fusion | flops 100925440 | bytes 917505 | tf_op jit(solution)/shard_map/kb,ab->ka/dot_general | solution.py:36
  9.5 1.7 %convolution_subtract_fusion.3 = f32[128,1024]{1,0:T(8,128)S(1)} fusion(f32[128,1024]{1,0:T(8,128)} %copy-done.1, f32[128,256]{1,0:T(8,128)S(1)} %fusion.21, f32[1024,256]{1,0:T(8,128)S(1)} %get-tuple-element.35), kind=kOutput, calls=%fused_computation.3 | convolution fusion | flops 201457664 | bytes 2228224 | tf_op jit(solution)/shard_map/ka,na->kn/dot_general | solution.py:217
  11.2 0.8 %copy-done.5 = f32[128,1024]{1,0:T(8,128)} copy-done((f32[128,1024]{1,0:T(8,128)}, f32[128,1024]{1,0:T(8,128)S(1)}, u32[]{:S(2)}) %copy-start.5) | copy-done | bytes 524312
  12.0 1.6 %fusion.107 = f32[128,256]{1,0:T(8,128)S(1)} fusion(f32[128,1024]{1,0:T(8,128)S(1)} %convolution_subtract_fusion.3, f32[1024,256]{1,0:T(8,128)} %copy-done), kind=kOutput, calls=%fused_computation.131 | convolution fusion | flops 201326592 | bytes 1703936 | tf_op jit(solution)/shard_map/kn,nr->kr/dot_general | solution.py:32
  13.6 0.4 collective-permute-start.1
  14.1 2.6 %collective-permute-start.9 = (f32[1,112,512]{2,1,0:T(8,128)}, f32[1,112,512]{2,1,0:T(8,128)S(1)}, u32[]{:S(2)}, u32[]{:S(2)}) collective-permute-start(f32[1,112,512]{2,1,0:T(8,128)} %bitcast.58), channel_id=1, source_target_pairs={{0,2},{1,3},{2,0},{3,1},{4,6},{5,7},{6,4},{7,5},{8,10},{9,11},{10,... | collective-permute-start | bytes 688136 | tf_op jit(solution)/shard_map/ppermute | solution.py:16
  16.7 0.9 %collective-permute-start.2 = (f32[64,256]{1,0:T(8,128)S(1)}, f32[64,256]{1,0:T(8,128)S(1)}, u32[]{:S(2)}, u32[]{:S(2)}) collective-permute-start(f32[64,256]{1,0:T(8,128)S(1)} %select_add_fusion), channel_id=1, source_target_pairs={{0,3},{1,2},{2,1},{3,0},{4,7},{5,6},{6,5},{7,4},{8,11},{9,10},{10,... | collective-permute-start | bytes 196616 | tf_op jit(solution)/shard_map/ppermute | solution.py:16
  17.6 1.4 %fusion.108 = f32[128,256]{1,0:T(8,128)S(1)} fusion(f32[128,1024]{1,0:T(8,128)} %copy-done.5, f32[1024,256]{1,0:T(8,128)S(1)} %get-tuple-element.42), kind=kOutput, calls=%fused_computation.132 | convolution fusion | flops 201326592 | bytes 1703936 | tf_op jit(solution)/shard_map/kn,nr->kr/dot_general | solution.py:32
  19.1 1.0 %fusion.109 = f32[256,256]{1,0:T(8,128)S(1)} fusion(f32[1024,256]{1,0:T(8,128)S(1)} %get-tuple-element.42, f32[1024,256]{1,0:T(8,128)S(1)} %get-tuple-element.40), kind=kOutput, calls=%fused_computation.133 | convolution fusion | flops 402653184 | bytes 2359296 | tf_op jit(solution)/shard_map/na,nb->ab/dot_general | solution.py:239
  20.1 0.4 collective-permute-start.6
  20.5 0.2 collective-permute-start.3
  20.7 0.4 collective-permute-start.5
  21.1 2.2 %collective-permute-done.9 = f32[1,112,512]{2,1,0:T(8,128)S(1)} collective-permute-done((f32[1,112,512]{2,1,0:T(8,128)}, f32[1,112,512]{2,1,0:T(8,128)S(1)}, u32[]{:S(2)}, u32[]{:S(2)}) %collective-permute-start.9) | collective-permute-done | bytes 229408 | tf_op jit(solution)/shard_map/ppermute | solution.py:16
  23.5 2.1 %collective-permute-start.17 = (f32[2,48,512]{2,1,0:T(8,128)S(1)}, f32[2,48,512]{2,1,0:T(8,128)S(1)}, u32[]{:S(2)}, u32[]{:S(2)}) collective-permute-start(f32[2,48,512]{2,1,0:T(8,128)S(1)} %slice.87), channel_id=1, source_target_pairs={{0,4},{1,5},{2,6},{3,7},{4,0},{5,1},{6,2},{7,3},{8,12},{9,13},{10,... | collective-permute-start | bytes 589832 | tf_op jit(solution)/shard_map/ppermute | solution.py:16
  25.7 0.4 fusion.35
  26.1 0.2 collective-permute-start.4
  26.3 0.3 add_subtract_fusion.2
  26.6 1.5 %collective-permute-start.7 = (f32[64,256]{1,0:T(8,128)S(1)}, f32[64,256]{1,0:T(8,128)S(1)}, u32[]{:S(2)}, u32[]{:S(2)}) collective-permute-start(f32[64,256]{1,0:T(8,128)S(1)} %add_subtract_fusion.2), channel_id=1, source_target_pairs={{0,3},{1,2},{2,1},{3,0},{4,7},{5,6},{6,5},{7,4},{8,11},{9,10},{10,... | collective-permute-start | bytes 196616 | tf_op jit(solution)/shard_map/ppermute | solution.py:16
  28.1 2.5 %fusion.6 = f32[256,256]{1,0:T(8,128)S(1)} fusion(f32[5,1024,256]{2,1,0:T(8,128)} %p_hbm.1, f32[5,1024,256]{2,1,0:T(8,128)} %w_hbm.1), kind=kOutput, calls=%fused_computation.10 | convolution fusion | flops 402653184 | bytes 2359296 | tf_op jit(solution)/shard_map/na,nb->ab/dot_general | solution.py:239
  30.6 0.2 collective-permute-start.13
  31.0 0.7 convolution_subtract_fusion.2
  31.6 1.6 %fusion.8 = f32[128,256]{1,0:T(8,128)S(1)} fusion(f32[128,1024]{1,0:T(8,128)S(1)} %convolution_subtract_fusion.2, f32[5,1024,256]{2,1,0:T(8,128)} %p_hbm.1), kind=kOutput, calls=%fused_computation.12 | convolution fusion | flops 201326592 | bytes 1703936 | tf_op jit(solution)/shard_map/kn,nr->kr/dot_general | solution.py:32
  33.3 0.5 collective-permute-start.8
  33.9 3.4 %collective-permute-done.8 = f32[64,256]{1,0:T(8,128)S(1)} collective-permute-done((f32[64,256]{1,0:T(8,128)S(1)}, f32[64,256]{1,0:T(8,128)S(1)}, u32[]{:S(2)}, u32[]{:S(2)}) %collective-permute-start.8) | collective-permute-done | bytes 65568 | tf_op jit(solution)/shard_map/ppermute | solution.py:16
  37.3 0.4 fusion.48
  37.7 0.3 collective-permute-start.11
  38.1 0.3 collective-permute-start.12
  38.4 0.3 collective-permute-start.18
  38.7 1.6 %collective-permute-start.26 = (f32[4,16,512]{2,1,0:T(8,128)S(1)}, f32[4,16,512]{2,1,0:T(8,128)S(1)}, u32[]{:S(2)}, u32[]{:S(2)}) collective-permute-start(f32[4,16,512]{2,1,0:T(8,128)S(1)} %slice.91), channel_id=1, source_target_pairs={{0,8},{1,9},{2,10},{3,11},{4,12},{5,13},{6,14},{7,15},{8,0},{9,1},... | collective-permute-start | bytes 393224 | tf_op jit(solution)/shard_map/ppermute | solution.py:16
  40.3 0.7 convolution_subtract_fusion.1
  41.0 0.3 add_subtract_fusion.1
  41.3 0.1 collective-permute-start.14
  41.4 2.2 %fusion.1 = f32[256,256]{1,0:T(8,128)S(1)} fusion(f32[5,1024,256]{2,1,0:T(8,128)S(1)} %bitcast.61, f32[5,1024,256]{2,1,0:T(8,128)} %p_hbm.1), kind=kOutput, calls=%fused_computation.5 | convolution fusion | flops 402653184 | bytes 2359296 | tf_op jit(solution)/shard_map/na,nb->ab/dot_general | solution.py:239
  43.6 0.6 collective-permute-start.21
  44.3 1.6 %fusion.4 = f32[128,256]{1,0:T(8,128)S(1)} fusion(f32[128,1024]{1,0:T(8,128)S(1)} %convolution_subtract_fusion.1, f32[5,1024,256]{2,1,0:T(8,128)} %p_hbm.1), kind=kOutput, calls=%fused_computation.8 | convolution fusion | flops 201326592 | bytes 1703936 | tf_op jit(solution)/shard_map/kn,nr->kr/dot_general | solution.py:32
  45.9 0.2 collective-permute-start.15
  46.2 0.6 collective-permute-start.20
  46.7 3.5 %collective-permute-done.15 = f32[64,256]{1,0:T(8,128)S(1)} collective-permute-done((f32[64,256]{1,0:T(8,128)S(1)}, f32[64,256]{1,0:T(8,128)S(1)}, u32[]{:S(2)}, u32[]{:S(2)}) %collective-permute-start.15) | collective-permute-done | bytes 65568 | tf_op jit(solution)/shard_map/ppermute | solution.py:16
  50.2 0.1 collective-permute-start.16
  50.5 3.9 %collective-permute-done.16 = f32[64,256]{1,0:T(8,128)S(1)} collective-permute-done((f32[64,256]{1,0:T(8,128)S(1)}, f32[64,256]{1,0:T(8,128)S(1)}, u32[]{:S(2)}, u32[]{:S(2)}) %collective-permute-start.16) | collective-permute-done | bytes 65568 | tf_op jit(solution)/shard_map/ppermute | solution.py:16
  54.4 0.4 fusion.61
  54.8 0.3 add_subtract_fusion
  55.1 1.3 %collective-permute-start.22 = (f32[64,256]{1,0:T(8,128)S(1)}, f32[64,256]{1,0:T(8,128)S(1)}, u32[]{:S(2)}, u32[]{:S(2)}) collective-permute-start(f32[64,256]{1,0:T(8,128)S(1)} %add_subtract_fusion), channel_id=1, source_target_pairs={{0,3},{1,2},{2,1},{3,0},{4,7},{5,6},{6,5},{7,4},{8,11},{9,10},{10,... | collective-permute-start | bytes 196616 | tf_op jit(solution)/shard_map/ppermute | solution.py:16
  56.4 0.5 collective-permute-start.27
  56.8 0.1 collective-permute-start.19
  56.9 2.3 %collective-permute-done.22 = f32[64,256]{1,0:T(8,128)S(1)} collective-permute-done((f32[64,256]{1,0:T(8,128)S(1)}, f32[64,256]{1,0:T(8,128)S(1)}, u32[]{:S(2)}, u32[]{:S(2)}) %collective-permute-start.22) | collective-permute-done | bytes 65568 | tf_op jit(solution)/shard_map/ppermute | solution.py:16
  59.2 0.3 collective-permute-start.23
  59.6 3.8 %collective-permute-done.23 = f32[64,256]{1,0:T(8,128)S(1)} collective-permute-done((f32[64,256]{1,0:T(8,128)S(1)}, f32[64,256]{1,0:T(8,128)S(1)}, u32[]{:S(2)}, u32[]{:S(2)}) %collective-permute-start.23) | collective-permute-done | bytes 65568 | tf_op jit(solution)/shard_map/ppermute | solution.py:16
  63.4 0.1 collective-permute-start.24
  63.5 0.7 convolution_subtract_fusion.x_ref
  64.2 3.4 %collective-permute-done.24 = f32[64,256]{1,0:T(8,128)S(1)} collective-permute-done((f32[64,256]{1,0:T(8,128)S(1)}, f32[64,256]{1,0:T(8,128)S(1)}, u32[]{:S(2)}, u32[]{:S(2)}) %collective-permute-start.24) | collective-permute-done | bytes 65568 | tf_op jit(solution)/shard_map/ppermute | solution.py:16
  67.6 2.4 %collective-permute-start.25 = (f32[64,256]{1,0:T(8,128)S(1)}, f32[64,256]{1,0:T(8,128)S(1)}, u32[]{:S(2)}, u32[]{:S(2)}) collective-permute-start(f32[64,256]{1,0:T(8,128)S(1)} %add.51), channel_id=1, source_target_pairs={{0,17},{1,16},{2,19},{3,18},{4,21},{5,20},{6,23},{7,22},{8,25},{9,... | collective-permute-start | bytes 196616 | tf_op jit(solution)/shard_map/ppermute | solution.py:16
  70.1 4.0 %collective-permute-done.25 = f32[64,256]{1,0:T(8,128)S(1)} collective-permute-done((f32[64,256]{1,0:T(8,128)S(1)}, f32[64,256]{1,0:T(8,128)S(1)}, u32[]{:S(2)}, u32[]{:S(2)}) %collective-permute-start.25) | collective-permute-done | bytes 65568 | tf_op jit(solution)/shard_map/ppermute | solution.py:16
  74.0 0.4 fusion.74
  74.4 0.2 collective-permute-start.28
  74.6 1.1 %collective-permute-done.28 = f32[64,256]{1,0:T(8,128)S(1)} collective-permute-done((f32[64,256]{1,0:T(8,128)S(1)}, f32[64,256]{1,0:T(8,128)S(1)}, u32[]{:S(2)}, u32[]{:S(2)}) %collective-permute-start.28) | collective-permute-done | bytes 65568 | tf_op jit(solution)/shard_map/ppermute | solution.py:16
  75.7 1.4 %finish.1 = f32[1024,128]{1,0:T(8,128)} custom-call(f32[128,1024]{1,0:T(8,128)S(1)} %convolution_subtract_fusion.x_ref, f32[1024,256]{1,0:T(8,128)S(1)} %slice_bitcast_fusion.w_ref, f32[128,256]{1,0:T(8,128)S(1)} %maximum_select_fusion.18.t_ref), custom_call_target="tpu_custom_call" | custom-call | flops 201326592 | bytes 2097152 | tf_op jit(solution)/shard_map/finish/pallas_call | solution.py:113
  (61 shorter events, 0.8 us)
Async XLA Ops:
  3.1 1.0 %copy-start = (f32[1024,256]{1,0:T(8,128)}, f32[1024,256]{1,0:T(8,128)S(1)}, u32[]{:S(2)}) copy-start(f32[1024,256]{1,0:T(8,128)S(1)} %get-tuple-element.36) | copy-start | bytes 3145732
  4.0 0.8 %copy-start.1 = (f32[128,1024]{1,0:T(8,128)}, f32[128,1024]{1,0:T(8,128)S(1)}, u32[]{:S(2)}) copy-start(f32[128,1024]{1,0:T(8,128)S(1)} %get-tuple-element.32) | copy-start | bytes 1572868
  4.8 0.8 %copy-start.2 = (f32[256,512]{1,0:T(8,128)}, f32[256,512]{1,0:T(8,128)S(1)}, u32[]{:S(2)}) copy-start(f32[256,512]{1,0:T(8,128)S(1)} %get-tuple-element.34) | copy-start | bytes 1572868
  5.6 0.7 copy-start.3
  6.3 1.6 %collective-permute-start = (f32[128,256]{1,0:T(8,128)S(1)}, f32[128,256]{1,0:T(8,128)}, u32[]{:S(2)}, u32[]{:S(2)}) collective-permute-start(f32[128,256]{1,0:T(8,128)S(1)} %get-tuple-element.33), channel_id=1, source_target_pairs={{0,1},{1,0},{2,3},{3,2},{4,5},{5,4},{6,7},{7,6},{8,9},{9,8},{10,11... | collective-permute-start | bytes 393224 | tf_op jit(solution)/shard_map/ppermute | solution.py:16
  11.2 0.8 %copy-start.5 = (f32[128,1024]{1,0:T(8,128)}, f32[128,1024]{1,0:T(8,128)S(1)}, u32[]{:S(2)}) copy-start(f32[128,1024]{1,0:T(8,128)S(1)} %convolution_subtract_fusion.3) | copy-start | bytes 1572868
  11.2 12.2 %copy-start.4 = (f32[112,512]{1,0:T(8,128)S(1)}, f32[112,512]{1,0:T(8,128)}, u32[]{:S(2)}) copy-start(f32[112,512]{1,0:T(8,128)} %copy-done.3) | copy-start | bytes 688132
  13.6 3.1 %collective-permute-start.1 = (f32[64,256]{1,0:T(8,128)S(1)}, f32[64,256]{1,0:T(8,128)S(1)}, u32[]{:S(2)}, u32[]{:S(2)}) collective-permute-start(f32[64,256]{1,0:T(8,128)S(1)} %slice_select_fusion.3), channel_id=1, source_target_pairs={{0,1},{1,0},{2,3},{3,2},{4,5},{5,4},{6,7},{7,6},{8,9},{9,8},{10,11... | collective-permute-start | bytes 196616 | tf_op jit(solution)/shard_map/ppermute | solution.py:16
  14.1 9.3 %collective-permute-start.9 = (f32[1,112,512]{2,1,0:T(8,128)}, f32[1,112,512]{2,1,0:T(8,128)S(1)}, u32[]{:S(2)}, u32[]{:S(2)}) collective-permute-start(f32[1,112,512]{2,1,0:T(8,128)} %bitcast.58), channel_id=1, source_target_pairs={{0,2},{1,3},{2,0},{3,1},{4,6},{5,7},{6,4},{7,5},{8,10},{9,11},{10,... | collective-permute-start | bytes 688136 | tf_op jit(solution)/shard_map/ppermute | solution.py:16
  16.7 8.9 %collective-permute-start.2 = (f32[64,256]{1,0:T(8,128)S(1)}, f32[64,256]{1,0:T(8,128)S(1)}, u32[]{:S(2)}, u32[]{:S(2)}) collective-permute-start(f32[64,256]{1,0:T(8,128)S(1)} %select_add_fusion), channel_id=1, source_target_pairs={{0,3},{1,2},{2,1},{3,0},{4,7},{5,6},{6,5},{7,4},{8,11},{9,10},{10,... | collective-permute-start | bytes 196616 | tf_op jit(solution)/shard_map/ppermute | solution.py:16
  19.1 11.9 %copy-start.6 = (f32[128,1024]{1,0:T(8,128)S(1)}, f32[128,1024]{1,0:T(8,128)}, u32[]{:S(2)}) copy-start(f32[128,1024]{1,0:T(8,128)} %copy-done.5) | copy-start | bytes 1572868
  20.1 6.2 %collective-permute-start.6 = (f32[256,256]{1,0:T(8,128)S(1)}, f32[256,256]{1,0:T(8,128)S(1)}, u32[]{:S(2)}, u32[]{:S(2)}) collective-permute-start(f32[256,256]{1,0:T(8,128)S(1)} %fusion.109), channel_id=1, source_target_pairs={{0,1},{1,0},{2,3},{3,2},{4,5},{5,4},{6,7},{7,6},{8,9},{9,8},{10,11... | collective-permute-start | bytes 786440 | tf_op jit(solution)/shard_map/ppermute | solution.py:16
  20.5 3.0 %collective-permute-start.3 = (f32[1,128,512]{2,1,0:T(8,128)S(1)}, f32[1,128,512]{2,1,0:T(8,128)S(1)}, u32[]{:S(2)}, u32[]{:S(2)}) collective-permute-start(f32[1,128,512]{2,1,0:T(8,128)S(1)} %bitcast.56), channel_id=1, source_target_pairs={{0,1},{1,0},{2,3},{3,2},{4,5},{5,4},{6,7},{7,6},{8,9},{9,8},{10,11... | collective-permute-start | bytes 786440 | tf_op jit(solution)/shard_map/ppermute | solution.py:16
  20.7 5.6 %collective-permute-start.5 = (f32[64,256]{1,0:T(8,128)S(1)}, f32[64,256]{1,0:T(8,128)S(1)}, u32[]{:S(2)}, u32[]{:S(2)}) collective-permute-start(f32[64,256]{1,0:T(8,128)S(1)} %slice_select_fusion.2), channel_id=1, source_target_pairs={{0,1},{1,0},{2,3},{3,2},{4,5},{5,4},{6,7},{7,6},{8,9},{9,8},{10,11... | collective-permute-start | bytes 196616 | tf_op jit(solution)/shard_map/ppermute | solution.py:16
  23.4 7.4 %collective-permute-start.10 = (f32[2,64,512]{2,1,0:T(8,128)S(1)}, f32[2,64,512]{2,1,0:T(8,128)S(1)}, u32[]{:S(2)}, u32[]{:S(2)}) collective-permute-start(f32[2,64,512]{2,1,0:T(8,128)S(1)} %slice.84), channel_id=1, source_target_pairs={{0,1},{1,0},{2,3},{3,2},{4,5},{5,4},{6,7},{7,6},{8,9},{9,8},{10,11... | collective-permute-start | bytes 786440 | tf_op jit(solution)/shard_map/ppermute | solution.py:16
  23.5 10.3 %collective-permute-start.17 = (f32[2,48,512]{2,1,0:T(8,128)S(1)}, f32[2,48,512]{2,1,0:T(8,128)S(1)}, u32[]{:S(2)}, u32[]{:S(2)}) collective-permute-start(f32[2,48,512]{2,1,0:T(8,128)S(1)} %slice.87), channel_id=1, source_target_pairs={{0,4},{1,5},{2,6},{3,7},{4,0},{5,1},{6,2},{7,3},{8,12},{9,13},{10,... | collective-permute-start | bytes 589832 | tf_op jit(solution)/shard_map/ppermute | solution.py:16
  25.6 14.7 %slice-start = ((s8[5242880]{0:T(1024)(128)(4,1)}), s8[4194304]{0:T(1024)(128)(4,1)S(1)}, s32[]{:S(2)}) async-start(s8[5242880]{0:T(1024)(128)(4,1)} %bitcast.60), calls=%async_computation | async-start | bytes 8388608
  26.1 4.9 %collective-permute-start.4 = (f32[64,256]{1,0:T(8,128)S(1)}, f32[64,256]{1,0:T(8,128)S(1)}, u32[]{:S(2)}, u32[]{:S(2)}) collective-permute-start(f32[64,256]{1,0:T(8,128)S(1)} %fusion.35), channel_id=1, source_target_pairs={{0,1},{1,0},{2,3},{3,2},{4,5},{5,4},{6,7},{7,6},{8,9},{9,8},{10,11... | collective-permute-start | bytes 196616 | tf_op jit(solution)/shard_map/ppermute | solution.py:16
  26.6 6.7 %collective-permute-start.7 = (f32[64,256]{1,0:T(8,128)S(1)}, f32[64,256]{1,0:T(8,128)S(1)}, u32[]{:S(2)}, u32[]{:S(2)}) collective-permute-start(f32[64,256]{1,0:T(8,128)S(1)} %add_subtract_fusion.2), channel_id=1, source_target_pairs={{0,3},{1,2},{2,1},{3,0},{4,7},{5,6},{6,5},{7,4},{8,11},{9,10},{10,... | collective-permute-start | bytes 196616 | tf_op jit(solution)/shard_map/ppermute | solution.py:16
  30.6 10.4 %collective-permute-start.13 = (f32[256,256]{1,0:T(8,128)S(1)}, f32[256,256]{1,0:T(8,128)S(1)}, u32[]{:S(2)}, u32[]{:S(2)}) collective-permute-start(f32[256,256]{1,0:T(8,128)S(1)} %fusion.6), channel_id=1, source_target_pairs={{0,1},{1,0},{2,3},{3,2},{4,5},{5,4},{6,7},{7,6},{8,9},{9,8},{10,11... | collective-permute-start | bytes 786440 | tf_op jit(solution)/shard_map/ppermute | solution.py:16
  30.9 9.4 %slice-start.1 = ((s8[5242880]{0:T(1024)(128)(4,1)}), s8[1048576]{0:T(1024)(128)(4,1)S(1)}, s32[]{:S(2)}) async-start(s8[5242880]{0:T(1024)(128)(4,1)} %bitcast.60), calls=%async_computation.1 | async-start | bytes 2097152
  33.3 4.0 %collective-permute-start.8 = (f32[64,256]{1,0:T(8,128)S(1)}, f32[64,256]{1,0:T(8,128)S(1)}, u32[]{:S(2)}, u32[]{:S(2)}) collective-permute-start(f32[64,256]{1,0:T(8,128)S(1)} %add.42), channel_id=1, source_target_pairs={{0,5},{1,4},{2,7},{3,6},{4,1},{5,0},{6,3},{7,2},{8,13},{9,12},{10,... | collective-permute-start | bytes 196616 | tf_op jit(solution)/shard_map/ppermute | solution.py:16
  37.7 2.6 %collective-permute-start.11 = (f32[64,256]{1,0:T(8,128)S(1)}, f32[64,256]{1,0:T(8,128)S(1)}, u32[]{:S(2)}, u32[]{:S(2)}) collective-permute-start(f32[64,256]{1,0:T(8,128)S(1)} %fusion.48), channel_id=1, source_target_pairs={{0,1},{1,0},{2,3},{3,2},{4,5},{5,4},{6,7},{7,6},{8,9},{9,8},{10,11... | collective-permute-start | bytes 196616 | tf_op jit(solution)/shard_map/ppermute | solution.py:16
  38.1 2.8 %collective-permute-start.12 = (f32[64,256]{1,0:T(8,128)S(1)}, f32[64,256]{1,0:T(8,128)S(1)}, u32[]{:S(2)}, u32[]{:S(2)}) collective-permute-start(f32[64,256]{1,0:T(8,128)S(1)} %slice_select_fusion.1), channel_id=1, source_target_pairs={{0,1},{1,0},{2,3},{3,2},{4,5},{5,4},{6,7},{7,6},{8,9},{9,8},{10,11... | collective-permute-start | bytes 196616 | tf_op jit(solution)/shard_map/ppermute | solution.py:16
  38.4 12.0 %collective-permute-start.18 = (f32[4,32,512]{2,1,0:T(8,128)S(1)}, f32[4,32,512]{2,1,0:T(8,128)S(1)}, u32[]{:S(2)}, u32[]{:S(2)}) collective-permute-start(f32[4,32,512]{2,1,0:T(8,128)S(1)} %slice.88), channel_id=1, source_target_pairs={{0,1},{1,0},{2,3},{3,2},{4,5},{5,4},{6,7},{7,6},{8,9},{9,8},{10,11... | collective-permute-start | bytes 786440 | tf_op jit(solution)/shard_map/ppermute | solution.py:16
  38.7 11.8 %collective-permute-start.26 = (f32[4,16,512]{2,1,0:T(8,128)S(1)}, f32[4,16,512]{2,1,0:T(8,128)S(1)}, u32[]{:S(2)}, u32[]{:S(2)}) collective-permute-start(f32[4,16,512]{2,1,0:T(8,128)S(1)} %slice.91), channel_id=1, source_target_pairs={{0,8},{1,9},{2,10},{3,11},{4,12},{5,13},{6,14},{7,15},{8,0},{9,1},... | collective-permute-start | bytes 393224 | tf_op jit(solution)/shard_map/ppermute | solution.py:16
  41.3 4.6 %collective-permute-start.14 = (f32[64,256]{1,0:T(8,128)S(1)}, f32[64,256]{1,0:T(8,128)S(1)}, u32[]{:S(2)}, u32[]{:S(2)}) collective-permute-start(f32[64,256]{1,0:T(8,128)S(1)} %add_subtract_fusion.1), channel_id=1, source_target_pairs={{0,3},{1,2},{2,1},{3,0},{4,7},{5,6},{6,5},{7,4},{8,11},{9,10},{10,... | collective-permute-start | bytes 196616 | tf_op jit(solution)/shard_map/ppermute | solution.py:16
  43.6 11.1 %collective-permute-start.21 = (f32[256,256]{1,0:T(8,128)S(1)}, f32[256,256]{1,0:T(8,128)S(1)}, u32[]{:S(2)}, u32[]{:S(2)}) collective-permute-start(f32[256,256]{1,0:T(8,128)S(1)} %fusion.1), channel_id=1, source_target_pairs={{0,1},{1,0},{2,3},{3,2},{4,5},{5,4},{6,7},{7,6},{8,9},{9,8},{10,11... | collective-permute-start | bytes 786440 | tf_op jit(solution)/shard_map/ppermute | solution.py:16
  45.9 4.3 %collective-permute-start.15 = (f32[64,256]{1,0:T(8,128)S(1)}, f32[64,256]{1,0:T(8,128)S(1)}, u32[]{:S(2)}, u32[]{:S(2)}) collective-permute-start(f32[64,256]{1,0:T(8,128)S(1)} %add.45), channel_id=1, source_target_pairs={{0,5},{1,4},{2,7},{3,6},{4,1},{5,0},{6,3},{7,2},{8,13},{9,12},{10,... | collective-permute-start | bytes 196616 | tf_op jit(solution)/shard_map/ppermute | solution.py:16
  46.2 8.6 %collective-permute-start.20 = (f32[64,256]{1,0:T(8,128)S(1)}, f32[64,256]{1,0:T(8,128)S(1)}, u32[]{:S(2)}, u32[]{:S(2)}) collective-permute-start(f32[64,256]{1,0:T(8,128)S(1)} %slice_select_fusion), channel_id=1, source_target_pairs={{0,1},{1,0},{2,3},{3,2},{4,5},{5,4},{6,7},{7,6},{8,9},{9,8},{10,11... | collective-permute-start | bytes 196616 | tf_op jit(solution)/shard_map/ppermute | solution.py:16
  50.2 4.2 %collective-permute-start.16 = (f32[64,256]{1,0:T(8,128)S(1)}, f32[64,256]{1,0:T(8,128)S(1)}, u32[]{:S(2)}, u32[]{:S(2)}) collective-permute-start(f32[64,256]{1,0:T(8,128)S(1)} %add.46), channel_id=1, source_target_pairs={{0,9},{1,8},{2,11},{3,10},{4,13},{5,12},{6,15},{7,14},{8,1},{9,0},... | collective-permute-start | bytes 196616 | tf_op jit(solution)/shard_map/ppermute | solution.py:16
  55.1 4.2 %collective-permute-start.22 = (f32[64,256]{1,0:T(8,128)S(1)}, f32[64,256]{1,0:T(8,128)S(1)}, u32[]{:S(2)}, u32[]{:S(2)}) collective-permute-start(f32[64,256]{1,0:T(8,128)S(1)} %add_subtract_fusion), channel_id=1, source_target_pairs={{0,3},{1,2},{2,1},{3,0},{4,7},{5,6},{6,5},{7,4},{8,11},{9,10},{10,... | collective-permute-start | bytes 196616 | tf_op jit(solution)/shard_map/ppermute | solution.py:16
  56.4 13.6 %collective-permute-start.27 = (f32[8,16,512]{2,1,0:T(8,128)S(1)}, f32[8,16,512]{2,1,0:T(8,128)S(1)}, u32[]{:S(2)}, u32[]{:S(2)}) collective-permute-start(f32[8,16,512]{2,1,0:T(8,128)S(1)} %maximum_select_fusion.7), channel_id=1, source_target_pairs={{0,1},{1,0},{2,3},{3,2},{4,5},{5,4},{6,7},{7,6},{8,9},{9,8},{10,11... | collective-permute-start | bytes 786440 | tf_op jit(solution)/shard_map/ppermute | solution.py:16
  56.8 6.7 %collective-permute-start.19 = (f32[64,256]{1,0:T(8,128)S(1)}, f32[64,256]{1,0:T(8,128)S(1)}, u32[]{:S(2)}, u32[]{:S(2)}) collective-permute-start(f32[64,256]{1,0:T(8,128)S(1)} %fusion.61), channel_id=1, source_target_pairs={{0,1},{1,0},{2,3},{3,2},{4,5},{5,4},{6,7},{7,6},{8,9},{9,8},{10,11... | collective-permute-start | bytes 196616 | tf_op jit(solution)/shard_map/ppermute | solution.py:16
  59.2 4.2 %collective-permute-start.23 = (f32[64,256]{1,0:T(8,128)S(1)}, f32[64,256]{1,0:T(8,128)S(1)}, u32[]{:S(2)}, u32[]{:S(2)}) collective-permute-start(f32[64,256]{1,0:T(8,128)S(1)} %add.49), channel_id=1, source_target_pairs={{0,5},{1,4},{2,7},{3,6},{4,1},{5,0},{6,3},{7,2},{8,13},{9,12},{10,... | collective-permute-start | bytes 196616 | tf_op jit(solution)/shard_map/ppermute | solution.py:16
  63.4 4.2 %collective-permute-start.24 = (f32[64,256]{1,0:T(8,128)S(1)}, f32[64,256]{1,0:T(8,128)S(1)}, u32[]{:S(2)}, u32[]{:S(2)}) collective-permute-start(f32[64,256]{1,0:T(8,128)S(1)} %add.50), channel_id=1, source_target_pairs={{0,9},{1,8},{2,11},{3,10},{4,13},{5,12},{6,15},{7,14},{8,1},{9,0},... | collective-permute-start | bytes 196616 | tf_op jit(solution)/shard_map/ppermute | solution.py:16
  67.6 6.4 %collective-permute-start.25 = (f32[64,256]{1,0:T(8,128)S(1)}, f32[64,256]{1,0:T(8,128)S(1)}, u32[]{:S(2)}, u32[]{:S(2)}) collective-permute-start(f32[64,256]{1,0:T(8,128)S(1)} %add.51), channel_id=1, source_target_pairs={{0,17},{1,16},{2,19},{3,18},{4,21},{5,20},{6,23},{7,22},{8,25},{9,... | collective-permute-start | bytes 196616 | tf_op jit(solution)/shard_map/ppermute | solution.py:16
  74.4 1.3 %collective-permute-start.28 = (f32[64,256]{1,0:T(8,128)S(1)}, f32[64,256]{1,0:T(8,128)S(1)}, u32[]{:S(2)}, u32[]{:S(2)}) collective-permute-start(f32[64,256]{1,0:T(8,128)S(1)} %fusion.74), channel_id=1, source_target_pairs={{0,1},{1,0},{2,3},{3,2},{4,5},{5,4},{6,7},{7,6},{8,9},{9,8},{10,11... | collective-permute-start | bytes 196616 | tf_op jit(solution)/shard_map/ppermute | solution.py:16

commit v5 on v2

--- a/solution.py
+++ b/solution.py
@@ -7,6 +7,7 @@
 
 LEVELS = 5
 HIGH = lax.Precision.HIGH
+MIB = 2**20
 IN_HBM = pl.BlockSpec(memory_space=pltpu.HBM)
 IN_VMEM = pl.BlockSpec(memory_space=pltpu.VMEM)
 
@@ -95,7 +96,7 @@
             pltpu.VMEM((rows, rank), jnp.float32),
             pltpu.SemaphoreType.DMA((count,)),
         ],
-        compiler_params=pltpu.CompilerParams(vmem_limit_bytes=52 * 2**20),
+        compiler_params=pltpu.CompilerParams(vmem_limit_bytes=52 * MIB),
         cost_estimate=pl.CostEstimate(
             flops=6 * rows * width * rank, bytes_accessed=2**22, transcendentals=0
         ),
@@ -103,6 +104,36 @@
     )(rhs, proj_bases, corr_bases, cores)
 
 
+def fetch(proj_bases, corr_bases, projs, corrs, after):
+    rows, rank = corr_bases.shape[1:]
+    count = len(projs) + len(corrs)
+
+    def body(p_hbm, w_hbm, _, *refs):
+        sources = [p_hbm.at[level] for level in projs] + [w_hbm.at[level] for level in corrs]
+        sems = refs[-1]
+        copies = [
+            pltpu.make_async_copy(source, out, sems.at[at])
+            for at, (source, out) in enumerate(zip(sources, refs[:-1]))
+        ]
+        for copy in copies:
+            copy.start()
+        for copy in copies:
+            copy.wait()
+
+    return pl.pallas_call(
+        body,
+        in_specs=[IN_HBM, IN_HBM, pl.BlockSpec(memory_space=pl.ANY)],
+        out_specs=[IN_VMEM] * count,
+        out_shape=[pltpu.VMEM((rows, rank), jnp.float32)] * count,
+        scratch_shapes=[pltpu.SemaphoreType.DMA((count,))],
+        compiler_params=pltpu.CompilerParams(vmem_limit_bytes=(54 - count) * MIB),
+        cost_estimate=pl.CostEstimate(
+            flops=0, bytes_accessed=8 * count * rows * rank, transcendentals=0
+        ),
+        name="fetch",
+    )(proj_bases, corr_bases, after)
+
+
 def finish(state, corr, held):
     width, rows = state.shape
 
@@ -114,7 +145,7 @@
         in_specs=[IN_VMEM] * 3,
         out_specs=IN_VMEM,
         out_shape=jax.ShapeDtypeStruct((rows, width), jnp.float32),
-        compiler_params=pltpu.CompilerParams(vmem_limit_bytes=16 * 2**20),
+        compiler_params=pltpu.CompilerParams(vmem_limit_bytes=16 * MIB),
         cost_estimate=pl.CostEstimate(
             flops=6 * rows * width * corr.shape[1], bytes_accessed=2**21, transcendentals=0
         ),
@@ -158,6 +189,7 @@
     value, state, top_corr, next_proj, *fetched = begin(
         rhs, proj_bases, corr_bases, cores, first, leaf_core, groups
     )
+    proj, corr = fetch(proj_bases, corr_bases, [first - 2], [first - 1], value)
 
     table = {}
     if leaf_core:
@@ -216,7 +248,7 @@
         return state - jnp.einsum("ka,na->kn", held, corr, precision=HIGH)
 
     if leaf_core:
-        top = pair_up(low(0), value, exchange(value, 1), 1)
+        top = pair_up(low(0), value, tie(exchange(value, 1), proj), 1)
         top = top / jnp.sqrt(jnp.float32(rows_here))
         held = times_transposed(top, table[first])
     else:
@@ -229,8 +261,18 @@
     for level in reversed(range(1, first)):
         start = value
         held = solve(level, value, {})
-        projs, corrs = lax.optimization_barrier((proj_bases, corr_bases, start))[:2]
-        proj, corr = projs[level - 1], corrs[level]
+        if level == first - 2:
+            later = fetch(
+                proj_bases,
+                corr_bases,
+                list(reversed(range(level))),
+                list(reversed(range(level + 1))),
+                start,
+            )
+            projs, corrs = list(later[:level]), list(later[level:])
+        if level < first - 1:
+            proj, corr = projs.pop(0), corrs.pop(0)
+        proj, corr = tie(proj, start), tie(corr, start)
         ahead = chip_sum(project(proj, state))
         own = jnp.einsum("na,nb->ab", proj, corr, precision=HIGH)
         if heads and level == first - 1:
@@ -238,15 +280,10 @@
         value = ahead - times_transposed(held, own + exchange(own, 1))
         if level > 1:
             state = update(corr, state, chip_gather(held))
-    last_corrs = tie(corr_bases, value)
-    one_corr, zero_corr = last_corrs[1], last_corrs[0]
-    state = update(one_corr, state, chip_gather(held))
-    ahead_of = {
-        bits[0] - 1: lambda v: tie(v, zero_corr),
-        bits[0]: lambda v: tie(v, state),
-    }
+    state = update(corr, state, chip_gather(held))
+    ahead_of = {bits[0]: lambda v: tie(v, state)}
     held = solve(0, value, ahead_of)
-    return finish(state, zero_corr, chip_gather(held))
+    return finish(state, corrs[0], chip_gather(held))
 
 
 def solution(mesh):

time: 72.6 us -> 76.4 us (1.052)
  matrix products: 20.5 us -> 14.6 us
  Pallas kernels: 3.68 us -> 7.77 us
  starting transfers between devices: 18.5 us -> 22.2 us
  local copies, waits for them, and re-layouts: 1.31 us -> 4.4 us
  waiting for transfers between devices: 27.4 us -> 24.4 us
  other arithmetic: 0.38 us -> 2.28 us
    dot_general x3, matrix products: 7.34 us -> 2.98 us  [on_device(): own = jnp.einsum('na,nb->ab', proj, corr, precision=HIGH)]
    pallas_call x0 -> x2, Pallas kernels: none -> 4.09 us  [fetch(): pl.pallas_call(body, in_specs=[IN_HBM, IN_HBM, pl.BlockSpec(memory_space=...]
    ppermute x29, starting transfers between devices: 18.5 us -> 22.2 us  [exchange(): return lax.ppermute(value, 'leaf', pairs)]
    unnamed x12 -> x18, local copies, waits for them, and re-layouts: 1.07 us -> 4.23 us
    ppermute x29, waiting for transfers between devices: 27.4 us -> 24.4 us  [exchange(): return lax.ppermute(value, 'leaf', pairs)]
    dot_general x4, matrix products: 5.46 us -> 3.89 us  [project(): return jnp.einsum('kn,nr->kr', state, basis, precision=HIGH)]
    select_n x4, other arithmetic: 0.09 us -> 1.16 us  [pair_up(): jnp.where(low, jnp.concatenate([mine, other], axis), jnp.concatenate([oth...]
    add x6, other arithmetic: 0.06 us -> 0.9 us  [solve(): value = value + across(value, bit)]
  transfers between devices with their start and end apart: 29 -> 29, of which waited for: 11 -> 11; matrix products, arithmetic and copies ran while one was open for 25% -> 15% of each run, Pallas kernels for 0% -> 5%
where the time goes in v5:
time: 76.4 us; the launch traced here: 76.1 us
  waiting for transfers between devices  24.4 us (32%)
  starting transfers between devices  22.2 us (29%)
  matrix products  14.6 us (19%)
  Pallas kernels  7.77 us (10%)
  local copies, waits for them, and re-layouts  4.4 us (6%)
  other arithmetic  2.28 us (3%)
    ppermute x29, waiting for transfers between devices, exchange(): return lax.ppermute(value, 'leaf', pairs)  24.4 us
    ppermute x29, starting transfers between devices, exchange(): return lax.ppermute(value, 'leaf', pairs)  22.2 us
    unnamed x18, local copies, waits for them, and re-layouts  4.23 us
    pallas_call x2, Pallas kernels, fetch(): pl.pallas_call(body, in_specs=[IN_HBM, IN_HBM, pl.BlockSpec(memory_space=...  4.09 us
    dot_general x8, matrix products, times_transposed(): return jnp.einsum('kb,ab->ka', left, right, precision=HIGH)  4.05 us
    dot_general x4, matrix products, project(): return jnp.einsum('kn,nr->kr', state, basis, precision=HIGH)  3.89 us
    dot_general x4, matrix products, update(): return state - jnp.einsum('ka,na->kn', held, corr, precision=HIGH)  3.68 us
    dot_general x3, matrix products, on_device(): own = jnp.einsum('na,nb->ab', proj, corr, precision=HIGH)  2.98 us
  transfers between devices with their start and end apart: 29, of which 11 were waited for; matrix products, arithmetic and copies ran while one was open for 15% of the time, Pallas kernels for 5%

profile of v5, /device:TPU:0, one launch (start us, length us, event | category | flops | bytes accessed | tf_op | source)
XLA Modules:
  0.0 76.1 jit_solution(58341777663084696)
XLA Ops:
  0.0 2.3 %begin.1 = (f32[128,256]{1,0:T(8,128)S(1)}, f32[128,1024]{1,0:T(8,128)S(1)}, f32[1024,256]{1,0:T(8,128)S(1)}, f32[1024,256]{1,0:T(8,128)S(1)}, f32[256,512]{1,0:...) custom-call(f32[1024,128]{1,0:T(8,128)} %x_hbm.1, f32[5,1024,256]{2,1,0:T(8,128)} %p_hbm.5, ...), custom_call_target="tpu_custom_call" | custom-call | flops 201326592 | bytes 4194304 | tf_op jit(solution)/shard_map/begin/pallas_call | solution.py:89
  2.3 1.0 %copy-done = f32[1024,256]{1,0:T(8,128)} copy-done((f32[1024,256]{1,0:T(8,128)}, f32[1024,256]{1,0:T(8,128)S(1)}, u32[]{:S(2)}) %copy-start) | copy-done | bytes 1048600
  3.3 0.8 %copy-done.1 = f32[128,1024]{1,0:T(8,128)} copy-done((f32[128,1024]{1,0:T(8,128)}, f32[128,1024]{1,0:T(8,128)S(1)}, u32[]{:S(2)}) %copy-start.1) | copy-done | bytes 524312
  4.1 0.8 %copy-done.2 = f32[256,512]{1,0:T(8,128)} copy-done((f32[256,512]{1,0:T(8,128)}, f32[256,512]{1,0:T(8,128)S(1)}, u32[]{:S(2)}) %copy-start.2) | copy-done | bytes 524312
  4.9 0.7 copy-done.4
  5.6 0.5 collective-permute-start
  6.2 1.6 %fetch.2 = (f32[1024,256]{1,0:T(8,128)S(1)}, f32[1024,256]{1,0:T(8,128)S(1)}) custom-call(f32[5,1024,256]{2,1,0:T(8,128)} %p_hbm.5, f32[5,1024,256]{2,1,0:T(8,128)} %w_hbm.5, f32[128,256]{1,0:T(8,128)} %copy-done.3), custom_call_target="tpu_custom_call" | custom-call | bytes 4194304 | tf_op jit(solution)/shard_map/fetch/pallas_call | solution.py:123
  7.8 1.7 %fusion.1 = f32[128,256]{1,0:T(8,128)S(1)} fusion(f32[256,512]{1,0:T(8,128)} %copy-done.2, f32[128,256]{1,0:T(8,128)} %collective-permute-done, f32[128,256]{1,0:T(8,128)} %copy-done.3, pred[]{:T(512)S(6)} %eq.12), kind=kOutput, calls=%fused_computation.12 | convolution fusion | flops 100925440 | bytes 917505 | tf_op jit(solution)/shard_map/kb,ab->ka/dot_general | solution.py:37
  9.5 1.7 %convolution_subtract_fusion.3 = f32[128,1024]{1,0:T(8,128)S(1)} fusion(f32[128,1024]{1,0:T(8,128)} %copy-done.1, f32[128,256]{1,0:T(8,128)S(1)} %fusion.1, f32[1024,256]{1,0:T(8,128)S(1)} %get-tuple-element.41), kind=kOutput, calls=%fused_computation.3 | convolution fusion | flops 201457664 | bytes 2228224 | tf_op jit(solution)/shard_map/ka,na->kn/dot_general | solution.py:248
  11.3 0.8 %copy-done.6 = f32[128,1024]{1,0:T(8,128)} copy-done((f32[128,1024]{1,0:T(8,128)}, f32[128,1024]{1,0:T(8,128)S(1)}, u32[]{:S(2)}) %copy-start.6) | copy-done | bytes 524312
  12.0 1.6 %fusion.87 = f32[128,256]{1,0:T(8,128)S(1)} fusion(f32[128,1024]{1,0:T(8,128)S(1)} %convolution_subtract_fusion.3, f32[1024,256]{1,0:T(8,128)} %copy-done), kind=kOutput, calls=%fused_computation.110 | convolution fusion | flops 201326592 | bytes 1703936 | tf_op jit(solution)/shard_map/kn,nr->kr/dot_general | solution.py:33
  13.7 0.5 collective-permute-start.1
  14.2 2.6 %collective-permute-start.9 = (f32[1,112,512]{2,1,0:T(8,128)}, f32[1,112,512]{2,1,0:T(8,128)}, u32[]{:S(2)}, u32[]{:S(2)}) collective-permute-start(f32[1,112,512]{2,1,0:T(8,128)} %bitcast.43), channel_id=1, source_target_pairs={{0,2},{1,3},{2,0},{3,1},{4,6},{5,7},{6,4},{7,5},{8,10},{9,11},{10,... | collective-permute-start | bytes 688136 | tf_op jit(solution)/shard_map/ppermute | solution.py:17
  16.8 1.0 %collective-permute-start.2 = (f32[64,256]{1,0:T(8,128)S(1)}, f32[64,256]{1,0:T(8,128)S(1)}, u32[]{:S(2)}, u32[]{:S(2)}) collective-permute-start(f32[64,256]{1,0:T(8,128)S(1)} %select_add_fusion), channel_id=1, source_target_pairs={{0,3},{1,2},{2,1},{3,0},{4,7},{5,6},{6,5},{7,4},{8,11},{9,10},{10,... | collective-permute-start | bytes 196616 | tf_op jit(solution)/shard_map/ppermute | solution.py:17
  17.8 1.0 %fusion.89 = f32[256,256]{1,0:T(8,128)S(1)} fusion(f32[1024,256]{1,0:T(8,128)S(1)} %get-tuple-element.47, f32[1024,256]{1,0:T(8,128)S(1)} %get-tuple-element.46), kind=kOutput, calls=%fused_computation.112 | convolution fusion | flops 402653184 | bytes 2359296 | tf_op jit(solution)/shard_map/na,nb->ab/dot_general | solution.py:277
  18.8 1.5 %fusion.88 = f32[128,256]{1,0:T(8,128)S(1)} fusion(f32[128,1024]{1,0:T(8,128)} %copy-done.6, f32[1024,256]{1,0:T(8,128)S(1)} %get-tuple-element.47), kind=kOutput, calls=%fused_computation.111 | convolution fusion | flops 201326592 | bytes 1703936 | tf_op jit(solution)/shard_map/kn,nr->kr/dot_general | solution.py:33
  20.3 0.4 collective-permute-start.3
  20.9 0.4 collective-permute-start.6
  21.3 2.3 %collective-permute-done.9 = f32[1,112,512]{2,1,0:T(8,128)} collective-permute-done((f32[1,112,512]{2,1,0:T(8,128)}, f32[1,112,512]{2,1,0:T(8,128)}, u32[]{:S(2)}, u32[]{:S(2)}) %collective-permute-start.9) | collective-permute-done | bytes 229408 | tf_op jit(solution)/shard_map/ppermute | solution.py:17
  23.6 1.1 %maximum_select_fusion.4 = f32[2,112,512]{2,1,0:T(8,128)S(1)} fusion(f32[1,112,512]{2,1,0:T(8,128)} %collective-permute-done.9, f32[1,112,512]{2,1,0:T(8,128)S(1)} %bitcast.44, pred[]{:T(512)S(6)} %eq.27), kind=kLoop, calls=%fused_computation.8 | loop fusion | flops 344064 | bytes 917505 | tf_op jit(solution)/shard_map/jit(_where)/select_n | solution.py:25
  24.7 2.0 %collective-permute-start.17 = (f32[2,48,512]{2,1,0:T(8,128)S(1)}, f32[2,48,512]{2,1,0:T(8,128)S(1)}, u32[]{:S(2)}, u32[]{:S(2)}) collective-permute-start(f32[2,48,512]{2,1,0:T(8,128)S(1)} %slice.63), channel_id=1, source_target_pairs={{0,4},{1,5},{2,6},{3,7},{4,0},{5,1},{6,2},{7,3},{8,12},{9,13},{10,... | collective-permute-start | bytes 589832 | tf_op jit(solution)/shard_map/ppermute | solution.py:17
  26.8 0.4 fusion.15
  27.2 0.6 collective-permute-start.4
  27.8 0.3 add_subtract_fusion.2._
  28.1 1.2 %collective-permute-start.7 = (f32[64,256]{1,0:T(8,128)S(1)}, f32[64,256]{1,0:T(8,128)S(1)}, u32[]{:S(2)}, u32[]{:S(2)}) collective-permute-start(f32[64,256]{1,0:T(8,128)S(1)} %add_subtract_fusion.2._), channel_id=1, source_target_pairs={{0,3},{1,2},{2,1},{3,0},{4,7},{5,6},{6,5},{7,4},{8,11},{9,10},{10,... | collective-permute-start | bytes 196616 | tf_op jit(solution)/shard_map/ppermute | solution.py:17
  29.3 2.5 %fetch.3 = (f32[1024,256]{1,0:T(8,128)S(1)}, f32[1024,256]{1,0:T(8,128)S(1)}, f32[1024,256]{1,0:T(8,128)S(1)}, f32[1024,256]{1,0:T(8,128)S(1)}, f32[1024,256]{1,0:T(8,128)S(1)}) custom-call(f32[5,1024,256]{2,1,0:T(8,128)} %p_hbm.5, f32[5,1024,256]{2,1,0:T(8,128)} %w_hbm.5, f32[64,256]{1,0:T(8,128)} %copy-done.8), custom_call_target="tpu_custom_call" | custom-call | bytes 10485760 | tf_op jit(solution)/shard_map/fetch/pallas_call | solution.py:123
  31.8 1.0 %fusion.91 = f32[256,256]{1,0:T(8,128)S(1)} fusion(f32[1024,256]{1,0:T(8,128)S(1)} %get-tuple-element.54, f32[1024,256]{1,0:T(8,128)S(1)} %get-tuple-element.52), kind=kOutput, calls=%fused_computation.114 | convolution fusion | flops 402653184 | bytes 2359296 | tf_op jit(solution)/shard_map/na,nb->ab/dot_general | solution.py:277
  32.8 0.5 collective-permute-start.13
  33.5 0.8 %add.42 = f32[64,256]{1,0:T(8,128)S(1)} add(f32[64,256]{1,0:T(8,128)} %copy-done.8, f32[64,256]{1,0:T(8,128)S(1)} %collective-permute-done.7) | non-fusion elementwise | flops 16384 | bytes 196608 | tf_op jit(solution)/shard_map/add | solution.py:236
  34.6 1.6 %collective-permute-start.26 = (f32[4,16,512]{2,1,0:T(8,128)S(1)}, f32[4,16,512]{2,1,0:T(8,128)S(1)}, u32[]{:S(2)}, u32[]{:S(2)}) collective-permute-start(f32[4,16,512]{2,1,0:T(8,128)S(1)} %slice.67), channel_id=1, source_target_pairs={{0,8},{1,9},{2,10},{3,11},{4,12},{5,13},{6,14},{7,15},{8,0},{9,1},... | collective-permute-start | bytes 393224 | tf_op jit(solution)/shard_map/ppermute | solution.py:17
  36.5 0.7 convolution_subtract_fusion.2
  37.1 0.4 fusion.90
  37.5 1.0 %collective-permute-done.8 = f32[64,256]{1,0:T(8,128)S(1)} collective-permute-done((f32[64,256]{1,0:T(8,128)S(1)}, f32[64,256]{1,0:T(8,128)S(1)}, u32[]{:S(2)}, u32[]{:S(2)}) %collective-permute-start.8) | collective-permute-done | bytes 65568 | tf_op jit(solution)/shard_map/ppermute | solution.py:17
  38.6 0.4 fusion.28
  38.9 0.4 collective-permute-start.11
  39.3 0.3 collective-permute-start.12
  39.6 0.7 collective-permute-done.11
  40.3 0.7 convolution_subtract_fusion.1
  41.0 0.3 add_subtract_fusion.1
  41.2 0.5 collective-permute-start.14
  41.8 1.0 %fusion.93 = f32[256,256]{1,0:T(8,128)S(1)} fusion(f32[1024,256]{1,0:T(8,128)S(1)} %get-tuple-element.62, f32[1024,256]{1,0:T(8,128)S(1)} %get-tuple-element.59), kind=kOutput, calls=%fused_computation.116 | convolution fusion | flops 402653184 | bytes 2359296 | tf_op jit(solution)/shard_map/na,nb->ab/dot_general | solution.py:277
  42.8 0.4 fusion.92
  43.2 2.1 %collective-permute-done.14 = f32[64,256]{1,0:T(8,128)S(1)} collective-permute-done((f32[64,256]{1,0:T(8,128)S(1)}, f32[64,256]{1,0:T(8,128)S(1)}, u32[]{:S(2)}, u32[]{:S(2)}) %collective-permute-start.14) | collective-permute-done | bytes 65568 | tf_op jit(solution)/shard_map/ppermute | solution.py:17
  45.3 0.4 collective-permute-start.15
  45.7 0.3 collective-permute-start.20
  46.3 3.1 %collective-permute-done.15 = f32[64,256]{1,0:T(8,128)S(1)} collective-permute-done((f32[64,256]{1,0:T(8,128)S(1)}, f32[64,256]{1,0:T(8,128)S(1)}, u32[]{:S(2)}, u32[]{:S(2)}) %collective-permute-start.15) | collective-permute-done | bytes 65568 | tf_op jit(solution)/shard_map/ppermute | solution.py:17
  49.4 1.4 %collective-permute-start.16 = (f32[64,256]{1,0:T(8,128)S(1)}, f32[64,256]{1,0:T(8,128)S(1)}, u32[]{:S(2)}, u32[]{:S(2)}) collective-permute-start(f32[64,256]{1,0:T(8,128)S(1)} %add.46), channel_id=1, source_target_pairs={{0,9},{1,8},{2,11},{3,10},{4,13},{5,12},{6,15},{7,14},{8,1},{9,0},... | collective-permute-start | bytes 196616 | tf_op jit(solution)/shard_map/ppermute | solution.py:17
  50.9 2.7 %collective-permute-done.16 = f32[64,256]{1,0:T(8,128)S(1)} collective-permute-done((f32[64,256]{1,0:T(8,128)S(1)}, f32[64,256]{1,0:T(8,128)S(1)}, u32[]{:S(2)}, u32[]{:S(2)}) %collective-permute-start.16) | collective-permute-done | bytes 65568 | tf_op jit(solution)/shard_map/ppermute | solution.py:17
  53.6 0.4 fusion.41
  54.0 0.3 add_subtract_fusion
  54.5 0.4 collective-permute-start.19
  54.9 3.5 %collective-permute-done.22 = f32[64,256]{1,0:T(8,128)S(1)} collective-permute-done((f32[64,256]{1,0:T(8,128)S(1)}, f32[64,256]{1,0:T(8,128)S(1)}, u32[]{:S(2)}, u32[]{:S(2)}) %collective-permute-start.22) | collective-permute-done | bytes 65568 | tf_op jit(solution)/shard_map/ppermute | solution.py:17
  58.4 0.3 collective-permute-start.23
  58.7 0.4 collective-permute-start.27
  59.1 3.4 %collective-permute-done.23 = f32[64,256]{1,0:T(8,128)S(1)} collective-permute-done((f32[64,256]{1,0:T(8,128)S(1)}, f32[64,256]{1,0:T(8,128)S(1)}, u32[]{:S(2)}, u32[]{:S(2)}) %collective-permute-start.23) | collective-permute-done | bytes 65568 | tf_op jit(solution)/shard_map/ppermute | solution.py:17
  62.6 1.4 %collective-permute-start.24 = (f32[64,256]{1,0:T(8,128)S(1)}, f32[64,256]{1,0:T(8,128)S(1)}, u32[]{:S(2)}, u32[]{:S(2)}) collective-permute-start(f32[64,256]{1,0:T(8,128)S(1)} %add.50), channel_id=1, source_target_pairs={{0,9},{1,8},{2,11},{3,10},{4,13},{5,12},{6,15},{7,14},{8,1},{9,0},... | collective-permute-start | bytes 196616 | tf_op jit(solution)/shard_map/ppermute | solution.py:17
  64.0 0.7 convolution_subtract_fusion.x_ref
  64.7 2.1 %collective-permute-done.24 = f32[64,256]{1,0:T(8,128)S(1)} collective-permute-done((f32[64,256]{1,0:T(8,128)S(1)}, f32[64,256]{1,0:T(8,128)S(1)}, u32[]{:S(2)}, u32[]{:S(2)}) %collective-permute-start.24) | collective-permute-done | bytes 65568 | tf_op jit(solution)/shard_map/ppermute | solution.py:17
  66.8 2.4 %collective-permute-start.25 = (f32[64,256]{1,0:T(8,128)S(1)}, f32[64,256]{1,0:T(8,128)S(1)}, u32[]{:S(2)}, u32[]{:S(2)}) collective-permute-start(f32[64,256]{1,0:T(8,128)S(1)} %add.51), channel_id=1, source_target_pairs={{0,17},{1,16},{2,19},{3,18},{4,21},{5,20},{6,23},{7,22},{8,25},{9,... | collective-permute-start | bytes 196616 | tf_op jit(solution)/shard_map/ppermute | solution.py:17
  69.3 2.6 %collective-permute-done.25 = f32[64,256]{1,0:T(8,128)S(1)} collective-permute-done((f32[64,256]{1,0:T(8,128)S(1)}, f32[64,256]{1,0:T(8,128)S(1)}, u32[]{:S(2)}, u32[]{:S(2)}) %collective-permute-start.25) | collective-permute-done | bytes 65568 | tf_op jit(solution)/shard_map/ppermute | solution.py:17
  71.8 0.4 fusion.54
  72.2 1.6 %collective-permute-start.28 = (f32[64,256]{1,0:T(8,128)S(1)}, f32[64,256]{1,0:T(8,128)S(1)}, u32[]{:S(2)}, u32[]{:S(2)}) collective-permute-start(f32[64,256]{1,0:T(8,128)S(1)} %fusion.54), channel_id=1, source_target_pairs={{0,1},{1,0},{2,3},{3,2},{4,5},{5,4},{6,7},{7,6},{8,9},{9,8},{10,11... | collective-permute-start | bytes 196616 | tf_op jit(solution)/shard_map/ppermute | solution.py:17
  73.8 0.9 %collective-permute-done.28 = f32[64,256]{1,0:T(8,128)S(1)} collective-permute-done((f32[64,256]{1,0:T(8,128)S(1)}, f32[64,256]{1,0:T(8,128)S(1)}, u32[]{:S(2)}, u32[]{:S(2)}) %collective-permute-start.28) | collective-permute-done | bytes 65568 | tf_op jit(solution)/shard_map/ppermute | solution.py:17
  74.7 1.4 %finish.1 = f32[1024,128]{1,0:T(8,128)} custom-call(f32[128,1024]{1,0:T(8,128)S(1)} %convolution_subtract_fusion.x_ref, f32[1024,256]{1,0:T(8,128)S(1)} %get-tuple-element.60.w_ref, f32[128,256]{1,0:T(8,128)S(1)} %maximum_select_fusion.18.t_ref), custom_call_target="tpu_custom_call" | custom-call | flops 201326592 | bytes 2097152 | tf_op jit(solution)/shard_map/finish/pallas_call | solution.py:143
  (61 shorter events, 1.9 us)
Async XLA Ops:
  2.3 1.0 %copy-start = (f32[1024,256]{1,0:T(8,128)}, f32[1024,256]{1,0:T(8,128)S(1)}, u32[]{:S(2)}) copy-start(f32[1024,256]{1,0:T(8,128)S(1)} %get-tuple-element.42) | copy-start | bytes 3145732
  3.3 0.8 %copy-start.1 = (f32[128,1024]{1,0:T(8,128)}, f32[128,1024]{1,0:T(8,128)S(1)}, u32[]{:S(2)}) copy-start(f32[128,1024]{1,0:T(8,128)S(1)} %get-tuple-element.36) | copy-start | bytes 1572868
  4.1 0.8 %copy-start.2 = (f32[256,512]{1,0:T(8,128)}, f32[256,512]{1,0:T(8,128)S(1)}, u32[]{:S(2)}) copy-start(f32[256,512]{1,0:T(8,128)S(1)} %get-tuple-element.40) | copy-start | bytes 1572868
  4.9 0.7 copy-start.4
  5.6 0.6 copy-start.3
  5.6 2.2 %collective-permute-start = (f32[128,256]{1,0:T(8,128)S(1)}, f32[128,256]{1,0:T(8,128)}, u32[]{:S(2)}, u32[]{:S(2)}) collective-permute-start(f32[128,256]{1,0:T(8,128)S(1)} %get-tuple-element.37._), channel_id=1, source_target_pairs={{0,1},{1,0},{2,3},{3,2},{4,5},{5,4},{6,7},{7,6},{8,9},{9,8},{10,11... | collective-permute-start | bytes 393224 | tf_op jit(solution)/shard_map/ppermute | solution.py:17
  11.3 0.8 %copy-start.6 = (f32[128,1024]{1,0:T(8,128)}, f32[128,1024]{1,0:T(8,128)S(1)}, u32[]{:S(2)}) copy-start(f32[128,1024]{1,0:T(8,128)S(1)} %convolution_subtract_fusion.3) | copy-start | bytes 1572868
  11.3 12.3 %copy-start.5 = (f32[112,512]{1,0:T(8,128)S(1)}, f32[112,512]{1,0:T(8,128)}, u32[]{:S(2)}) copy-start(f32[112,512]{1,0:T(8,128)} %copy-done.4) | copy-start | bytes 688132
  13.7 3.1 %collective-permute-start.1 = (f32[64,256]{1,0:T(8,128)S(1)}, f32[64,256]{1,0:T(8,128)S(1)}, u32[]{:S(2)}, u32[]{:S(2)}) collective-permute-start(f32[64,256]{1,0:T(8,128)S(1)} %slice_select_fusion.3), channel_id=1, source_target_pairs={{0,1},{1,0},{2,3},{3,2},{4,5},{5,4},{6,7},{7,6},{8,9},{9,8},{10,11... | collective-permute-start | bytes 196616 | tf_op jit(solution)/shard_map/ppermute | solution.py:17
  14.2 9.3 %collective-permute-start.9 = (f32[1,112,512]{2,1,0:T(8,128)}, f32[1,112,512]{2,1,0:T(8,128)}, u32[]{:S(2)}, u32[]{:S(2)}) collective-permute-start(f32[1,112,512]{2,1,0:T(8,128)} %bitcast.43), channel_id=1, source_target_pairs={{0,2},{1,3},{2,0},{3,1},{4,6},{5,7},{6,4},{7,5},{8,10},{9,11},{10,... | collective-permute-start | bytes 688136 | tf_op jit(solution)/shard_map/ppermute | solution.py:17
  16.8 10.0 %collective-permute-start.2 = (f32[64,256]{1,0:T(8,128)S(1)}, f32[64,256]{1,0:T(8,128)S(1)}, u32[]{:S(2)}, u32[]{:S(2)}) collective-permute-start(f32[64,256]{1,0:T(8,128)S(1)} %select_add_fusion), channel_id=1, source_target_pairs={{0,3},{1,2},{2,1},{3,0},{4,7},{5,6},{6,5},{7,4},{8,11},{9,10},{10,... | collective-permute-start | bytes 196616 | tf_op jit(solution)/shard_map/ppermute | solution.py:17
  20.3 6.5 %collective-permute-start.3 = (f32[1,128,512]{2,1,0:T(8,128)S(1)}, f32[1,128,512]{2,1,0:T(8,128)S(1)}, u32[]{:S(2)}, u32[]{:S(2)}) collective-permute-start(f32[1,128,512]{2,1,0:T(8,128)S(1)} %bitcast.41), channel_id=1, source_target_pairs={{0,1},{1,0},{2,3},{3,2},{4,5},{5,4},{6,7},{7,6},{8,9},{9,8},{10,11... | collective-permute-start | bytes 786440 | tf_op jit(solution)/shard_map/ppermute | solution.py:17
  20.7 7.1 %collective-permute-start.5 = (f32[64,256]{1,0:T(8,128)S(1)}, f32[64,256]{1,0:T(8,128)S(1)}, u32[]{:S(2)}, u32[]{:S(2)}) collective-permute-start(f32[64,256]{1,0:T(8,128)S(1)} %slice_select_fusion.2), channel_id=1, source_target_pairs={{0,1},{1,0},{2,3},{3,2},{4,5},{5,4},{6,7},{7,6},{8,9},{9,8},{10,11... | collective-permute-start | bytes 196616 | tf_op jit(solution)/shard_map/ppermute | solution.py:17
  20.9 6.9 %collective-permute-start.6 = (f32[256,256]{1,0:T(8,128)S(1)}, f32[256,256]{1,0:T(8,128)S(1)}, u32[]{:S(2)}, u32[]{:S(2)}) collective-permute-start(f32[256,256]{1,0:T(8,128)S(1)} %fusion.89), channel_id=1, source_target_pairs={{0,1},{1,0},{2,3},{3,2},{4,5},{5,4},{6,7},{7,6},{8,9},{9,8},{10,11... | collective-permute-start | bytes 786440 | tf_op jit(solution)/shard_map/ppermute | solution.py:17
  24.7 9.8 %collective-permute-start.17 = (f32[2,48,512]{2,1,0:T(8,128)S(1)}, f32[2,48,512]{2,1,0:T(8,128)S(1)}, u32[]{:S(2)}, u32[]{:S(2)}) collective-permute-start(f32[2,48,512]{2,1,0:T(8,128)S(1)} %slice.63), channel_id=1, source_target_pairs={{0,4},{1,5},{2,6},{3,7},{4,0},{5,1},{6,2},{7,3},{8,12},{9,13},{10,... | collective-permute-start | bytes 589832 | tf_op jit(solution)/shard_map/ppermute | solution.py:17
  26.8 6.6 %collective-permute-start.10 = (f32[2,64,512]{2,1,0:T(8,128)S(1)}, f32[2,64,512]{2,1,0:T(8,128)S(1)}, u32[]{:S(2)}, u32[]{:S(2)}) collective-permute-start(f32[2,64,512]{2,1,0:T(8,128)S(1)} %slice.60), channel_id=1, source_target_pairs={{0,1},{1,0},{2,3},{3,2},{4,5},{5,4},{6,7},{7,6},{8,9},{9,8},{10,11... | collective-permute-start | bytes 786440 | tf_op jit(solution)/shard_map/ppermute | solution.py:17
  27.2 9.3 %collective-permute-start.4 = (f32[64,256]{1,0:T(8,128)S(1)}, f32[64,256]{1,0:T(8,128)S(1)}, u32[]{:S(2)}, u32[]{:S(2)}) collective-permute-start(f32[64,256]{1,0:T(8,128)S(1)} %fusion.15), channel_id=1, source_target_pairs={{0,1},{1,0},{2,3},{3,2},{4,5},{5,4},{6,7},{7,6},{8,9},{9,8},{10,11... | collective-permute-start | bytes 196616 | tf_op jit(solution)/shard_map/ppermute | solution.py:17
  28.1 1.2 %copy-start.8 = (f32[64,256]{1,0:T(8,128)}, f32[64,256]{1,0:T(8,128)S(1)}, u32[]{:S(2)}) copy-start(f32[64,256]{1,0:T(8,128)S(1)} %add_subtract_fusion.2._) | copy-start | bytes 196612
  28.1 5.4 %collective-permute-start.7 = (f32[64,256]{1,0:T(8,128)S(1)}, f32[64,256]{1,0:T(8,128)S(1)}, u32[]{:S(2)}, u32[]{:S(2)}) collective-permute-start(f32[64,256]{1,0:T(8,128)S(1)} %add_subtract_fusion.2._), channel_id=1, source_target_pairs={{0,3},{1,2},{2,1},{3,0},{4,7},{5,6},{6,5},{7,4},{8,11},{9,10},{10,... | collective-permute-start | bytes 196616 | tf_op jit(solution)/shard_map/ppermute | solution.py:17
  31.8 4.7 %copy-start.7 = (f32[128,1024]{1,0:T(8,128)S(1)}, f32[128,1024]{1,0:T(8,128)}, u32[]{:S(2)}) copy-start(f32[128,1024]{1,0:T(8,128)} %copy-done.6) | copy-start | bytes 1572868
  32.8 8.1 %collective-permute-start.13 = (f32[256,256]{1,0:T(8,128)S(1)}, f32[256,256]{1,0:T(8,128)S(1)}, u32[]{:S(2)}, u32[]{:S(2)}) collective-permute-start(f32[256,256]{1,0:T(8,128)S(1)} %fusion.91), channel_id=1, source_target_pairs={{0,1},{1,0},{2,3},{3,2},{4,5},{5,4},{6,7},{7,6},{8,9},{9,8},{10,11... | collective-permute-start | bytes 786440 | tf_op jit(solution)/shard_map/ppermute | solution.py:17
  34.3 4.2 %collective-permute-start.8 = (f32[64,256]{1,0:T(8,128)S(1)}, f32[64,256]{1,0:T(8,128)S(1)}, u32[]{:S(2)}, u32[]{:S(2)}) collective-permute-start(f32[64,256]{1,0:T(8,128)S(1)} %add.42), channel_id=1, source_target_pairs={{0,5},{1,4},{2,7},{3,6},{4,1},{5,0},{6,3},{7,2},{8,13},{9,12},{10,... | collective-permute-start | bytes 196616 | tf_op jit(solution)/shard_map/ppermute | solution.py:17
  34.6 19.9 %collective-permute-start.26 = (f32[4,16,512]{2,1,0:T(8,128)S(1)}, f32[4,16,512]{2,1,0:T(8,128)S(1)}, u32[]{:S(2)}, u32[]{:S(2)}) collective-permute-start(f32[4,16,512]{2,1,0:T(8,128)S(1)} %slice.67), channel_id=1, source_target_pairs={{0,8},{1,9},{2,10},{3,11},{4,12},{5,13},{6,14},{7,15},{8,0},{9,1},... | collective-permute-start | bytes 393224 | tf_op jit(solution)/shard_map/ppermute | solution.py:17
  36.3 14.6 %collective-permute-start.18 = (f32[4,32,512]{2,1,0:T(8,128)S(1)}, f32[4,32,512]{2,1,0:T(8,128)S(1)}, u32[]{:S(2)}, u32[]{:S(2)}) collective-permute-start(f32[4,32,512]{2,1,0:T(8,128)S(1)} %slice.64), channel_id=1, source_target_pairs={{0,1},{1,0},{2,3},{3,2},{4,5},{5,4},{6,7},{7,6},{8,9},{9,8},{10,11... | collective-permute-start | bytes 786440 | tf_op jit(solution)/shard_map/ppermute | solution.py:17
  38.9 1.3 %collective-permute-start.11 = (f32[64,256]{1,0:T(8,128)S(1)}, f32[64,256]{1,0:T(8,128)S(1)}, u32[]{:S(2)}, u32[]{:S(2)}) collective-permute-start(f32[64,256]{1,0:T(8,128)S(1)} %fusion.28), channel_id=1, source_target_pairs={{0,1},{1,0},{2,3},{3,2},{4,5},{5,4},{6,7},{7,6},{8,9},{9,8},{10,11... | collective-permute-start | bytes 196616 | tf_op jit(solution)/shard_map/ppermute | solution.py:17
  39.3 1.6 %collective-permute-start.12 = (f32[64,256]{1,0:T(8,128)S(1)}, f32[64,256]{1,0:T(8,128)S(1)}, u32[]{:S(2)}, u32[]{:S(2)}) collective-permute-start(f32[64,256]{1,0:T(8,128)S(1)} %slice_select_fusion.1), channel_id=1, source_target_pairs={{0,1},{1,0},{2,3},{3,2},{4,5},{5,4},{6,7},{7,6},{8,9},{9,8},{10,11... | collective-permute-start | bytes 196616 | tf_op jit(solution)/shard_map/ppermute | solution.py:17
  41.2 4.0 %collective-permute-start.14 = (f32[64,256]{1,0:T(8,128)S(1)}, f32[64,256]{1,0:T(8,128)S(1)}, u32[]{:S(2)}, u32[]{:S(2)}) collective-permute-start(f32[64,256]{1,0:T(8,128)S(1)} %add_subtract_fusion.1), channel_id=1, source_target_pairs={{0,3},{1,2},{2,1},{3,0},{4,7},{5,6},{6,5},{7,4},{8,11},{9,10},{10,... | collective-permute-start | bytes 196616 | tf_op jit(solution)/shard_map/ppermute | solution.py:17
  45.3 4.1 %collective-permute-start.15 = (f32[64,256]{1,0:T(8,128)S(1)}, f32[64,256]{1,0:T(8,128)S(1)}, u32[]{:S(2)}, u32[]{:S(2)}) collective-permute-start(f32[64,256]{1,0:T(8,128)S(1)} %add.45), channel_id=1, source_target_pairs={{0,5},{1,4},{2,7},{3,6},{4,1},{5,0},{6,3},{7,2},{8,13},{9,12},{10,... | collective-permute-start | bytes 196616 | tf_op jit(solution)/shard_map/ppermute | solution.py:17
  45.7 8.2 %collective-permute-start.20 = (f32[64,256]{1,0:T(8,128)S(1)}, f32[64,256]{1,0:T(8,128)S(1)}, u32[]{:S(2)}, u32[]{:S(2)}) collective-permute-start(f32[64,256]{1,0:T(8,128)S(1)} %slice_select_fusion), channel_id=1, source_target_pairs={{0,1},{1,0},{2,3},{3,2},{4,5},{5,4},{6,7},{7,6},{8,9},{9,8},{10,11... | collective-permute-start | bytes 196616 | tf_op jit(solution)/shard_map/ppermute | solution.py:17
  46.1 7.9 %collective-permute-start.21 = (f32[256,256]{1,0:T(8,128)S(1)}, f32[256,256]{1,0:T(8,128)S(1)}, u32[]{:S(2)}, u32[]{:S(2)}) collective-permute-start(f32[256,256]{1,0:T(8,128)S(1)} %fusion.93), channel_id=1, source_target_pairs={{0,1},{1,0},{2,3},{3,2},{4,5},{5,4},{6,7},{7,6},{8,9},{9,8},{10,11... | collective-permute-start | bytes 786440 | tf_op jit(solution)/shard_map/ppermute | solution.py:17
  49.4 4.2 %collective-permute-start.16 = (f32[64,256]{1,0:T(8,128)S(1)}, f32[64,256]{1,0:T(8,128)S(1)}, u32[]{:S(2)}, u32[]{:S(2)}) collective-permute-start(f32[64,256]{1,0:T(8,128)S(1)} %add.46), channel_id=1, source_target_pairs={{0,9},{1,8},{2,11},{3,10},{4,13},{5,12},{6,15},{7,14},{8,1},{9,0},... | collective-permute-start | bytes 196616 | tf_op jit(solution)/shard_map/ppermute | solution.py:17
  54.3 4.2 %collective-permute-start.22 = (f32[64,256]{1,0:T(8,128)S(1)}, f32[64,256]{1,0:T(8,128)S(1)}, u32[]{:S(2)}, u32[]{:S(2)}) collective-permute-start(f32[64,256]{1,0:T(8,128)S(1)} %add_subtract_fusion), channel_id=1, source_target_pairs={{0,3},{1,2},{2,1},{3,0},{4,7},{5,6},{6,5},{7,4},{8,11},{9,10},{10,... | collective-permute-start | bytes 196616 | tf_op jit(solution)/shard_map/ppermute | solution.py:17
  54.5 9.5 %collective-permute-start.19 = (f32[64,256]{1,0:T(8,128)S(1)}, f32[64,256]{1,0:T(8,128)S(1)}, u32[]{:S(2)}, u32[]{:S(2)}) collective-permute-start(f32[64,256]{1,0:T(8,128)S(1)} %fusion.41), channel_id=1, source_target_pairs={{0,1},{1,0},{2,3},{3,2},{4,5},{5,4},{6,7},{7,6},{8,9},{9,8},{10,11... | collective-permute-start | bytes 196616 | tf_op jit(solution)/shard_map/ppermute | solution.py:17
  58.4 4.2 %collective-permute-start.23 = (f32[64,256]{1,0:T(8,128)S(1)}, f32[64,256]{1,0:T(8,128)S(1)}, u32[]{:S(2)}, u32[]{:S(2)}) collective-permute-start(f32[64,256]{1,0:T(8,128)S(1)} %add.49), channel_id=1, source_target_pairs={{0,5},{1,4},{2,7},{3,6},{4,1},{5,0},{6,3},{7,2},{8,13},{9,12},{10,... | collective-permute-start | bytes 196616 | tf_op jit(solution)/shard_map/ppermute | solution.py:17
  58.7 10.4 %collective-permute-start.27 = (f32[8,16,512]{2,1,0:T(8,128)S(1)}, f32[8,16,512]{2,1,0:T(8,128)S(1)}, u32[]{:S(2)}, u32[]{:S(2)}) collective-permute-start(f32[8,16,512]{2,1,0:T(8,128)S(1)} %maximum_select_fusion.7), channel_id=1, source_target_pairs={{0,1},{1,0},{2,3},{3,2},{4,5},{5,4},{6,7},{7,6},{8,9},{9,8},{10,11... | collective-permute-start | bytes 786440 | tf_op jit(solution)/shard_map/ppermute | solution.py:17
  62.6 4.2 %collective-permute-start.24 = (f32[64,256]{1,0:T(8,128)S(1)}, f32[64,256]{1,0:T(8,128)S(1)}, u32[]{:S(2)}, u32[]{:S(2)}) collective-permute-start(f32[64,256]{1,0:T(8,128)S(1)} %add.50), channel_id=1, source_target_pairs={{0,9},{1,8},{2,11},{3,10},{4,13},{5,12},{6,15},{7,14},{8,1},{9,0},... | collective-permute-start | bytes 196616 | tf_op jit(solution)/shard_map/ppermute | solution.py:17
  66.8 5.1 %collective-permute-start.25 = (f32[64,256]{1,0:T(8,128)S(1)}, f32[64,256]{1,0:T(8,128)S(1)}, u32[]{:S(2)}, u32[]{:S(2)}) collective-permute-start(f32[64,256]{1,0:T(8,128)S(1)} %add.51), channel_id=1, source_target_pairs={{0,17},{1,16},{2,19},{3,18},{4,21},{5,20},{6,23},{7,22},{8,25},{9,... | collective-permute-start | bytes 196616 | tf_op jit(solution)/shard_map/ppermute | solution.py:17
  72.2 2.5 %collective-permute-start.28 = (f32[64,256]{1,0:T(8,128)S(1)}, f32[64,256]{1,0:T(8,128)S(1)}, u32[]{:S(2)}, u32[]{:S(2)}) collective-permute-start(f32[64,256]{1,0:T(8,128)S(1)} %fusion.54), channel_id=1, source_target_pairs={{0,1},{1,0},{2,3},{3,2},{4,5},{5,4},{6,7},{7,6},{8,9},{9,8},{10,11... | collective-permute-start | bytes 196616 | tf_op jit(solution)/shard_map/ppermute | solution.py:17
